TPU v7x, 32 devices: a whole 2x2x4 slice. The times are simulated.
32 devices in a mesh: cells: 8 (over z, x), rep: 4 (over y, core).
Axes of the slice: x: 2, y: 2, z: 4, core: 2. Of those that a mesh axis runs over, the one named last changes fastest.
Arguments:
- snapshots: bfloat16 [512, 4, 8192], P('cells', 'rep'), may hold values from -6 to 6
- base_field: bfloat16 [4, 8192], P('rep', 'cells'), may hold values from -6 to 6
- design: float32 [512, 64], replicated, may hold values from -0.25 to 0.25
Outputs:
- basis: bfloat16 [64, 4, 8192], P(None, 'rep', 'cells')
- factor: float32 [512, 512], replicated
All inputs are finite; a program needn't handle non-finite values.
Results may differ from a plain program's by a relative error of at most 0.0085.
The roundings to bfloat16 on the way count: a program that leaves them out, or rounds other values in their place, can miss the bound.
Values may be sent and summed in bfloat16 or wider, within the bound.
No kernel may reach another device: no remote copies, remote signals or barrier semaphores. Data moves between devices by JAX's collectives and lax.ppermute only.
A program may use at most 256 MiB of HBM per device.

v0:
```python
import jax
import jax.numpy as jnp
from jax import lax
from jax.sharding import PartitionSpec as P


def upper_factor(gram):
    size_all = gram.shape[0]
    width = 64
    high = lax.Precision.HIGHEST
    columns = lax.broadcasted_iota(jnp.int32, (1, size_all), 1)
    work = gram
    rows_out = []
    for block in range(size_all // width):
        start = block * width
        panel = work[start : start + width, :]
        result = jnp.zeros((width, size_all), jnp.float32)

        def upper_step(index, carry):
            panel_now, result_now = carry
            line = lax.dynamic_index_in_dim(panel_now, index, 0, keepdims=True)
            where = columns == index + start
            pivot = jnp.sqrt(jnp.sum(jnp.where(where, line, 0.0)))
            line = jnp.where(columns >= index + start, line / pivot, 0.0)
            coeffs = line[:, start : start + width]
            panel_now = panel_now - coeffs.T * line
            result_now = lax.dynamic_update_index_in_dim(result_now, line[0], index, 0)
            return (panel_now, result_now)

        panel, result = lax.fori_loop(0, width, upper_step, (panel, result))
        rows_out.append(result)
        work = work - jnp.dot(result.T, result, precision=high, preferred_element_type=jnp.float32)
    return jnp.concatenate(rows_out, axis=0)


def back_solve(factor, right):
    size_all = factor.shape[0]
    width = 64
    high = lax.Precision.HIGHEST
    count = size_all // width
    solved = [None] * count
    rows_small = lax.broadcasted_iota(jnp.int32, (width, 1), 0)
    for block in reversed(range(count)):
        start = block * width
        rhs = right[start : start + width, :]
        if block + 1 < count:
            later = jnp.concatenate(solved[block + 1 :], axis=0)
            rhs = rhs - jnp.dot(
                factor[start : start + width, start + width :],
                later,
                precision=high,
                preferred_element_type=jnp.float32,
            )
        square = factor[start : start + width, start : start + width]
        answer = jnp.zeros_like(rhs)

        def back_step(turn, answer_now):
            index = width - 1 - turn
            line = lax.dynamic_index_in_dim(square, index, 0, keepdims=True)
            target = lax.dynamic_index_in_dim(rhs, index, 0, keepdims=True)
            diag = jnp.sum(jnp.where(rows_small.T == index, line, 0.0))
            value = (
                target
                - jnp.dot(line, answer_now, precision=high, preferred_element_type=jnp.float32)
            ) / diag
            return jnp.where(rows_small == index, value, answer_now)

        solved[block] = lax.fori_loop(0, width, back_step, answer)
    return jnp.concatenate(solved, axis=0)


def shards(snapshots, base_field, design):
    panel = lax.all_to_all(snapshots, "cells", split_axis=2, concat_axis=0, tiled=True)
    run_count = panel.shape[0]
    cell_count = panel.shape[2]
    anomaly = (panel.astype(jnp.float32) - base_field.astype(jnp.float32)[None, :, :]).astype(
        jnp.bfloat16
    )
    flat = anomaly.reshape(run_count, cell_count)
    local_gram = lax.dot_general(
        flat, flat, (((1,), (1,)), ((), ())), preferred_element_type=jnp.float32
    )
    total_cells = cell_count * lax.axis_size("cells") * lax.axis_size("rep")
    gram = lax.psum(local_gram, ("cells", "rep")) / total_cells
    factor = upper_factor(gram)
    mixing = back_solve(factor, design).astype(jnp.bfloat16)
    fields = lax.dot_general(
        mixing, flat, (((0,), (0,)), ((), ())), preferred_element_type=jnp.float32
    )
    basis = fields.astype(jnp.bfloat16).reshape(mixing.shape[1], 1, cell_count)
    return (basis, factor)


def solution(mesh):
    in_specs = (P("cells", "rep", None), P("rep", "cells"), P())
    out_specs = (P(None, "rep", "cells"), P())
    return jax.shard_map(shards, mesh=mesh, in_specs=in_specs, out_specs=out_specs, check_vma=False)
```

profile of v0, /device:TPU:0, one launch (start us, length us, event | category | flops | bytes accessed | tf_op | source)
XLA Modules:
  0.0 1893.7 jit_solution(2909032308073240910)
XLA Ops:
  7.2 9.2 copy.44
  16.9 45.2 %reduce = bf16[8192,64]{1,0:T(8,128)(2,1)S(1)} reduce(bf16[8192,1,64]{2,1,0:T(2,128)(2,1)} %bitcast.266, bf16[]{:T(256)} %broadcast.518), dimensions={1}, to_apply=%bitcast.148.reduce_sub_computation | reduce | bytes 2097154
  62.1 2.7 reshape.555
  64.7 7.3 all-to-all-start
  72.3 25.4 %all-to-all-done = bf16[8,2,32768]{2,1,0:T(2,128)(2,1)S(1)} async-done(((bf16[8,2,32768]{2,1,0:T(2,128)(2,1)}), bf16[8,2,32768]{2,1,0:T(2,128)(2,1)S(1)}, u32[]{:S(2)}, u32[]{:S(2)}) %all-to-all-start) | async-done | bytes 1048608 | tf_op jit(solution)/shard_map/all_to_all | solution.py:73
  97.8 4.3 reshape.556
  102.1 8.2 copy.45
  112.1 1.7 fusion.123
  119.7 123.2 %all-reduce.2.cloned.1.call-done = f32[512,512]{1,0:T(8,128)} async-done(((f32[512,512]{1,0:T(8,128)}), f32[512,512]{1,0:T(8,128)}) %all-reduce.2.cloned.1.call-update) | async-done | bytes 1048592 | tf_op jit(solution)/shard_map/psum | solution.py:84
  244.4 96.8 %while.264 = (s32[]{:T(128)}, f32[64,512]{1,0:T(8,128)S(1)}, f32[64,512]{1,0:T(8,128)S(1)}, s32[]{:T(128)}, s32[]{:T(128)}) while((s32[]{:T(128)}, f32[64,512]{1,0:T(8,128)S(1)}, f32[64,512]{1,0:T(8,128)S(1)}, s32[]{:T(128)}, s32[]{:T(128)}) %tuple.528), condition=%wide.region_3.4_spmd.clone.clone, body=%wide.region_1.3_spmd.clone.clone.sunk | while | flops 68609 | bytes 277329 | solution.py:30
  343.0 101.1 %while.265 = (s32[]{:T(128)}, f32[64,512]{1,0:T(8,128)S(1)}, f32[64,512]{1,0:T(8,128)S(1)}, s32[]{:T(128)}, s32[]{:T(128)}, /*index=5*/s32[]{:T(128)}) while((s32[]{:T(128)}, f32[64,512]{1,0:T(8,128)S(1)}, f32[64,512]{1,0:T(8,128)S(1)}, s32[]{:T(128)}, s32[]{:T(128)}, /*index=5*/s32[]{:T(128)}) %tuple.531), condition=%wide.region_6.7_spmd.clone.clone, body=%wide.region_4.6_spmd.clone.clone.sunk | while | flops 68610 | bytes 275317 | solution.py:30
  444.7 2.0 convolution_subtract_fusion.12
  446.8 104.9 %while.266 = (s32[]{:T(128)}, f32[64,512]{1,0:T(8,128)S(1)}, f32[64,512]{1,0:T(8,128)S(1)}, s32[]{:T(128)}, s32[]{:T(128)}, /*index=5*/s32[]{:T(128)}) while((s32[]{:T(128)}, f32[64,512]{1,0:T(8,128)S(1)}, f32[64,512]{1,0:T(8,128)S(1)}, s32[]{:T(128)}, s32[]{:T(128)}, /*index=5*/s32[]{:T(128)}) %tuple.534), condition=%wide.region_9.10_spmd.clone.clone, body=%wide.region_7.9_spmd.clone.clone.sunk | while | flops 68610 | bytes 275317 | solution.py:30
  552.3 2.0 convolution_subtract_fusion.11
  554.3 103.2 %while.267 = (s32[]{:T(128)}, f32[64,512]{1,0:T(8,128)S(1)}, f32[64,512]{1,0:T(8,128)S(1)}, s32[]{:T(128)}, s32[]{:T(128)}, /*index=5*/s32[]{:T(128)}) while((s32[]{:T(128)}, f32[64,512]{1,0:T(8,128)S(1)}, f32[64,512]{1,0:T(8,128)S(1)}, s32[]{:T(128)}, s32[]{:T(128)}, /*index=5*/s32[]{:T(128)}) %tuple.537), condition=%wide.region_12.13_spmd.clone.clone, body=%wide.region_10.12_spmd.clone.clone.sunk | while | flops 68610 | bytes 275317 | solution.py:30
  658.2 2.0 convolution_subtract_fusion.10
  660.3 98.0 %while.268 = (s32[]{:T(128)}, f32[64,512]{1,0:T(8,128)S(1)}, f32[64,512]{1,0:T(8,128)S(1)}, s32[]{:T(128)}, s32[]{:T(128)}, /*index=5*/s32[]{:T(128)}) while((s32[]{:T(128)}, f32[64,512]{1,0:T(8,128)S(1)}, f32[64,512]{1,0:T(8,128)S(1)}, s32[]{:T(128)}, s32[]{:T(128)}, /*index=5*/s32[]{:T(128)}) %tuple.540), condition=%wide.region_15.16_spmd.clone.clone, body=%wide.region_13.15_spmd.clone.clone.sunk | while | flops 68610 | bytes 275317 | solution.py:30
  758.9 2.0 convolution_subtract_fusion.9
  761.0 109.0 %while.269 = (s32[]{:T(128)}, f32[64,512]{1,0:T(8,128)S(1)}, f32[64,512]{1,0:T(8,128)S(1)}, s32[]{:T(128)}, s32[]{:T(128)}, /*index=5*/s32[]{:T(128)}) while((s32[]{:T(128)}, f32[64,512]{1,0:T(8,128)S(1)}, f32[64,512]{1,0:T(8,128)S(1)}, s32[]{:T(128)}, s32[]{:T(128)}, /*index=5*/s32[]{:T(128)}) %tuple.543), condition=%wide.region_18.19_spmd.clone.clone, body=%wide.region_16.18_spmd.clone.clone.sunk | while | flops 68610 | bytes 275317 | solution.py:30
  872.1 98.0 %while.270 = (s32[]{:T(128)}, f32[64,512]{1,0:T(8,128)S(1)}, f32[64,512]{1,0:T(8,128)S(1)}, s32[]{:T(128)}, s32[]{:T(128)}, /*index=5*/s32[]{:T(128)}) while((s32[]{:T(128)}, f32[64,512]{1,0:T(8,128)S(1)}, f32[64,512]{1,0:T(8,128)S(1)}, s32[]{:T(128)}, s32[]{:T(128)}, /*index=5*/s32[]{:T(128)}) %tuple.546), condition=%wide.region_21.22_spmd.clone.clone, body=%wide.region_19.21_spmd.clone.clone.sunk | while | flops 68610 | bytes 275317 | solution.py:30
  976.3 101.1 %while.271 = (s32[]{:T(128)}, f32[64,512]{1,0:T(8,128)S(1)}, f32[64,512]{1,0:T(8,128)S(1)}, s32[]{:T(128)}, s32[]{:T(128)}, /*index=5*/s32[]{:T(128)}) while((s32[]{:T(128)}, f32[64,512]{1,0:T(8,128)S(1)}, f32[64,512]{1,0:T(8,128)S(1)}, s32[]{:T(128)}, s32[]{:T(128)}, /*index=5*/s32[]{:T(128)}) %tuple.549), condition=%wide.region_24.25_spmd.clone.clone, body=%wide.region_22.24_spmd.clone.clone.sunk | while | flops 68610 | bytes 275317 | solution.py:30
  1078.1 138.8 %while.272 = (s32[]{:T(128)}, f32[64,64]{1,0:T(8,128)S(1)}, f32[64,64]{1,0:T(8,128)}, f32[64,64]{1,0:T(8,128)S(1)}, s32[]{:T(128)}, /*index=5*/s32[]{:T(128)}, s32[]{:T(128)}, s32[]{:T(128)}) while((s32[]{:T(128)}, f32[64,64]{1,0:T(8,128)S(1)}, f32[64,64]{1,0:T(8,128)}, f32[64,64]{1,0:T(8,128)S(1)}, s32[]{:T(128)}, ...), condition=%wide.region_27.28_spmd.clone, body=%wide.region_25.27_spmd.clone.sunk | while | flops 61830 | bytes 68897 | solution.py:68
  1096.0 1.5 fusion.224
  1098.2 1.5 fusion.224
  1100.4 1.5 fusion.224
  1102.6 1.5 fusion.224
  1104.7 1.5 fusion.224
  1106.9 1.5 fusion.224
  1109.1 1.5 fusion.224
  1111.3 1.5 fusion.224
  1130.7 1.5 fusion.224
  1132.9 1.5 fusion.224
  1145.9 1.5 fusion.224
  1148.1 1.5 fusion.224
  1150.2 1.5 fusion.224
  1152.4 1.5 fusion.224
  1154.6 1.5 fusion.224
  1156.7 1.5 fusion.224
  1158.9 1.5 fusion.224
  1161.1 1.5 fusion.224
  1163.3 1.5 fusion.224
  1182.7 1.5 fusion.224
  1184.9 1.5 fusion.224
  1187.1 1.5 fusion.224
  1189.3 1.5 fusion.224
  1191.4 1.5 fusion.224
  1193.6 1.5 fusion.224
  1195.8 1.5 fusion.224
  1197.9 1.5 fusion.224
  1200.1 1.5 fusion.224
  1202.3 1.5 fusion.224
  1204.5 1.5 fusion.224
  1206.6 1.5 fusion.224
  1208.8 1.5 fusion.224
  1211.0 1.5 fusion.224
  1213.1 1.5 fusion.224
  1215.3 1.5 fusion.224
  1217.1 95.2 %while.273 = (s32[]{:T(128)}, f32[64,64]{1,0:T(8,128)S(1)}, f32[64,64]{1,0:T(8,128)S(1)}, f32[64,64]{1,0:T(8,128)S(1)}, s32[]{:T(128)}, /*index=5*/s32[]{:T(128)}, s32[]{:T(128)}, s32[]{:T(128)}) while((s32[]{:T(128)}, f32[64,64]{1,0:T(8,128)S(1)}, f32[64,64]{1,0:T(8,128)S(1)}, f32[64,64]{1,0:T(8,128)S(1)}, s32[]{:T(128)}, ...), condition=%wide.region_30.31_spmd.clone, body=%wide.region_28.30_spmd.clone.sunk | while | flops 61830 | bytes 69153 | solution.py:68
  1312.6 95.2 %while.274 = (s32[]{:T(128)}, f32[64,64]{1,0:T(8,128)S(1)}, f32[64,64]{1,0:T(8,128)S(1)}, f32[64,64]{1,0:T(8,128)S(1)}, s32[]{:T(128)}, /*index=5*/s32[]{:T(128)}, s32[]{:T(128)}, s32[]{:T(128)}) while((s32[]{:T(128)}, f32[64,64]{1,0:T(8,128)S(1)}, f32[64,64]{1,0:T(8,128)S(1)}, f32[64,64]{1,0:T(8,128)S(1)}, s32[]{:T(128)}, ...), condition=%wide.region_33.34_spmd.clone, body=%wide.region_31.33_spmd.clone.sunk | while | flops 61830 | bytes 69153 | solution.py:68
  1408.1 95.2 %while.275 = (s32[]{:T(128)}, f32[64,64]{1,0:T(8,128)S(1)}, f32[64,64]{1,0:T(8,128)S(1)}, f32[64,64]{1,0:T(8,128)S(1)}, s32[]{:T(128)}, /*index=5*/s32[]{:T(128)}, s32[]{:T(128)}, s32[]{:T(128)}) while((s32[]{:T(128)}, f32[64,64]{1,0:T(8,128)S(1)}, f32[64,64]{1,0:T(8,128)S(1)}, f32[64,64]{1,0:T(8,128)S(1)}, s32[]{:T(128)}, ...), condition=%wide.region_36.37_spmd.clone, body=%wide.region_34.36_spmd.clone.sunk | while | flops 61830 | bytes 69153 | solution.py:68
  1503.6 95.2 %while.276 = (s32[]{:T(128)}, f32[64,64]{1,0:T(8,128)S(1)}, f32[64,64]{1,0:T(8,128)S(1)}, f32[64,64]{1,0:T(8,128)S(1)}, s32[]{:T(128)}, /*index=5*/s32[]{:T(128)}, s32[]{:T(128)}, s32[]{:T(128)}) while((s32[]{:T(128)}, f32[64,64]{1,0:T(8,128)S(1)}, f32[64,64]{1,0:T(8,128)S(1)}, f32[64,64]{1,0:T(8,128)S(1)}, s32[]{:T(128)}, ...), condition=%wide.region_39.40_spmd.clone, body=%wide.region_37.39_spmd.clone.sunk | while | flops 61830 | bytes 69153 | solution.py:68
  1599.2 95.2 %while.277 = (s32[]{:T(128)}, f32[64,64]{1,0:T(8,128)S(1)}, f32[64,64]{1,0:T(8,128)S(1)}, f32[64,64]{1,0:T(8,128)S(1)}, s32[]{:T(128)}, /*index=5*/s32[]{:T(128)}, s32[]{:T(128)}, s32[]{:T(128)}) while((s32[]{:T(128)}, f32[64,64]{1,0:T(8,128)S(1)}, f32[64,64]{1,0:T(8,128)S(1)}, f32[64,64]{1,0:T(8,128)S(1)}, s32[]{:T(128)}, ...), condition=%wide.region_42.43_spmd.clone, body=%wide.region_40.42_spmd.clone.sunk | while | flops 61830 | bytes 69153 | solution.py:68
  1694.8 95.2 %while.278 = (s32[]{:T(128)}, f32[64,64]{1,0:T(8,128)S(1)}, f32[64,64]{1,0:T(8,128)S(1)}, f32[64,64]{1,0:T(8,128)S(1)}, s32[]{:T(128)}, /*index=5*/s32[]{:T(128)}, s32[]{:T(128)}, s32[]{:T(128)}) while((s32[]{:T(128)}, f32[64,64]{1,0:T(8,128)S(1)}, f32[64,64]{1,0:T(8,128)S(1)}, f32[64,64]{1,0:T(8,128)S(1)}, s32[]{:T(128)}, ...), condition=%wide.region_45.46_spmd.clone, body=%wide.region_43.45_spmd.clone.sunk | while | flops 61830 | bytes 69153 | solution.py:68
  1790.5 95.2 %while.279 = (s32[]{:T(128)}, f32[64,64]{1,0:T(8,128)S(1)}, f32[64,64]{1,0:T(8,128)S(1)}, f32[64,64]{1,0:T(8,128)S(1)}, s32[]{:T(128)}, /*index=5*/s32[]{:T(128)}, s32[]{:T(128)}, s32[]{:T(128)}) while((s32[]{:T(128)}, f32[64,64]{1,0:T(8,128)S(1)}, f32[64,64]{1,0:T(8,128)S(1)}, f32[64,64]{1,0:T(8,128)S(1)}, s32[]{:T(128)}, ...), condition=%wide.region_48.49_spmd.clone, body=%wide.region_46.48_spmd.clone.sunk | while | flops 61830 | bytes 69153 | solution.py:68
  (4705 shorter events, 1209.4 us)
Async XLA Ops:
  62.1 10.2 copy-start.18
  64.7 33.0 %all-to-all-start = ((bf16[8,2,32768]{2,1,0:T(2,128)(2,1)}), bf16[8,2,32768]{2,1,0:T(2,128)(2,1)S(1)}, u32[]{:S(2)}, u32[]{:S(2)}) async-start(bf16[8,2,32768]{2,1,0:T(2,128)(2,1)} %reshape.555), calls=%async_computation | async-start | bytes 2097152 | tf_op jit(solution)/shard_map/all_to_all | solution.py:73
  72.0 170.9 %all-reduce.2.cloned.1.call-start = ((), (), s32[]{:S(2)}) async-start(), calls=%async_computation.1 | async-start | bytes 2097152 | tf_op jit(solution)/shard_map/psum | solution.py:84
  112.1 1.8 copy-start.10
  242.9 99.0 %copy-start = (f32[512,512]{1,0:T(8,128)S(1)}, f32[512,512]{1,0:T(8,128)}, u32[]{:S(2)}) copy-start(f32[512,512]{1,0:T(8,128)} %all-reduce.2.cloned.1.call-done) | copy-start | bytes 3145732
  444.1 0.7 copy-start.1
  551.6 0.6 copy-start.3
  657.6 0.7 copy-start.5
  758.3 0.6 copy-start.7
  871.0 1.0 copy-start.9
  872.0 99.1 %copy-start.8 = (f32[64,512]{1,0:T(8,128)S(1)}, f32[64,512]{1,0:T(8,128)}, u32[]{:S(2)}) copy-start(f32[64,512]{1,0:T(8,128)} %copy-done.7) | copy-start | bytes 393220
  872.0 99.2 %copy-start.6 = (f32[64,512]{1,0:T(8,128)S(1)}, f32[64,512]{1,0:T(8,128)}, u32[]{:S(2)}) copy-start(f32[64,512]{1,0:T(8,128)} %copy-done.5) | copy-start | bytes 393220
  872.0 99.2 %copy-start.4 = (f32[64,512]{1,0:T(8,128)S(1)}, f32[64,512]{1,0:T(8,128)}, u32[]{:S(2)}) copy-start(f32[64,512]{1,0:T(8,128)} %copy-done.3) | copy-start | bytes 393220
  872.0 99.2 %copy-start.2 = (f32[64,512]{1,0:T(8,128)S(1)}, f32[64,512]{1,0:T(8,128)}, u32[]{:S(2)}) copy-start(f32[64,512]{1,0:T(8,128)} %copy-done.1) | copy-start | bytes 393220
  972.7 244.2 %copy-start.14 = (f32[64,64]{1,0:T(8,128)S(1)}, f32[64,64]{1,0:T(8,128)}, u32[]{:S(2)}) copy-start(f32[64,64]{1,0:T(8,128)} %copy.61) | copy-start | bytes 49156
  975.3 337.0 %copy-start.13 = (f32[64,64]{1,0:T(8,128)S(1)}, f32[64,64]{1,0:T(8,128)}, u32[]{:S(2)}) copy-start(f32[64,64]{1,0:T(8,128)} %copy.60) | copy-start | bytes 49156
  976.3 431.5 %copy-start.12 = (f32[64,64]{1,0:T(8,128)S(1)}, f32[64,64]{1,0:T(8,128)}, u32[]{:S(2)}) copy-start(f32[64,64]{1,0:T(8,128)} %copy.59) | copy-start | bytes 49156
  1077.4 426.0 %copy-start.17 = (f32[64,64]{1,0:T(8,128)S(1)}, f32[64,64]{1,0:T(8,128)}, u32[]{:S(2)}) copy-start(f32[64,64]{1,0:T(8,128)} %copy.58) | copy-start | bytes 49156
  1216.9 382.1 %copy-start.11 = (f32[64,64]{1,0:T(8,128)S(1)}, f32[64,64]{1,0:T(8,128)}, u32[]{:S(2)}) copy-start(f32[64,64]{1,0:T(8,128)} %copy.57) | copy-start | bytes 49156
  1312.6 382.0 %copy-start.16 = (f32[64,64]{1,0:T(8,128)S(1)}, f32[64,64]{1,0:T(8,128)}, u32[]{:S(2)}) copy-start(f32[64,64]{1,0:T(8,128)} %copy.56) | copy-start | bytes 49156
  1503.6 286.6 %copy-start.15 = (f32[64,64]{1,0:T(8,128)S(1)}, f32[64,64]{1,0:T(8,128)}, u32[]{:S(2)}) copy-start(f32[64,64]{1,0:T(8,128)} %copy.55) | copy-start | bytes 49156
Sparse Core Ops, SparseCore 0:
  114.0 128.9 all-reduce.1
where the time goes:
time: 1910 us; the launch traced here: 1890 us
  other arithmetic  786 us (41%)
  matrix products  460 us (24%)
  loops' own time  383 us (20%)
  waiting for transfers between devices  149 us (8%)
  local copies, waits for them, and re-layouts  92.9 us (5%)
    dot_general x512, matrix products, back_step(): jnp.dot(line, answer_now, precision=high, preferred_element_type=jnp.floa...  445 us
    another operation x8, loops' own time, upper_factor(): panel, result = lax.fori_loop(0, width, upper_step, (panel, result))  378 us
    reduce_sum x512, other arithmetic, upper_step(): pivot = jnp.sqrt(jnp.sum(jnp.where(where, line, 0.0)))  331 us
    reduce_sum x512, other arithmetic, back_step(): diag = jnp.sum(jnp.where(rows_small.T == index, line, 0.0))  313 us
    psum x1, waiting for transfers between devices, shards(): gram = lax.psum(local_gram, ('cells', 'rep')) / total_cells  123 us
    unnamed x16, other arithmetic  45.3 us
    sub x512, other arithmetic, upper_step(): panel_now = panel_now - coeffs.T * line  44.2 us
    select_n x512, other arithmetic, back_step(): return jnp.where(rows_small == index, value, answer_now)  39.1 us

commit v1 on v0

v1 whole, which is shorter than its diff:
```python
import jax
import jax.numpy as jnp
from jax import lax
from jax.experimental import pallas as pl
from jax.experimental.pallas import tpu as pltpu
from jax.sharding import PartitionSpec as P

BLOCK = 128
HALF = BLOCK // 2
LANES = 128
AXES = ("cells", "rep")
HIGH = lax.Precision.HIGHEST
NARROW = (((1,), (0,)), ((), ()))
FIRST = (((0,), (0,)), ((), ()))
LAST = (((1,), (1,)), ((), ()))


def dot(a, b, dims=NARROW):
    return lax.dot_general(a, b, dims, precision=HIGH, preferred_element_type=jnp.float32)


def upper_pairs(count):
    return [(i, j) for i in range(count) for j in range(i, count)]


def factor_half(square):
    tile = (8, LANES)
    sub = lax.broadcasted_iota(jnp.int32, tile, 0)
    eye = (
        lax.broadcasted_iota(jnp.int32, (HALF, HALF), 0)
        == lax.broadcasted_iota(jnp.int32, (HALF, HALF), 1)
    ).astype(jnp.float32)
    both = jnp.concatenate([square, eye], axis=1)
    count = HALF // 8
    strips = [both[8 * j : 8 * j + 8, :] for j in range(count)]
    for m in range(count):
        spread = {}
        for j in range(m, count):
            for t in range(8):
                at = 8 * m + t
                spread[j, t] = jnp.broadcast_to(strips[j][:, at : at + 1], tile)
        for t in range(8):
            root = lax.rsqrt(jnp.broadcast_to(spread[m, t][t : t + 1, :], tile))
            inverse = root * root
            row = jnp.broadcast_to(strips[m][t : t + 1, :], tile)
            scaled = row * inverse
            later = {
                u: jnp.broadcast_to(spread[m, u][t : t + 1, :], tile) * inverse
                for u in range(t + 1, 8)
            }
            for j in range(m, count):
                column = spread[j, t]
                if j == m:
                    column = jnp.where(sub > t, column, 0.0)
                for u in range(t + 1, 8):
                    spread[j, u] = spread[j, u] - column * later[u]
                updated = strips[j] - column * scaled
                strips[j] = jnp.where(sub == t, row * root, updated) if j == m else updated
    return jnp.concatenate(strips, axis=0)


def upper_part(square):
    shape = square.shape
    keep = lax.broadcasted_iota(jnp.int32, shape, 0) <= lax.broadcasted_iota(jnp.int32, shape, 1)
    return jnp.where(keep, square, 0.0)


def factor_block(square):
    low, high = slice(0, HALF), slice(HALF, BLOCK)
    both = factor_half(square[low, low])
    r00, v00 = upper_part(both[:, :HALF]), both[:, HALF:]
    r01 = dot(v00, square[low, high])
    both = factor_half(square[high, high] - dot(r01, r01, FIRST))
    r11, v11 = upper_part(both[:, :HALF]), both[:, HALF:]
    v10 = -dot(v11, dot(r01, v00, FIRST))
    zero = jnp.zeros((HALF, HALF), jnp.float32)
    factor = jnp.concatenate(
        [jnp.concatenate([r00, r01], axis=1), jnp.concatenate([zero, r11], axis=1)], axis=0
    )
    inverse = jnp.concatenate(
        [jnp.concatenate([v00, zero], axis=1), jnp.concatenate([v10, v11], axis=1)], axis=0
    )
    return factor, inverse


def gram_kernel(panel_ref, base_ref, anomaly_ref, gram_ref):
    count = panel_ref.shape[0] // BLOCK
    anomaly_ref[...] = (
        panel_ref[...].astype(jnp.float32) - base_ref[...].astype(jnp.float32)
    ).astype(jnp.bfloat16)
    at = 0
    for i in range(count):
        rows = anomaly_ref[pl.ds(i * BLOCK, BLOCK), :]
        rest = anomaly_ref[pl.ds(i * BLOCK, (count - i) * BLOCK), :]
        part = lax.dot_general(rows, rest, LAST, preferred_element_type=jnp.float32)
        for j in range(count - i):
            gram_ref[pl.ds(at * BLOCK, BLOCK), :] = part[:, j * BLOCK : (j + 1) * BLOCK]
            at += 1


def factor_kernel(
    scale, place_ref, mine_ref, other_ref, design_ref, anomaly_ref, basis_ref, factor_ref, gram_ref, inv_ref
):
    count = factor_ref.shape[0] // BLOCK
    slots, size = mine_ref.shape[0], mine_ref.shape[1]
    half, quarter = place_ref[0], place_ref[1]
    for slot in range(slots):
        piece = lax.bitwise_xor(quarter, slot)
        for side, ref in ((half, mine_ref), (1 - half, other_ref)):
            start = pl.multiple_of((side * slots + piece) * size, 8)
            gram_ref[pl.ds(start, size), :] = ref[slot] * scale
    pairs = upper_pairs(count)
    where = {pair: at for at, pair in enumerate(pairs)}

    def gram_at(i, j):
        return pl.ds(where[i, j] * BLOCK, BLOCK)

    def span(i):
        return pl.ds(i * BLOCK, BLOCK)

    for k in range(count):
        factor, inverse = factor_block(gram_ref[gram_at(k, k), :])
        factor_ref[span(k), span(k)] = factor
        rows = {}
        for j in range(k + 1, count):
            rows[j] = dot(inverse, gram_ref[gram_at(k, j), :])
            factor_ref[span(k), span(j)] = rows[j]
            factor_ref[span(j), span(k)] = jnp.zeros((BLOCK, BLOCK), jnp.float32)
        for i in range(k + 1, count):
            for j in range(i, count):
                gram_ref[gram_at(i, j), :] = gram_ref[gram_at(i, j), :] - dot(
                    rows[i], rows[j], FIRST
                )
        done = {}
        for j in range(k):
            done[j] = dot(inverse, inv_ref[span(k), span(j)])
            inv_ref[span(k), span(j)] = done[j]
        done[k] = inverse
        inv_ref[span(k), span(k)] = inverse
        for i in range(k + 1, count):
            for j in range(k + 1):
                old = inv_ref[span(i), span(j)] if j < k else 0.0
                inv_ref[span(i), span(j)] = old - dot(rows[i], done[j], FIRST)
    columns = []
    for j in range(count):
        tail = pl.ds(j * BLOCK, (count - j) * BLOCK)
        columns.append(dot(design_ref[tail, :], inv_ref[tail, span(j)], FIRST))
    mixing = jnp.concatenate(columns, axis=1).astype(jnp.bfloat16)
    basis_ref[...] = lax.dot_general(
        mixing, anomaly_ref[...], NARROW, preferred_element_type=jnp.float32
    ).astype(jnp.bfloat16)


def swap(value, mask, devices):
    return lax.ppermute(value, AXES, [(i, i ^ mask) for i in range(devices)])


def shards(snapshots, base_field, design):
    n_cells, n_rep = lax.axis_size("cells"), lax.axis_size("rep")
    devices = n_cells * n_rep
    local_runs = snapshots.shape[0]
    runs, modes = design.shape
    slab = base_field.shape[1]
    blocks = runs // BLOCK
    packed = len(upper_pairs(blocks)) * BLOCK
    slabs = snapshots.reshape(local_runs, n_cells, slab).transpose(1, 0, 2)
    panel = lax.all_to_all(slabs, "cells", split_axis=0, concat_axis=0, tiled=True)
    vmem = pl.BlockSpec(memory_space=pltpu.VMEM)
    anomaly, gram = pl.pallas_call(
        gram_kernel,
        out_shape=(
            jax.ShapeDtypeStruct((runs, slab), jnp.bfloat16),
            jax.ShapeDtypeStruct((packed, LANES), jnp.float32),
        ),
        in_specs=[vmem, vmem],
        out_specs=(vmem, vmem),
        compiler_params=pltpu.CompilerParams(vmem_limit_bytes=32 * 2**20),
    )(panel.reshape(runs, slab), base_field)

    me = lax.axis_index("cells") * n_rep + lax.axis_index("rep")
    half, quarter = me % 2, (me // 2) % 4
    halves = gram.reshape(2, packed // 2, LANES)
    got = swap(lax.dynamic_index_in_dim(halves, 1 - half, 0, keepdims=False), 1, devices)
    own = lax.dynamic_index_in_dim(halves, half, 0, keepdims=False) + got
    quarters = own.reshape(4, packed // 8, LANES)
    total = lax.dynamic_index_in_dim(quarters, quarter, 0, keepdims=False)
    parts = [
        swap(lax.dynamic_index_in_dim(quarters, quarter ^ m, 0, keepdims=False), 2 * m, devices)
        for m in (1, 2, 3)
    ]
    for part in parts:
        total = total + part
    mask = 8
    while mask < devices:
        total = total + swap(total, mask, devices)
        mask *= 2
    mine = jnp.stack([total] + [swap(total, 2 * m, devices) for m in (1, 2, 3)])
    other = swap(mine, 1, devices)

    def kernel(*refs):
        factor_kernel(1.0 / (slab * devices), *refs)

    basis, factor = pl.pallas_call(
        kernel,
        out_shape=(
            jax.ShapeDtypeStruct((modes, slab), jnp.bfloat16),
            jax.ShapeDtypeStruct((runs, runs), jnp.float32),
        ),
        in_specs=[pl.BlockSpec(memory_space=pltpu.SMEM), vmem, vmem, vmem, vmem],
        out_specs=(vmem, vmem),
        scratch_shapes=[
            pltpu.VMEM((packed, LANES), jnp.float32),
            pltpu.VMEM((runs, runs), jnp.float32),
        ],
        compiler_params=pltpu.CompilerParams(vmem_limit_bytes=32 * 2**20),
    )(jnp.stack([half, quarter]).astype(jnp.int32), mine, other, design, anomaly)
    return (basis.reshape(modes, 1, slab), factor)


def solution(mesh):
    in_specs = (P("cells", "rep", None), P("rep", "cells"), P())
    out_specs = (P(None, "rep", "cells"), P())
    return jax.shard_map(shards, mesh=mesh, in_specs=in_specs, out_specs=out_specs, check_vma=False)
```

time: 1910 us -> 91.1 us (0.05)
  other arithmetic: 786 us -> 0.17 us
  matrix products: 460 us -> 0 us
  loops' own time: 383 us -> 0 us
  waiting for transfers between devices: 149 us -> 46.1 us
  local copies, waits for them, and re-layouts: 92.9 us -> 4.35 us
  Pallas kernels: 0 us -> 24.8 us
    reduce_sum x1024 -> x0, other arithmetic: 643 us -> none  [the longest x512 331 us: upper_step(): pivot = jnp.sqrt(jnp.sum(jnp.where(where, line, 0.0)))]
    dot_general x528 -> x0, matrix products: 460 us -> none  [the longest x512 445 us: back_step(): jnp.dot(line, answer_now, precision=high, preferred_element_type=jnp.floa...]
    another operation x16 -> x0, loops' own time: 383 us -> none  [the longest x8 378 us: upper_factor(): panel, result = lax.fori_loop(0, width, upper_step, (panel, result))]
    psum x1 -> x0, waiting for transfers between devices: 123 us -> none  [shards(): gram = lax.psum(local_gram, ('cells', 'rep')) / total_cells]
    select_n x1024 -> x0, other arithmetic: 47.1 us -> none  [the longest x512 39.1 us: back_step(): return jnp.where(rows_small == index, value, answer_now)]
    unnamed x16 -> x0, other arithmetic: 45.3 us -> none
    sub x513 -> x0, other arithmetic: 45.1 us -> none  [the longest x512 44.2 us: upper_step(): panel_now = panel_now - coeffs.T * line]
    dynamic_update_slice x512 -> x0, local copies, waits for them, and re-layouts: 32.1 us -> none  [upper_step(): result_now = lax.dynamic_update_index_in_dim(result_now, line[0], index, 0)]
where the time goes in v1:
time: 91.1 us; the launch traced here: 90.9 us
  waiting for transfers between devices  46.1 us (51%)
  Pallas kernels  24.8 us (27%)
  starting transfers between devices  14.6 us (16%)
  local copies, waits for them, and re-layouts  4.35 us (5%)
    all_to_all x1, waiting for transfers between devices, shards(): lax.all_to_all(slabs, 'cells', split_axis=0, concat_axis=0, tiled=True)  25.8 us
    pallas_call x1, Pallas kernels, shards(): pl.pallas_call(kernel, out_shape=(jax.ShapeDtypeStruct((modes, slab), jnp...  23.9 us
    ppermute x10, waiting for transfers between devices, swap(): return lax.ppermute(value, AXES, [(i, i ^ mask) for i in range(devices)])  20.3 us
    ppermute x10, starting transfers between devices, swap(): return lax.ppermute(value, AXES, [(i, i ^ mask) for i in range(devices)])  7.39 us
    all_to_all x1, starting transfers between devices, shards(): lax.all_to_all(slabs, 'cells', split_axis=0, concat_axis=0, tiled=True)  7.25 us
    unnamed x6, local copies, waits for them, and re-layouts  2.75 us
  transfers between devices with their start and end apart: 11, of which 10 were waited for; matrix products, arithmetic and copies ran while one was open for 0% of the time, Pallas kernels for 0%

profile of v1, /device:TPU:0, one launch (start us, length us, event | category | flops | bytes accessed | tf_op | source)
XLA Modules:
  0.0 90.9 jit_solution(6588210300215073734)
XLA Ops:
  0.6 1.8 %copy.7 = bf16[8,8,8,1024]{3,2,1,0:T(8,128)(2,1)S(1)} copy(bf16[8,8,8,1024]{3,1,2,0:T(8,128)(2,1)} %bitcast.39) | data formatting | bytes 2097152
  2.5 1.5 %copy.9 = bf16[64,8,1024]{2,0,1:T(8,128)(2,1)} copy(bf16[64,8,1024]{2,1,0:T(8,128)(2,1)S(1)} %bitcast.36) | data formatting | bytes 2097152 | tf_op jit(solution)/shard_map/reshape | solution.py:166
  4.0 7.3 %all-to-all-start = ((bf16[8,64,1024]{2,1,0:T(8,128)(2,1)}), bf16[8,64,1024]{2,1,0:T(8,128)(2,1)S(1)}, u32[]{:S(2)}, u32[]{:S(2)}) async-start(bf16[8,64,1024]{2,1,0:T(8,128)(2,1)} %bitcast.32), calls=%async_computation | async-start | bytes 2097152 | tf_op jit(solution)/shard_map/all_to_all | solution.py:167
  11.3 0.0 copy-start
  11.3 25.8 %all-to-all-done = bf16[8,64,1024]{2,1,0:T(8,128)(2,1)S(1)} async-done(((bf16[8,64,1024]{2,1,0:T(8,128)(2,1)}), bf16[8,64,1024]{2,1,0:T(8,128)(2,1)S(1)}, u32[]{:S(2)}, u32[]{:S(2)}) %all-to-all-start) | async-done | bytes 1048608 | tf_op jit(solution)/shard_map/all_to_all | solution.py:167
  37.0 0.0 copy-done
  37.0 1.0 %shard_map.50 = (bf16[512,1024]{1,0:T(8,128)(2,1)S(1)}, f32[1280,128]{1,0:T(8,128)S(1)}) custom-call(bf16[512,1024]{1,0:T(8,128)(2,1)S(1)} %bitcast.33, bf16[1,1024]{1,0:T(2,128)(2,1)S(1)} %copy-done), custom_call_target="tpu_custom_call" | custom-call | tf_op jit(solution)/shard_map/pallas_call | solution.py:169
  38.0 0.1 collective-permute-start
  38.2 1.6 %collective-permute-done = f32[640,128]{1,0:T(8,128)S(1)} collective-permute-done((f32[640,128]{1,0:T(8,128)S(1)}, f32[640,128]{1,0:T(8,128)S(1)}, u32[]{:S(2)}, u32[]{:S(2)}) %collective-permute-start) | collective-permute-done | bytes 327712 | tf_op jit(solution)/shard_map/ppermute | solution.py:155
  39.8 1.6 %collective-permute-start.1 = (f32[160,128]{1,0:T(8,128)S(1)}, f32[160,128]{1,0:T(8,128)S(1)}, u32[]{:S(2)}, u32[]{:S(2)}) collective-permute-start(f32[160,128]{1,0:T(8,128)S(1)} %get-tuple-element.10), channel_id=1, source_target_pairs={{0,2},{1,3},{2,0},{3,1},{4,6},{5,7},{6,4},{7,5},{8,10},{9,11},{10,... | collective-permute-start | bytes 245768 | tf_op jit(solution)/shard_map/ppermute | solution.py:155
  41.4 1.4 %collective-permute-start.3 = (f32[160,128]{1,0:T(8,128)S(1)}, f32[160,128]{1,0:T(8,128)S(1)}, u32[]{:S(2)}, u32[]{:S(2)}) collective-permute-start(f32[160,128]{1,0:T(8,128)S(1)} %get-tuple-element.11), channel_id=1, source_target_pairs={{0,6},{1,7},{2,4},{3,5},{4,2},{5,3},{6,0},{7,1},{8,14},{9,15},{10,... | collective-permute-start | bytes 245768 | tf_op jit(solution)/shard_map/ppermute | solution.py:155
  42.7 0.6 collective-permute-start.2
  43.4 1.2 %collective-permute-done.1 = f32[160,128]{1,0:T(8,128)S(1)} collective-permute-done((f32[160,128]{1,0:T(8,128)S(1)}, f32[160,128]{1,0:T(8,128)S(1)}, u32[]{:S(2)}, u32[]{:S(2)}) %collective-permute-start.1) | collective-permute-done | bytes 81952 | tf_op jit(solution)/shard_map/ppermute | solution.py:155
  44.5 3.0 %collective-permute-done.3 = f32[160,128]{1,0:T(8,128)S(1)} collective-permute-done((f32[160,128]{1,0:T(8,128)S(1)}, f32[160,128]{1,0:T(8,128)S(1)}, u32[]{:S(2)}, u32[]{:S(2)}) %collective-permute-start.3) | collective-permute-done | bytes 81952 | tf_op jit(solution)/shard_map/ppermute | solution.py:155
  47.6 0.0 collective-permute-done.2
  47.6 0.1 collective-permute-start.4
  47.7 4.4 %collective-permute-done.4 = f32[160,128]{1,0:T(8,128)S(1)} collective-permute-done((f32[160,128]{1,0:T(8,128)S(1)}, f32[160,128]{1,0:T(8,128)S(1)}, u32[]{:S(2)}, u32[]{:S(2)}) %collective-permute-start.4) | collective-permute-done | bytes 81952 | tf_op jit(solution)/shard_map/ppermute | solution.py:155
  52.1 0.1 collective-permute-start.5
  52.2 5.6 %collective-permute-done.5 = f32[160,128]{1,0:T(8,128)S(1)} collective-permute-done((f32[160,128]{1,0:T(8,128)S(1)}, f32[160,128]{1,0:T(8,128)S(1)}, u32[]{:S(2)}, u32[]{:S(2)}) %collective-permute-start.5) | collective-permute-done | bytes 81952 | tf_op jit(solution)/shard_map/ppermute | solution.py:155
  57.9 2.1 %collective-permute-start.8 = (f32[160,128]{1,0:T(8,128)S(1)}, f32[160,128]{1,0:T(8,128)S(1)}, u32[]{:S(2)}, u32[]{:S(2)}) collective-permute-start(f32[160,128]{1,0:T(8,128)S(1)} %add.64), channel_id=1, source_target_pairs={{0,6},{1,7},{2,4},{3,5},{4,2},{5,3},{6,0},{7,1},{8,14},{9,15},{10,... | collective-permute-start | bytes 245768 | tf_op jit(solution)/shard_map/ppermute | solution.py:155
  60.0 0.8 collective-permute-start.7
  60.9 0.6 collective-permute-start.6
  61.4 1.9 %collective-permute-done.8 = f32[160,128]{1,0:T(8,128)S(1)} collective-permute-done((f32[160,128]{1,0:T(8,128)S(1)}, f32[160,128]{1,0:T(8,128)S(1)}, u32[]{:S(2)}, u32[]{:S(2)}) %collective-permute-start.8) | collective-permute-done | bytes 81952 | tf_op jit(solution)/shard_map/ppermute | solution.py:155
  63.3 1.2 %collective-permute-done.7 = f32[160,128]{1,0:T(8,128)S(1)} collective-permute-done((f32[160,128]{1,0:T(8,128)S(1)}, f32[160,128]{1,0:T(8,128)S(1)}, u32[]{:S(2)}, u32[]{:S(2)}) %collective-permute-start.7) | collective-permute-done | bytes 81952 | tf_op jit(solution)/shard_map/ppermute | solution.py:155
  64.5 0.8 collective-permute-done.6
  65.3 0.0 copy-start.1
  65.3 0.1 collective-permute-start.9
  65.4 0.8 copy-done.1
  66.2 0.1 copy.6.refs_3_
  66.3 0.1 pad_add_fusion.refs_0_
  66.4 0.6 collective-permute-done.9.refs_2_
  67.0 23.9 %shard_map.51 = (bf16[64,1024]{1,0:T(8,128)(2,1)}, f32[512,512]{1,0:T(8,128)}) custom-call(s32[2]{0:T(128)S(1)} %pad_add_fusion.refs_0_, f32[4,160,128]{2,1,0:T(8,128)S(1)} %pad_maximum_fusion.refs_1_, f32[4,160,128]{2,1,0:T(8,128)S(1)} %collective-permute-done.9.refs_2_, f32[512,64]{1,0:T(8,128)S(1)} %copy.6.refs_3_, ...), custom_call_target="tpu_custom_call" | custom-call | tf_op jit(solution)/shard_map/pallas_call | solution.py:203
  (7 shorter events, 0.2 us)
Async XLA Ops:
  4.0 33.0 %all-to-all-start = ((bf16[8,64,1024]{2,1,0:T(8,128)(2,1)}), bf16[8,64,1024]{2,1,0:T(8,128)(2,1)S(1)}, u32[]{:S(2)}, u32[]{:S(2)}) async-start(bf16[8,64,1024]{2,1,0:T(8,128)(2,1)} %bitcast.32), calls=%async_computation | async-start | bytes 2097152 | tf_op jit(solution)/shard_map/all_to_all | solution.py:167
  11.3 25.8 %copy-start = (bf16[1,1024]{1,0:T(2,128)(2,1)S(1)}, bf16[1,1024]{1,0:T(2,128)(2,1)}, u32[]{:S(2)}) copy-start(bf16[1,1024]{1,0:T(2,128)(2,1)} %base_ref.1) | copy-start | bytes 6148
  38.0 1.7 %collective-permute-start = (f32[640,128]{1,0:T(8,128)S(1)}, f32[640,128]{1,0:T(8,128)S(1)}, u32[]{:S(2)}, u32[]{:S(2)}) collective-permute-start(f32[640,128]{1,0:T(8,128)S(1)} %dynamic-slice_bitcast_fusion), channel_id=1, source_target_pairs={{0,1},{1,0},{2,3},{3,2},{4,5},{5,4},{6,7},{7,6},{8,9},{9,8},{10,11... | collective-permute-start | bytes 983048 | tf_op jit(solution)/shard_map/ppermute | solution.py:155
  39.8 4.7 %collective-permute-start.1 = (f32[160,128]{1,0:T(8,128)S(1)}, f32[160,128]{1,0:T(8,128)S(1)}, u32[]{:S(2)}, u32[]{:S(2)}) collective-permute-start(f32[160,128]{1,0:T(8,128)S(1)} %get-tuple-element.10), channel_id=1, source_target_pairs={{0,2},{1,3},{2,0},{3,1},{4,6},{5,7},{6,4},{7,5},{8,10},{9,11},{10,... | collective-permute-start | bytes 245768 | tf_op jit(solution)/shard_map/ppermute | solution.py:155
  41.4 6.2 %collective-permute-start.3 = (f32[160,128]{1,0:T(8,128)S(1)}, f32[160,128]{1,0:T(8,128)S(1)}, u32[]{:S(2)}, u32[]{:S(2)}) collective-permute-start(f32[160,128]{1,0:T(8,128)S(1)} %get-tuple-element.11), channel_id=1, source_target_pairs={{0,6},{1,7},{2,4},{3,5},{4,2},{5,3},{6,0},{7,1},{8,14},{9,15},{10,... | collective-permute-start | bytes 245768 | tf_op jit(solution)/shard_map/ppermute | solution.py:155
  42.7 4.8 %collective-permute-start.2 = (f32[160,128]{1,0:T(8,128)S(1)}, f32[160,128]{1,0:T(8,128)S(1)}, u32[]{:S(2)}, u32[]{:S(2)}) collective-permute-start(f32[160,128]{1,0:T(8,128)S(1)} %get-tuple-element.12), channel_id=1, source_target_pairs={{0,4},{1,5},{2,6},{3,7},{4,0},{5,1},{6,2},{7,3},{8,12},{9,13},{10,... | collective-permute-start | bytes 245768 | tf_op jit(solution)/shard_map/ppermute | solution.py:155
  47.6 4.5 %collective-permute-start.4 = (f32[160,128]{1,0:T(8,128)S(1)}, f32[160,128]{1,0:T(8,128)S(1)}, u32[]{:S(2)}, u32[]{:S(2)}) collective-permute-start(f32[160,128]{1,0:T(8,128)S(1)} %fusion.1), channel_id=1, source_target_pairs={{0,8},{1,9},{2,10},{3,11},{4,12},{5,13},{6,14},{7,15},{8,0},{9,1},... | collective-permute-start | bytes 245768 | tf_op jit(solution)/shard_map/ppermute | solution.py:155
  52.1 5.7 %collective-permute-start.5 = (f32[160,128]{1,0:T(8,128)S(1)}, f32[160,128]{1,0:T(8,128)S(1)}, u32[]{:S(2)}, u32[]{:S(2)}) collective-permute-start(f32[160,128]{1,0:T(8,128)S(1)} %add.63), channel_id=1, source_target_pairs={{0,16},{1,17},{2,18},{3,19},{4,20},{5,21},{6,22},{7,23},{8,24},{9,... | collective-permute-start | bytes 245768 | tf_op jit(solution)/shard_map/ppermute | solution.py:155
  57.9 5.4 %collective-permute-start.8 = (f32[160,128]{1,0:T(8,128)S(1)}, f32[160,128]{1,0:T(8,128)S(1)}, u32[]{:S(2)}, u32[]{:S(2)}) collective-permute-start(f32[160,128]{1,0:T(8,128)S(1)} %add.64), channel_id=1, source_target_pairs={{0,6},{1,7},{2,4},{3,5},{4,2},{5,3},{6,0},{7,1},{8,14},{9,15},{10,... | collective-permute-start | bytes 245768 | tf_op jit(solution)/shard_map/ppermute | solution.py:155
  60.0 4.4 %collective-permute-start.7 = (f32[160,128]{1,0:T(8,128)S(1)}, f32[160,128]{1,0:T(8,128)S(1)}, u32[]{:S(2)}, u32[]{:S(2)}) collective-permute-start(f32[160,128]{1,0:T(8,128)S(1)} %add.64), channel_id=1, source_target_pairs={{0,4},{1,5},{2,6},{3,7},{4,0},{5,1},{6,2},{7,3},{8,12},{9,13},{10,... | collective-permute-start | bytes 245768 | tf_op jit(solution)/shard_map/ppermute | solution.py:155
  60.9 4.4 %collective-permute-start.6 = (f32[160,128]{1,0:T(8,128)S(1)}, f32[160,128]{1,0:T(8,128)S(1)}, u32[]{:S(2)}, u32[]{:S(2)}) collective-permute-start(f32[160,128]{1,0:T(8,128)S(1)} %add.64), channel_id=1, source_target_pairs={{0,2},{1,3},{2,0},{3,1},{4,6},{5,7},{6,4},{7,5},{8,10},{9,11},{10,... | collective-permute-start | bytes 245768 | tf_op jit(solution)/shard_map/ppermute | solution.py:155
  65.3 0.9 copy-start.1
  65.3 1.7 %collective-permute-start.9 = (f32[4,160,128]{2,1,0:T(8,128)S(1)}, f32[4,160,128]{2,1,0:T(8,128)S(1)}, u32[]{:S(2)}, u32[]{:S(2)}) collective-permute-start(f32[4,160,128]{2,1,0:T(8,128)S(1)} %pad_maximum_fusion.refs_1_), channel_id=1, source_target_pairs={{0,1},{1,0},{2,3},{3,2},{4,5},{5,4},{6,7},{7,6},{8,9},{9,8},{10,11... | collective-permute-start | bytes 983048 | tf_op jit(solution)/shard_map/ppermute | solution.py:155

commit v2 on v1

--- a/solution.py
+++ b/solution.py
@@ -1,3 +1,5 @@
+import functools
+
 import jax
 import jax.numpy as jnp
 from jax import lax
@@ -83,11 +85,24 @@
     return factor, inverse
 
 
-def gram_kernel(panel_ref, base_ref, anomaly_ref, gram_ref):
-    count = panel_ref.shape[0] // BLOCK
-    anomaly_ref[...] = (
-        panel_ref[...].astype(jnp.float32) - base_ref[...].astype(jnp.float32)
-    ).astype(jnp.bfloat16)
+def pack_kernel(partners, waited, place_ref, field_ref, *refs):
+    piece_refs = refs[waited:]
+    slab = piece_refs[0].shape[1]
+    for partner, piece_ref in zip(partners, piece_refs):
+        start = lax.bitwise_xor(place_ref[0], partner) * slab
+        piece_ref[...] = field_ref[:, pl.ds(pl.multiple_of(start, LANES), slab)]
+
+
+def gram_kernel(place_ref, *refs):
+    *piece_refs, base_ref, anomaly_ref, gram_ref = refs
+    count = anomaly_ref.shape[0] // BLOCK
+    base = base_ref[...].astype(jnp.float32)
+    for partner, piece_ref in enumerate(piece_refs):
+        size = piece_ref.shape[0]
+        start = lax.bitwise_xor(place_ref[0], partner) * size if len(piece_refs) > 1 else 0
+        anomaly_ref[pl.ds(pl.multiple_of(start, size), size), :] = (
+            piece_ref[...].astype(jnp.float32) - base
+        ).astype(jnp.bfloat16)
     at = 0
     for i in range(count):
         rows = anomaly_ref[pl.ds(i * BLOCK, BLOCK), :]
@@ -163,19 +178,38 @@
     slab = base_field.shape[1]
     blocks = runs // BLOCK
     packed = len(upper_pairs(blocks)) * BLOCK
-    slabs = snapshots.reshape(local_runs, n_cells, slab).transpose(1, 0, 2)
-    panel = lax.all_to_all(slabs, "cells", split_axis=0, concat_axis=0, tiled=True)
     vmem = pl.BlockSpec(memory_space=pltpu.VMEM)
+    smem = pl.BlockSpec(memory_space=pltpu.SMEM)
+    column = lax.axis_index("cells").astype(jnp.int32).reshape(1)
+    if n_cells == 8 and local_runs % 16 == 0:
+        field = snapshots.reshape(local_runs, n_cells * slab)
+        pieces = {}
+        for partners, after in (((4, 5, 3, 0), ()), ((6, 7, 2, 1), (3,))):
+            packed_pieces = pl.pallas_call(
+                functools.partial(pack_kernel, partners, len(after)),
+                out_shape=[jax.ShapeDtypeStruct((local_runs, slab), jnp.bfloat16)] * len(partners),
+                in_specs=[smem, vmem] + [pl.BlockSpec(memory_space=pl.ANY)] * len(after),
+                out_specs=[vmem] * len(partners),
+                compiler_params=pltpu.CompilerParams(vmem_limit_bytes=16 * 2**20),
+            )(column, field, *[pieces[m] for m in after])
+            for m, piece in zip(partners, packed_pieces):
+                route = [(i, i ^ m) for i in range(n_cells)]
+                pieces[m] = lax.ppermute(piece, "cells", route) if m else piece
+        panel = [pieces[m] for m in range(n_cells)]
+    else:
+        slabs = snapshots.reshape(local_runs, n_cells, slab).transpose(1, 0, 2)
+        moved = lax.all_to_all(slabs, "cells", split_axis=0, concat_axis=0, tiled=True)
+        panel = [moved.reshape(runs, slab)]
     anomaly, gram = pl.pallas_call(
         gram_kernel,
         out_shape=(
             jax.ShapeDtypeStruct((runs, slab), jnp.bfloat16),
             jax.ShapeDtypeStruct((packed, LANES), jnp.float32),
         ),
-        in_specs=[vmem, vmem],
+        in_specs=[smem] + [vmem] * (len(panel) + 1),
         out_specs=(vmem, vmem),
         compiler_params=pltpu.CompilerParams(vmem_limit_bytes=32 * 2**20),
-    )(panel.reshape(runs, slab), base_field)
+    )(column, *panel, base_field)
 
     me = lax.axis_index("cells") * n_rep + lax.axis_index("rep")
     half, quarter = me % 2, (me // 2) % 4
@@ -206,7 +240,7 @@
             jax.ShapeDtypeStruct((modes, slab), jnp.bfloat16),
             jax.ShapeDtypeStruct((runs, runs), jnp.float32),
         ),
-        in_specs=[pl.BlockSpec(memory_space=pltpu.SMEM), vmem, vmem, vmem, vmem],
+        in_specs=[smem, vmem, vmem, vmem, vmem],
         out_specs=(vmem, vmem),
         scratch_shapes=[
             pltpu.VMEM((packed, LANES), jnp.float32),

time: 91.1 us -> 84.1 us (0.923)
  waiting for transfers between devices: 46.1 us -> 24.3 us
  starting transfers between devices: 14.6 us -> 31.2 us
  local copies, waits for them, and re-layouts: 4.35 us -> 2.2 us
    all_to_all x1 -> x0, waiting for transfers between devices: 25.8 us -> none  [shards(): lax.all_to_all(slabs, 'cells', split_axis=0, concat_axis=0, tiled=True)]
    ppermute x0 -> x7, starting transfers between devices: none -> 15.3 us  [shards(): pieces[m] = lax.ppermute(piece, 'cells', route) if m else piece]
    ppermute x0 -> x7, waiting for transfers between devices: none -> 9.02 us  [shards(): pieces[m] = lax.ppermute(piece, 'cells', route) if m else piece]
    ppermute x10, starting transfers between devices: 7.39 us -> 15.9 us  [swap(): return lax.ppermute(value, AXES, [(i, i ^ mask) for i in range(devices)])]
    all_to_all x1 -> x0, starting transfers between devices: 7.25 us -> none  [shards(): lax.all_to_all(slabs, 'cells', split_axis=0, concat_axis=0, tiled=True)]
    ppermute x10, waiting for transfers between devices: 20.3 us -> 15.3 us  [swap(): return lax.ppermute(value, AXES, [(i, i ^ mask) for i in range(devices)])]
    reshape x1 -> x0, local copies, waits for them, and re-layouts: 1.55 us -> none  [shards(): slabs = snapshots.reshape(local_runs, n_cells, slab).transpose(1, 0, 2)]
    unnamed x6 -> x7, local copies, waits for them, and re-layouts: 2.75 us -> 2.14 us
  transfers between devices with their start and end apart: 11 -> 17, of which waited for: 10 -> 13; matrix products, arithmetic and copies ran while one was open for 0% -> 0% of each run, Pallas kernels for 0% -> 0%
where the time goes in v2:
time: 84.1 us; the launch traced here: 84 us
  starting transfers between devices  31.2 us (37%)
  Pallas kernels  25.2 us (30%)
  waiting for transfers between devices  24.3 us (29%)
  local copies, waits for them, and re-layouts  2.2 us (3%)
    pallas_call x1, Pallas kernels, shards(): pl.pallas_call(kernel, out_shape=(jax.ShapeDtypeStruct((modes, slab), jnp...  24 us
    ppermute x10, starting transfers between devices, swap(): return lax.ppermute(value, AXES, [(i, i ^ mask) for i in range(devices)])  15.9 us
    ppermute x7, starting transfers between devices, shards(): pieces[m] = lax.ppermute(piece, 'cells', route) if m else piece  15.3 us
    ppermute x10, waiting for transfers between devices, swap(): return lax.ppermute(value, AXES, [(i, i ^ mask) for i in range(devices)])  15.3 us
    ppermute x7, waiting for transfers between devices, shards(): pieces[m] = lax.ppermute(piece, 'cells', route) if m else piece  9.02 us
    unnamed x7, local copies, waits for them, and re-layouts  2.14 us
  transfers between devices with their start and end apart: 17, of which 13 were waited for; matrix products, arithmetic and copies ran while one was open for 0% of the time, Pallas kernels for 0%

profile of v2, /device:TPU:0, one launch (start us, length us, event | category | flops | bytes accessed | tf_op | source)
XLA Modules:
  0.0 84.0 jit_solution(5075099482236408310)
XLA Ops:
  0.6 0.0 copy-start
  0.6 1.2 %copy-done = bf16[64,1,8192]{2,0,1:T(8,128)(2,1)S(1)} copy-done((bf16[64,1,8192]{2,0,1:T(8,128)(2,1)S(1)}, bf16[64,1,8192]{2,0,1:T(8,128)(2,1)}, u32[]{:S(2)}) %copy-start) | copy-done | bytes 1048600
  1.9 4.0 %collective-permute-start = (bf16[64,1024]{1,0:T(8,128)(2,1)S(1)}, bf16[64,1024]{1,0:T(8,128)(2,1)S(1)}, u32[]{:S(2)}, u32[]{:S(2)}) collective-permute-start(bf16[64,1024]{1,0:T(8,128)(2,1)S(1)} %get-tuple-element.15), channel_id=1, source_target_pairs={{0,12},{4,8},{8,4},{12,0},{16,28},{20,24},{24,20},{28,16},{1,13},{... | collective-permute-start | bytes 393224 | tf_op jit(solution)/shard_map/ppermute | solution.py:197
  5.9 2.6 %collective-permute-start.3 = (bf16[64,1024]{1,0:T(8,128)(2,1)S(1)}, bf16[64,1024]{1,0:T(8,128)(2,1)S(1)}, u32[]{:S(2)}, u32[]{:S(2)}) collective-permute-start(bf16[64,1024]{1,0:T(8,128)(2,1)S(1)} %get-tuple-element.18), channel_id=1, source_target_pairs={{0,16},{4,20},{8,24},{12,28},{16,0},{20,4},{24,8},{28,12},{1,17},{... | collective-permute-start | bytes 393224 | tf_op jit(solution)/shard_map/ppermute | solution.py:197
  8.5 0.3 collective-permute-start.4
  8.8 2.5 %collective-permute-done.refs_0_.refs_3_ = bf16[64,1024]{1,0:T(8,128)(2,1)S(1)} collective-permute-done((bf16[64,1024]{1,0:T(8,128)(2,1)S(1)}, bf16[64,1024]{1,0:T(8,128)(2,1)S(1)}, u32[]{:S(2)}, u32[]{:S(2)}) %collective-permute-start) | collective-permute-done | bytes 131104 | tf_op jit(solution)/shard_map/ppermute | solution.py:197
  11.3 1.9 %collective-permute-start.1 = (bf16[64,1024]{1,0:T(8,128)(2,1)S(1)}, bf16[64,1024]{1,0:T(8,128)(2,1)S(1)}, u32[]{:S(2)}, u32[]{:S(2)}) collective-permute-start(bf16[64,1024]{1,0:T(8,128)(2,1)S(1)} %get-tuple-element.16), channel_id=1, source_target_pairs={{0,4},{4,0},{8,12},{12,8},{16,20},{20,16},{24,28},{28,24},{1,5},{5... | collective-permute-start | bytes 393224 | tf_op jit(solution)/shard_map/ppermute | solution.py:197
  13.2 0.0 collective-permute-start.2
  13.2 3.1 %collective-permute-start.5 = (bf16[64,1024]{1,0:T(8,128)(2,1)S(1)}, bf16[64,1024]{1,0:T(8,128)(2,1)S(1)}, u32[]{:S(2)}, u32[]{:S(2)}) collective-permute-start(bf16[64,1024]{1,0:T(8,128)(2,1)S(1)} %get-tuple-element.20), channel_id=1, source_target_pairs={{0,24},{4,28},{8,16},{12,20},{16,8},{20,12},{24,0},{28,4},{1,25},{... | collective-permute-start | bytes 393224 | tf_op jit(solution)/shard_map/ppermute | solution.py:197
  16.3 2.1 %collective-permute-done.3.refs_4_ = bf16[64,1024]{1,0:T(8,128)(2,1)S(1)} collective-permute-done((bf16[64,1024]{1,0:T(8,128)(2,1)S(1)}, bf16[64,1024]{1,0:T(8,128)(2,1)S(1)}, u32[]{:S(2)}, u32[]{:S(2)}) %collective-permute-start.3) | collective-permute-done | bytes 131104 | tf_op jit(solution)/shard_map/ppermute | solution.py:197
  18.4 3.4 %collective-permute-start.6 = (bf16[64,1024]{1,0:T(8,128)(2,1)S(1)}, bf16[64,1024]{1,0:T(8,128)(2,1)S(1)}, u32[]{:S(2)}, u32[]{:S(2)}) collective-permute-start(bf16[64,1024]{1,0:T(8,128)(2,1)S(1)} %get-tuple-element.21), channel_id=1, source_target_pairs={{0,28},{4,24},{8,20},{12,16},{16,12},{20,8},{24,4},{28,0},{1,29},{... | collective-permute-start | bytes 393224 | tf_op jit(solution)/shard_map/ppermute | solution.py:197
  21.8 0.0 copy-start.1
  21.8 4.5 %collective-permute-done.4.refs_5_ = bf16[64,1024]{1,0:T(8,128)(2,1)S(1)} collective-permute-done((bf16[64,1024]{1,0:T(8,128)(2,1)S(1)}, bf16[64,1024]{1,0:T(8,128)(2,1)S(1)}, u32[]{:S(2)}, u32[]{:S(2)}) %collective-permute-start.4) | collective-permute-done | bytes 131104 | tf_op jit(solution)/shard_map/ppermute | solution.py:197
  26.3 0.0 collective-permute-done.1.refs_1_
  26.3 0.0 collective-permute-done.2.refs_2_
  26.3 0.0 collective-permute-done.5.refs_6_
  26.3 0.0 collective-permute-done.6.refs_7_
  26.3 0.0 copy-done.1
  26.3 1.1 %shard_map.52 = (bf16[512,1024]{1,0:T(8,128)(2,1)S(1)}, f32[1280,128]{1,0:T(8,128)S(1)}) custom-call(s32[1]{0:T(128)} %bitcast.2.place_ref, bf16[64,1024]{1,0:T(8,128)(2,1)S(1)} %get-tuple-element.14.refs_0_, bf16[64,1024]{1,0:T(8,128)(2,1)S(1)} %collective-permute-done.1.refs_1_, bf16[64,1024]{1,0:T(8,128)(2,1)S(1)} %collective-permute-done.2.refs_2_, ...), custom_call_target="tpu_custom_call" | custom-call | tf_op jit(solution)/shard_map/pallas_call | solution.py:203
  27.5 0.1 collective-permute-start.7
  27.6 1.6 %collective-permute-done.7 = f32[640,128]{1,0:T(8,128)S(1)} collective-permute-done((f32[640,128]{1,0:T(8,128)S(1)}, f32[640,128]{1,0:T(8,128)S(1)}, u32[]{:S(2)}, u32[]{:S(2)}) %collective-permute-start.7) | collective-permute-done | bytes 327712 | tf_op jit(solution)/shard_map/ppermute | solution.py:170
  29.3 1.6 %collective-permute-start.8 = (f32[160,128]{1,0:T(8,128)S(1)}, f32[160,128]{1,0:T(8,128)S(1)}, u32[]{:S(2)}, u32[]{:S(2)}) collective-permute-start(f32[160,128]{1,0:T(8,128)S(1)} %get-tuple-element.26), channel_id=1, source_target_pairs={{0,2},{1,3},{2,0},{3,1},{4,6},{5,7},{6,4},{7,5},{8,10},{9,11},{10,... | collective-permute-start | bytes 245768 | tf_op jit(solution)/shard_map/ppermute | solution.py:170
  30.9 2.0 %collective-permute-start.10 = (f32[160,128]{1,0:T(8,128)S(1)}, f32[160,128]{1,0:T(8,128)S(1)}, u32[]{:S(2)}, u32[]{:S(2)}) collective-permute-start(f32[160,128]{1,0:T(8,128)S(1)} %get-tuple-element.27), channel_id=1, source_target_pairs={{0,6},{1,7},{2,4},{3,5},{4,2},{5,3},{6,0},{7,1},{8,14},{9,15},{10,... | collective-permute-start | bytes 245768 | tf_op jit(solution)/shard_map/ppermute | solution.py:170
  32.9 0.1 collective-permute-start.9
  32.9 0.9 %collective-permute-done.8 = f32[160,128]{1,0:T(8,128)S(1)} collective-permute-done((f32[160,128]{1,0:T(8,128)S(1)}, f32[160,128]{1,0:T(8,128)S(1)}, u32[]{:S(2)}, u32[]{:S(2)}) %collective-permute-start.8) | collective-permute-done | bytes 81952 | tf_op jit(solution)/shard_map/ppermute | solution.py:170
  33.8 2.6 %collective-permute-done.10 = f32[160,128]{1,0:T(8,128)S(1)} collective-permute-done((f32[160,128]{1,0:T(8,128)S(1)}, f32[160,128]{1,0:T(8,128)S(1)}, u32[]{:S(2)}, u32[]{:S(2)}) %collective-permute-start.10) | collective-permute-done | bytes 81952 | tf_op jit(solution)/shard_map/ppermute | solution.py:170
  36.5 0.8 collective-permute-done.9
  37.3 5.5 %collective-permute-start.11 = (f32[160,128]{1,0:T(8,128)S(1)}, f32[160,128]{1,0:T(8,128)S(1)}, u32[]{:S(2)}, u32[]{:S(2)}) collective-permute-start(f32[160,128]{1,0:T(8,128)S(1)} %fusion.1), channel_id=1, source_target_pairs={{0,8},{1,9},{2,10},{3,11},{4,12},{5,13},{6,14},{7,15},{8,0},{9,1},... | collective-permute-start | bytes 245768 | tf_op jit(solution)/shard_map/ppermute | solution.py:170
  42.8 2.4 %collective-permute-done.11 = f32[160,128]{1,0:T(8,128)S(1)} collective-permute-done((f32[160,128]{1,0:T(8,128)S(1)}, f32[160,128]{1,0:T(8,128)S(1)}, u32[]{:S(2)}, u32[]{:S(2)}) %collective-permute-start.11) | collective-permute-done | bytes 81952 | tf_op jit(solution)/shard_map/ppermute | solution.py:170
  45.3 3.0 %collective-permute-start.12 = (f32[160,128]{1,0:T(8,128)S(1)}, f32[160,128]{1,0:T(8,128)S(1)}, u32[]{:S(2)}, u32[]{:S(2)}) collective-permute-start(f32[160,128]{1,0:T(8,128)S(1)} %add.63), channel_id=1, source_target_pairs={{0,16},{1,17},{2,18},{3,19},{4,20},{5,21},{6,22},{7,23},{8,24},{9,... | collective-permute-start | bytes 245768 | tf_op jit(solution)/shard_map/ppermute | solution.py:170
  48.3 2.4 %collective-permute-done.12 = f32[160,128]{1,0:T(8,128)S(1)} collective-permute-done((f32[160,128]{1,0:T(8,128)S(1)}, f32[160,128]{1,0:T(8,128)S(1)}, u32[]{:S(2)}, u32[]{:S(2)}) %collective-permute-start.12) | collective-permute-done | bytes 81952 | tf_op jit(solution)/shard_map/ppermute | solution.py:170
  50.7 2.3 %collective-permute-start.15 = (f32[160,128]{1,0:T(8,128)S(1)}, f32[160,128]{1,0:T(8,128)S(1)}, u32[]{:S(2)}, u32[]{:S(2)}) collective-permute-start(f32[160,128]{1,0:T(8,128)S(1)} %add.64), channel_id=1, source_target_pairs={{0,6},{1,7},{2,4},{3,5},{4,2},{5,3},{6,0},{7,1},{8,14},{9,15},{10,... | collective-permute-start | bytes 245768 | tf_op jit(solution)/shard_map/ppermute | solution.py:170
  53.0 0.8 collective-permute-start.14
  53.8 0.5 collective-permute-start.13
  54.3 1.9 %collective-permute-done.15 = f32[160,128]{1,0:T(8,128)S(1)} collective-permute-done((f32[160,128]{1,0:T(8,128)S(1)}, f32[160,128]{1,0:T(8,128)S(1)}, u32[]{:S(2)}, u32[]{:S(2)}) %collective-permute-start.15) | collective-permute-done | bytes 81952 | tf_op jit(solution)/shard_map/ppermute | solution.py:170
  56.1 1.3 %collective-permute-done.14 = f32[160,128]{1,0:T(8,128)S(1)} collective-permute-done((f32[160,128]{1,0:T(8,128)S(1)}, f32[160,128]{1,0:T(8,128)S(1)}, u32[]{:S(2)}, u32[]{:S(2)}) %collective-permute-start.14) | collective-permute-done | bytes 81952 | tf_op jit(solution)/shard_map/ppermute | solution.py:170
  57.5 0.8 collective-permute-done.13
  58.2 0.0 copy-start.2
  58.3 0.1 collective-permute-start.16
  58.3 0.8 copy-done.2
  59.1 0.1 copy.5.refs_3_
  59.3 0.1 pad_add_fusion.refs_0_
  59.3 0.6 collective-permute-done.16.refs_2_
  60.0 24.0 %shard_map.53 = (bf16[64,1024]{1,0:T(8,128)(2,1)}, f32[512,512]{1,0:T(8,128)}) custom-call(s32[2]{0:T(128)S(1)} %pad_add_fusion.refs_0_, f32[4,160,128]{2,1,0:T(8,128)S(1)} %pad_maximum_fusion.refs_1_, f32[4,160,128]{2,1,0:T(8,128)S(1)} %collective-permute-done.16.refs_2_, f32[512,64]{1,0:T(8,128)S(1)} %copy.5.refs_3_, ...), custom_call_target="tpu_custom_call" | custom-call | tf_op jit(solution)/shard_map/pallas_call | solution.py:237
  (9 shorter events, 0.2 us)
Async XLA Ops:
  0.6 1.2 %copy-start = (bf16[64,1,8192]{2,0,1:T(8,128)(2,1)S(1)}, bf16[64,1,8192]{2,0,1:T(8,128)(2,1)}, u32[]{:S(2)}) copy-start(bf16[64,1,8192]{2,0,1:T(8,128)(2,1)} %param.3) | copy-start | bytes 3145732
  1.9 9.4 %collective-permute-start = (bf16[64,1024]{1,0:T(8,128)(2,1)S(1)}, bf16[64,1024]{1,0:T(8,128)(2,1)S(1)}, u32[]{:S(2)}, u32[]{:S(2)}) collective-permute-start(bf16[64,1024]{1,0:T(8,128)(2,1)S(1)} %get-tuple-element.15), channel_id=1, source_target_pairs={{0,12},{4,8},{8,4},{12,0},{16,28},{20,24},{24,20},{28,16},{1,13},{... | collective-permute-start | bytes 393224 | tf_op jit(solution)/shard_map/ppermute | solution.py:197
  5.9 12.5 %collective-permute-start.3 = (bf16[64,1024]{1,0:T(8,128)(2,1)S(1)}, bf16[64,1024]{1,0:T(8,128)(2,1)S(1)}, u32[]{:S(2)}, u32[]{:S(2)}) collective-permute-start(bf16[64,1024]{1,0:T(8,128)(2,1)S(1)} %get-tuple-element.18), channel_id=1, source_target_pairs={{0,16},{4,20},{8,24},{12,28},{16,0},{20,4},{24,8},{28,12},{1,17},{... | collective-permute-start | bytes 393224 | tf_op jit(solution)/shard_map/ppermute | solution.py:197
  8.5 17.8 %collective-permute-start.4 = (bf16[64,1024]{1,0:T(8,128)(2,1)S(1)}, bf16[64,1024]{1,0:T(8,128)(2,1)S(1)}, u32[]{:S(2)}, u32[]{:S(2)}) collective-permute-start(bf16[64,1024]{1,0:T(8,128)(2,1)S(1)} %get-tuple-element.19), channel_id=1, source_target_pairs={{0,20},{4,16},{8,28},{12,24},{16,4},{20,0},{24,12},{28,8},{1,21},{... | collective-permute-start | bytes 393224 | tf_op jit(solution)/shard_map/ppermute | solution.py:197
  11.3 15.0 %collective-permute-start.1 = (bf16[64,1024]{1,0:T(8,128)(2,1)S(1)}, bf16[64,1024]{1,0:T(8,128)(2,1)S(1)}, u32[]{:S(2)}, u32[]{:S(2)}) collective-permute-start(bf16[64,1024]{1,0:T(8,128)(2,1)S(1)} %get-tuple-element.16), channel_id=1, source_target_pairs={{0,4},{4,0},{8,12},{12,8},{16,20},{20,16},{24,28},{28,24},{1,5},{5... | collective-permute-start | bytes 393224 | tf_op jit(solution)/shard_map/ppermute | solution.py:197
  13.2 13.1 %collective-permute-start.2 = (bf16[64,1024]{1,0:T(8,128)(2,1)S(1)}, bf16[64,1024]{1,0:T(8,128)(2,1)S(1)}, u32[]{:S(2)}, u32[]{:S(2)}) collective-permute-start(bf16[64,1024]{1,0:T(8,128)(2,1)S(1)} %get-tuple-element.17), channel_id=1, source_target_pairs={{0,8},{4,12},{8,0},{12,4},{16,24},{20,28},{24,16},{28,20},{1,9},{5... | collective-permute-start | bytes 393224 | tf_op jit(solution)/shard_map/ppermute | solution.py:197
  13.2 13.1 %collective-permute-start.5 = (bf16[64,1024]{1,0:T(8,128)(2,1)S(1)}, bf16[64,1024]{1,0:T(8,128)(2,1)S(1)}, u32[]{:S(2)}, u32[]{:S(2)}) collective-permute-start(bf16[64,1024]{1,0:T(8,128)(2,1)S(1)} %get-tuple-element.20), channel_id=1, source_target_pairs={{0,24},{4,28},{8,16},{12,20},{16,8},{20,12},{24,0},{28,4},{1,25},{... | collective-permute-start | bytes 393224 | tf_op jit(solution)/shard_map/ppermute | solution.py:197
  18.4 7.9 %collective-permute-start.6 = (bf16[64,1024]{1,0:T(8,128)(2,1)S(1)}, bf16[64,1024]{1,0:T(8,128)(2,1)S(1)}, u32[]{:S(2)}, u32[]{:S(2)}) collective-permute-start(bf16[64,1024]{1,0:T(8,128)(2,1)S(1)} %get-tuple-element.21), channel_id=1, source_target_pairs={{0,28},{4,24},{8,20},{12,16},{16,12},{20,8},{24,4},{28,0},{1,29},{... | collective-permute-start | bytes 393224 | tf_op jit(solution)/shard_map/ppermute | solution.py:197
  21.8 4.5 %copy-start.1 = (bf16[1,1024]{1,0:T(2,128)(2,1)S(1)}, bf16[1,1024]{1,0:T(2,128)(2,1)}, u32[]{:S(2)}) copy-start(bf16[1,1024]{1,0:T(2,128)(2,1)} %refs_8_.1) | copy-start | bytes 6148
  27.5 1.7 %collective-permute-start.7 = (f32[640,128]{1,0:T(8,128)S(1)}, f32[640,128]{1,0:T(8,128)S(1)}, u32[]{:S(2)}, u32[]{:S(2)}) collective-permute-start(f32[640,128]{1,0:T(8,128)S(1)} %dynamic-slice_bitcast_fusion), channel_id=1, source_target_pairs={{0,1},{1,0},{2,3},{3,2},{4,5},{5,4},{6,7},{7,6},{8,9},{9,8},{10,11... | collective-permute-start | bytes 983048 | tf_op jit(solution)/shard_map/ppermute | solution.py:170
  29.3 4.6 %collective-permute-start.8 = (f32[160,128]{1,0:T(8,128)S(1)}, f32[160,128]{1,0:T(8,128)S(1)}, u32[]{:S(2)}, u32[]{:S(2)}) collective-permute-start(f32[160,128]{1,0:T(8,128)S(1)} %get-tuple-element.26), channel_id=1, source_target_pairs={{0,2},{1,3},{2,0},{3,1},{4,6},{5,7},{6,4},{7,5},{8,10},{9,11},{10,... | collective-permute-start | bytes 245768 | tf_op jit(solution)/shard_map/ppermute | solution.py:170
  30.9 5.6 %collective-permute-start.10 = (f32[160,128]{1,0:T(8,128)S(1)}, f32[160,128]{1,0:T(8,128)S(1)}, u32[]{:S(2)}, u32[]{:S(2)}) collective-permute-start(f32[160,128]{1,0:T(8,128)S(1)} %get-tuple-element.27), channel_id=1, source_target_pairs={{0,6},{1,7},{2,4},{3,5},{4,2},{5,3},{6,0},{7,1},{8,14},{9,15},{10,... | collective-permute-start | bytes 245768 | tf_op jit(solution)/shard_map/ppermute | solution.py:170
  32.9 4.4 %collective-permute-start.9 = (f32[160,128]{1,0:T(8,128)S(1)}, f32[160,128]{1,0:T(8,128)S(1)}, u32[]{:S(2)}, u32[]{:S(2)}) collective-permute-start(f32[160,128]{1,0:T(8,128)S(1)} %get-tuple-element.28), channel_id=1, source_target_pairs={{0,4},{1,5},{2,6},{3,7},{4,0},{5,1},{6,2},{7,3},{8,12},{9,13},{10,... | collective-permute-start | bytes 245768 | tf_op jit(solution)/shard_map/ppermute | solution.py:170
  37.3 7.9 %collective-permute-start.11 = (f32[160,128]{1,0:T(8,128)S(1)}, f32[160,128]{1,0:T(8,128)S(1)}, u32[]{:S(2)}, u32[]{:S(2)}) collective-permute-start(f32[160,128]{1,0:T(8,128)S(1)} %fusion.1), channel_id=1, source_target_pairs={{0,8},{1,9},{2,10},{3,11},{4,12},{5,13},{6,14},{7,15},{8,0},{9,1},... | collective-permute-start | bytes 245768 | tf_op jit(solution)/shard_map/ppermute | solution.py:170
  45.3 5.5 %collective-permute-start.12 = (f32[160,128]{1,0:T(8,128)S(1)}, f32[160,128]{1,0:T(8,128)S(1)}, u32[]{:S(2)}, u32[]{:S(2)}) collective-permute-start(f32[160,128]{1,0:T(8,128)S(1)} %add.63), channel_id=1, source_target_pairs={{0,16},{1,17},{2,18},{3,19},{4,20},{5,21},{6,22},{7,23},{8,24},{9,... | collective-permute-start | bytes 245768 | tf_op jit(solution)/shard_map/ppermute | solution.py:170
  50.7 5.4 %collective-permute-start.15 = (f32[160,128]{1,0:T(8,128)S(1)}, f32[160,128]{1,0:T(8,128)S(1)}, u32[]{:S(2)}, u32[]{:S(2)}) collective-permute-start(f32[160,128]{1,0:T(8,128)S(1)} %add.64), channel_id=1, source_target_pairs={{0,6},{1,7},{2,4},{3,5},{4,2},{5,3},{6,0},{7,1},{8,14},{9,15},{10,... | collective-permute-start | bytes 245768 | tf_op jit(solution)/shard_map/ppermute | solution.py:170
  53.0 4.4 %collective-permute-start.14 = (f32[160,128]{1,0:T(8,128)S(1)}, f32[160,128]{1,0:T(8,128)S(1)}, u32[]{:S(2)}, u32[]{:S(2)}) collective-permute-start(f32[160,128]{1,0:T(8,128)S(1)} %add.64), channel_id=1, source_target_pairs={{0,4},{1,5},{2,6},{3,7},{4,0},{5,1},{6,2},{7,3},{8,12},{9,13},{10,... | collective-permute-start | bytes 245768 | tf_op jit(solution)/shard_map/ppermute | solution.py:170
  53.8 4.4 %collective-permute-start.13 = (f32[160,128]{1,0:T(8,128)S(1)}, f32[160,128]{1,0:T(8,128)S(1)}, u32[]{:S(2)}, u32[]{:S(2)}) collective-permute-start(f32[160,128]{1,0:T(8,128)S(1)} %add.64), channel_id=1, source_target_pairs={{0,2},{1,3},{2,0},{3,1},{4,6},{5,7},{6,4},{7,5},{8,10},{9,11},{10,... | collective-permute-start | bytes 245768 | tf_op jit(solution)/shard_map/ppermute | solution.py:170
  58.2 0.9 %copy-start.2 = (f32[512,64]{0,1:T(8,128)S(1)}, f32[512,64]{0,1:T(8,128)}, u32[]{:S(2)}) copy-start(f32[512,64]{0,1:T(8,128)} %param.5) | copy-start | bytes 393220
  58.3 1.7 %collective-permute-start.16 = (f32[4,160,128]{2,1,0:T(8,128)S(1)}, f32[4,160,128]{2,1,0:T(8,128)S(1)}, u32[]{:S(2)}, u32[]{:S(2)}) collective-permute-start(f32[4,160,128]{2,1,0:T(8,128)S(1)} %pad_maximum_fusion.refs_1_), channel_id=1, source_target_pairs={{0,1},{1,0},{2,3},{3,2},{4,5},{5,4},{6,7},{7,6},{8,9},{9,8},{10,11... | collective-permute-start | bytes 983048 | tf_op jit(solution)/shard_map/ppermute | solution.py:170

commit v3 on v2

--- a/solution.py
+++ b/solution.py
@@ -35,29 +35,39 @@
     both = jnp.concatenate([square, eye], axis=1)
     count = HALF // 8
     strips = [both[8 * j : 8 * j + 8, :] for j in range(count)]
+
+    def spread_row(value, at):
+        return jnp.broadcast_to(value[at : at + 1, :], tile)
+
+    def spread_column(value, at):
+        return jnp.broadcast_to(value[:, at : at + 1], tile)
+
+    ahead = [spread_column(strips[0], t) for t in range(8)]
     for m in range(count):
-        spread = {}
-        for j in range(m, count):
+        columns = {(m, t): ahead[t] for t in range(8)}
+        for j in range(m + 1, count):
             for t in range(8):
-                at = 8 * m + t
-                spread[j, t] = jnp.broadcast_to(strips[j][:, at : at + 1], tile)
+                columns[j, t] = spread_column(strips[j], 8 * m + t)
+        if m + 1 < count:
+            ahead = [spread_column(strips[m + 1], 8 * m + 8 + t) for t in range(8)]
+        corner = {(t, u): spread_row(columns[m, u], t) for t in range(8) for u in range(t, 8)}
         for t in range(8):
-            root = lax.rsqrt(jnp.broadcast_to(spread[m, t][t : t + 1, :], tile))
-            inverse = root * root
-            row = jnp.broadcast_to(strips[m][t : t + 1, :], tile)
-            scaled = row * inverse
-            later = {
-                u: jnp.broadcast_to(spread[m, u][t : t + 1, :], tile) * inverse
-                for u in range(t + 1, 8)
-            }
+            root = lax.rsqrt(corner[t, t])
+            line = {u: corner[t, u] * root for u in range(t + 1, 8)}
+            for u in range(t + 1, 8):
+                for v in range(u, 8):
+                    corner[u, v] = corner[u, v] - line[u] * line[v]
+            row = spread_row(strips[m], t) * root
             for j in range(m, count):
-                column = spread[j, t]
+                column = columns[j, t] * root
                 if j == m:
                     column = jnp.where(sub > t, column, 0.0)
                 for u in range(t + 1, 8):
-                    spread[j, u] = spread[j, u] - column * later[u]
-                updated = strips[j] - column * scaled
-                strips[j] = jnp.where(sub == t, row * root, updated) if j == m else updated
+                    columns[j, u] = columns[j, u] - column * line[u]
+                updated = strips[j] - column * row
+                strips[j] = jnp.where(sub == t, row, updated) if j == m else updated
+                if j == m + 1:
+                    ahead = [ahead[u] - column * spread_row(column, u) for u in range(8)]
     return jnp.concatenate(strips, axis=0)
 
 

time: 84.1 us -> 76.6 us (0.911)
  Pallas kernels: 25.2 us -> 17.6 us
    pallas_call x1, Pallas kernels: 24 us -> 16.4 us  [shards(): pl.pallas_call(kernel, out_shape=(jax.ShapeDtypeStruct((modes, slab), jnp...]
where the time goes in v3:
time: 76.6 us; the launch traced here: 76.4 us
  starting transfers between devices  31.2 us (41%)
  waiting for transfers between devices  24.3 us (32%)
  Pallas kernels  17.6 us (23%)
  local copies, waits for them, and re-layouts  2.2 us (3%)
  between operations  0.81 us (1%)
    pallas_call x1, Pallas kernels, shards(): pl.pallas_call(kernel, out_shape=(jax.ShapeDtypeStruct((modes, slab), jnp...  16.4 us
    ppermute x10, starting transfers between devices, swap(): return lax.ppermute(value, AXES, [(i, i ^ mask) for i in range(devices)])  15.9 us
    ppermute x7, starting transfers between devices, shards(): pieces[m] = lax.ppermute(piece, 'cells', route) if m else piece  15.3 us
    ppermute x10, waiting for transfers between devices, swap(): return lax.ppermute(value, AXES, [(i, i ^ mask) for i in range(devices)])  15.3 us
    ppermute x7, waiting for transfers between devices, shards(): pieces[m] = lax.ppermute(piece, 'cells', route) if m else piece  9.02 us
    unnamed x7, local copies, waits for them, and re-layouts  2.14 us
  transfers between devices with their start and end apart: 17, of which 13 were waited for; matrix products, arithmetic and copies ran while one was open for 0% of the time, Pallas kernels for 0%

profile of v3, /device:TPU:0, one launch (start us, length us, event | category | flops | bytes accessed | tf_op | source)
XLA Modules:
  0.0 76.4 jit_solution(15775523775131850181)
XLA Ops:
  0.6 0.0 copy-start
  0.6 1.2 %copy-done = bf16[64,1,8192]{2,0,1:T(8,128)(2,1)S(1)} copy-done((bf16[64,1,8192]{2,0,1:T(8,128)(2,1)S(1)}, bf16[64,1,8192]{2,0,1:T(8,128)(2,1)}, u32[]{:S(2)}) %copy-start) | copy-done | bytes 1048600
  1.9 4.0 %collective-permute-start = (bf16[64,1024]{1,0:T(8,128)(2,1)S(1)}, bf16[64,1024]{1,0:T(8,128)(2,1)S(1)}, u32[]{:S(2)}, u32[]{:S(2)}) collective-permute-start(bf16[64,1024]{1,0:T(8,128)(2,1)S(1)} %get-tuple-element.15), channel_id=1, source_target_pairs={{0,12},{4,8},{8,4},{12,0},{16,28},{20,24},{24,20},{28,16},{1,13},{... | collective-permute-start | bytes 393224 | tf_op jit(solution)/shard_map/ppermute | solution.py:207
  5.9 2.6 %collective-permute-start.3 = (bf16[64,1024]{1,0:T(8,128)(2,1)S(1)}, bf16[64,1024]{1,0:T(8,128)(2,1)S(1)}, u32[]{:S(2)}, u32[]{:S(2)}) collective-permute-start(bf16[64,1024]{1,0:T(8,128)(2,1)S(1)} %get-tuple-element.18), channel_id=1, source_target_pairs={{0,16},{4,20},{8,24},{12,28},{16,0},{20,4},{24,8},{28,12},{1,17},{... | collective-permute-start | bytes 393224 | tf_op jit(solution)/shard_map/ppermute | solution.py:207
  8.5 0.3 collective-permute-start.4
  8.8 2.5 %collective-permute-done.refs_0_.refs_3_ = bf16[64,1024]{1,0:T(8,128)(2,1)S(1)} collective-permute-done((bf16[64,1024]{1,0:T(8,128)(2,1)S(1)}, bf16[64,1024]{1,0:T(8,128)(2,1)S(1)}, u32[]{:S(2)}, u32[]{:S(2)}) %collective-permute-start) | collective-permute-done | bytes 131104 | tf_op jit(solution)/shard_map/ppermute | solution.py:207
  11.3 1.9 %collective-permute-start.1 = (bf16[64,1024]{1,0:T(8,128)(2,1)S(1)}, bf16[64,1024]{1,0:T(8,128)(2,1)S(1)}, u32[]{:S(2)}, u32[]{:S(2)}) collective-permute-start(bf16[64,1024]{1,0:T(8,128)(2,1)S(1)} %get-tuple-element.16), channel_id=1, source_target_pairs={{0,4},{4,0},{8,12},{12,8},{16,20},{20,16},{24,28},{28,24},{1,5},{5... | collective-permute-start | bytes 393224 | tf_op jit(solution)/shard_map/ppermute | solution.py:207
  13.2 0.0 collective-permute-start.2
  13.2 3.1 %collective-permute-start.5 = (bf16[64,1024]{1,0:T(8,128)(2,1)S(1)}, bf16[64,1024]{1,0:T(8,128)(2,1)S(1)}, u32[]{:S(2)}, u32[]{:S(2)}) collective-permute-start(bf16[64,1024]{1,0:T(8,128)(2,1)S(1)} %get-tuple-element.20), channel_id=1, source_target_pairs={{0,24},{4,28},{8,16},{12,20},{16,8},{20,12},{24,0},{28,4},{1,25},{... | collective-permute-start | bytes 393224 | tf_op jit(solution)/shard_map/ppermute | solution.py:207
  16.3 2.1 %collective-permute-done.3.refs_4_ = bf16[64,1024]{1,0:T(8,128)(2,1)S(1)} collective-permute-done((bf16[64,1024]{1,0:T(8,128)(2,1)S(1)}, bf16[64,1024]{1,0:T(8,128)(2,1)S(1)}, u32[]{:S(2)}, u32[]{:S(2)}) %collective-permute-start.3) | collective-permute-done | bytes 131104 | tf_op jit(solution)/shard_map/ppermute | solution.py:207
  18.4 3.4 %collective-permute-start.6 = (bf16[64,1024]{1,0:T(8,128)(2,1)S(1)}, bf16[64,1024]{1,0:T(8,128)(2,1)S(1)}, u32[]{:S(2)}, u32[]{:S(2)}) collective-permute-start(bf16[64,1024]{1,0:T(8,128)(2,1)S(1)} %get-tuple-element.21), channel_id=1, source_target_pairs={{0,28},{4,24},{8,20},{12,16},{16,12},{20,8},{24,4},{28,0},{1,29},{... | collective-permute-start | bytes 393224 | tf_op jit(solution)/shard_map/ppermute | solution.py:207
  21.8 0.0 copy-start.1
  21.8 4.5 %collective-permute-done.4.refs_5_ = bf16[64,1024]{1,0:T(8,128)(2,1)S(1)} collective-permute-done((bf16[64,1024]{1,0:T(8,128)(2,1)S(1)}, bf16[64,1024]{1,0:T(8,128)(2,1)S(1)}, u32[]{:S(2)}, u32[]{:S(2)}) %collective-permute-start.4) | collective-permute-done | bytes 131104 | tf_op jit(solution)/shard_map/ppermute | solution.py:207
  26.3 0.0 collective-permute-done.1.refs_1_
  26.3 0.0 collective-permute-done.2.refs_2_
  26.3 0.0 collective-permute-done.5.refs_6_
  26.3 0.0 collective-permute-done.6.refs_7_
  26.3 0.0 copy-done.1
  26.3 1.1 %shard_map.52 = (bf16[512,1024]{1,0:T(8,128)(2,1)S(1)}, f32[1280,128]{1,0:T(8,128)S(1)}) custom-call(s32[1]{0:T(128)} %bitcast.2.place_ref, bf16[64,1024]{1,0:T(8,128)(2,1)S(1)} %get-tuple-element.14.refs_0_, bf16[64,1024]{1,0:T(8,128)(2,1)S(1)} %collective-permute-done.1.refs_1_, bf16[64,1024]{1,0:T(8,128)(2,1)S(1)} %collective-permute-done.2.refs_2_, ...), custom_call_target="tpu_custom_call" | custom-call | tf_op jit(solution)/shard_map/pallas_call | solution.py:213
  27.5 0.1 collective-permute-start.7
  27.6 1.6 %collective-permute-done.7 = f32[640,128]{1,0:T(8,128)S(1)} collective-permute-done((f32[640,128]{1,0:T(8,128)S(1)}, f32[640,128]{1,0:T(8,128)S(1)}, u32[]{:S(2)}, u32[]{:S(2)}) %collective-permute-start.7) | collective-permute-done | bytes 327712 | tf_op jit(solution)/shard_map/ppermute | solution.py:180
  29.3 1.6 %collective-permute-start.8 = (f32[160,128]{1,0:T(8,128)S(1)}, f32[160,128]{1,0:T(8,128)S(1)}, u32[]{:S(2)}, u32[]{:S(2)}) collective-permute-start(f32[160,128]{1,0:T(8,128)S(1)} %get-tuple-element.26), channel_id=1, source_target_pairs={{0,2},{1,3},{2,0},{3,1},{4,6},{5,7},{6,4},{7,5},{8,10},{9,11},{10,... | collective-permute-start | bytes 245768 | tf_op jit(solution)/shard_map/ppermute | solution.py:180
  30.9 2.0 %collective-permute-start.10 = (f32[160,128]{1,0:T(8,128)S(1)}, f32[160,128]{1,0:T(8,128)S(1)}, u32[]{:S(2)}, u32[]{:S(2)}) collective-permute-start(f32[160,128]{1,0:T(8,128)S(1)} %get-tuple-element.27), channel_id=1, source_target_pairs={{0,6},{1,7},{2,4},{3,5},{4,2},{5,3},{6,0},{7,1},{8,14},{9,15},{10,... | collective-permute-start | bytes 245768 | tf_op jit(solution)/shard_map/ppermute | solution.py:180
  32.9 0.1 collective-permute-start.9
  32.9 0.9 %collective-permute-done.8 = f32[160,128]{1,0:T(8,128)S(1)} collective-permute-done((f32[160,128]{1,0:T(8,128)S(1)}, f32[160,128]{1,0:T(8,128)S(1)}, u32[]{:S(2)}, u32[]{:S(2)}) %collective-permute-start.8) | collective-permute-done | bytes 81952 | tf_op jit(solution)/shard_map/ppermute | solution.py:180
  33.8 2.6 %collective-permute-done.10 = f32[160,128]{1,0:T(8,128)S(1)} collective-permute-done((f32[160,128]{1,0:T(8,128)S(1)}, f32[160,128]{1,0:T(8,128)S(1)}, u32[]{:S(2)}, u32[]{:S(2)}) %collective-permute-start.10) | collective-permute-done | bytes 81952 | tf_op jit(solution)/shard_map/ppermute | solution.py:180
  36.5 0.8 %collective-permute-done.9 = f32[160,128]{1,0:T(8,128)S(1)} collective-permute-done((f32[160,128]{1,0:T(8,128)S(1)}, f32[160,128]{1,0:T(8,128)S(1)}, u32[]{:S(2)}, u32[]{:S(2)}) %collective-permute-start.9) | collective-permute-done | bytes 81952 | tf_op jit(solution)/shard_map/ppermute | solution.py:180
  37.3 5.5 %collective-permute-start.11 = (f32[160,128]{1,0:T(8,128)S(1)}, f32[160,128]{1,0:T(8,128)S(1)}, u32[]{:S(2)}, u32[]{:S(2)}) collective-permute-start(f32[160,128]{1,0:T(8,128)S(1)} %fusion.1), channel_id=1, source_target_pairs={{0,8},{1,9},{2,10},{3,11},{4,12},{5,13},{6,14},{7,15},{8,0},{9,1},... | collective-permute-start | bytes 245768 | tf_op jit(solution)/shard_map/ppermute | solution.py:180
  42.8 2.4 %collective-permute-done.11 = f32[160,128]{1,0:T(8,128)S(1)} collective-permute-done((f32[160,128]{1,0:T(8,128)S(1)}, f32[160,128]{1,0:T(8,128)S(1)}, u32[]{:S(2)}, u32[]{:S(2)}) %collective-permute-start.11) | collective-permute-done | bytes 81952 | tf_op jit(solution)/shard_map/ppermute | solution.py:180
  45.3 3.1 %collective-permute-start.12 = (f32[160,128]{1,0:T(8,128)S(1)}, f32[160,128]{1,0:T(8,128)S(1)}, u32[]{:S(2)}, u32[]{:S(2)}) collective-permute-start(f32[160,128]{1,0:T(8,128)S(1)} %add.63), channel_id=1, source_target_pairs={{0,16},{1,17},{2,18},{3,19},{4,20},{5,21},{6,22},{7,23},{8,24},{9,... | collective-permute-start | bytes 245768 | tf_op jit(solution)/shard_map/ppermute | solution.py:180
  48.3 2.4 %collective-permute-done.12 = f32[160,128]{1,0:T(8,128)S(1)} collective-permute-done((f32[160,128]{1,0:T(8,128)S(1)}, f32[160,128]{1,0:T(8,128)S(1)}, u32[]{:S(2)}, u32[]{:S(2)}) %collective-permute-start.12) | collective-permute-done | bytes 81952 | tf_op jit(solution)/shard_map/ppermute | solution.py:180
  50.7 2.3 %collective-permute-start.15 = (f32[160,128]{1,0:T(8,128)S(1)}, f32[160,128]{1,0:T(8,128)S(1)}, u32[]{:S(2)}, u32[]{:S(2)}) collective-permute-start(f32[160,128]{1,0:T(8,128)S(1)} %add.64), channel_id=1, source_target_pairs={{0,6},{1,7},{2,4},{3,5},{4,2},{5,3},{6,0},{7,1},{8,14},{9,15},{10,... | collective-permute-start | bytes 245768 | tf_op jit(solution)/shard_map/ppermute | solution.py:180
  53.0 0.8 %collective-permute-start.14 = (f32[160,128]{1,0:T(8,128)S(1)}, f32[160,128]{1,0:T(8,128)S(1)}, u32[]{:S(2)}, u32[]{:S(2)}) collective-permute-start(f32[160,128]{1,0:T(8,128)S(1)} %add.64), channel_id=1, source_target_pairs={{0,4},{1,5},{2,6},{3,7},{4,0},{5,1},{6,2},{7,3},{8,12},{9,13},{10,... | collective-permute-start | bytes 245768 | tf_op jit(solution)/shard_map/ppermute | solution.py:180
  53.8 0.5 collective-permute-start.13
  54.3 1.9 %collective-permute-done.15 = f32[160,128]{1,0:T(8,128)S(1)} collective-permute-done((f32[160,128]{1,0:T(8,128)S(1)}, f32[160,128]{1,0:T(8,128)S(1)}, u32[]{:S(2)}, u32[]{:S(2)}) %collective-permute-start.15) | collective-permute-done | bytes 81952 | tf_op jit(solution)/shard_map/ppermute | solution.py:180
  56.2 1.3 %collective-permute-done.14 = f32[160,128]{1,0:T(8,128)S(1)} collective-permute-done((f32[160,128]{1,0:T(8,128)S(1)}, f32[160,128]{1,0:T(8,128)S(1)}, u32[]{:S(2)}, u32[]{:S(2)}) %collective-permute-start.14) | collective-permute-done | bytes 81952 | tf_op jit(solution)/shard_map/ppermute | solution.py:180
  57.5 0.8 %collective-permute-done.13 = f32[160,128]{1,0:T(8,128)S(1)} collective-permute-done((f32[160,128]{1,0:T(8,128)S(1)}, f32[160,128]{1,0:T(8,128)S(1)}, u32[]{:S(2)}, u32[]{:S(2)}) %collective-permute-start.13) | collective-permute-done | bytes 81952 | tf_op jit(solution)/shard_map/ppermute | solution.py:180
  58.2 0.0 copy-start.2
  58.3 0.1 collective-permute-start.16
  58.3 0.8 %copy-done.2 = f32[512,64]{0,1:T(8,128)S(1)} copy-done((f32[512,64]{0,1:T(8,128)S(1)}, f32[512,64]{0,1:T(8,128)}, u32[]{:S(2)}) %copy-start.2) | copy-done | bytes 131096
  59.1 0.1 copy.5.refs_3_
  59.3 0.1 pad_add_fusion.refs_0_
  59.3 0.6 collective-permute-done.16.refs_2_
  60.0 16.4 %shard_map.53 = (bf16[64,1024]{1,0:T(8,128)(2,1)}, f32[512,512]{1,0:T(8,128)}) custom-call(s32[2]{0:T(128)S(1)} %pad_add_fusion.refs_0_, f32[4,160,128]{2,1,0:T(8,128)S(1)} %pad_maximum_fusion.refs_1_, f32[4,160,128]{2,1,0:T(8,128)S(1)} %collective-permute-done.16.refs_2_, f32[512,64]{1,0:T(8,128)S(1)} %copy.5.refs_3_, ...), custom_call_target="tpu_custom_call" | custom-call | tf_op jit(solution)/shard_map/pallas_call | solution.py:247
  (9 shorter events, 0.2 us)
Async XLA Ops:
  0.6 1.2 %copy-start = (bf16[64,1,8192]{2,0,1:T(8,128)(2,1)S(1)}, bf16[64,1,8192]{2,0,1:T(8,128)(2,1)}, u32[]{:S(2)}) copy-start(bf16[64,1,8192]{2,0,1:T(8,128)(2,1)} %param.3) | copy-start | bytes 3145732
  1.9 9.4 %collective-permute-start = (bf16[64,1024]{1,0:T(8,128)(2,1)S(1)}, bf16[64,1024]{1,0:T(8,128)(2,1)S(1)}, u32[]{:S(2)}, u32[]{:S(2)}) collective-permute-start(bf16[64,1024]{1,0:T(8,128)(2,1)S(1)} %get-tuple-element.15), channel_id=1, source_target_pairs={{0,12},{4,8},{8,4},{12,0},{16,28},{20,24},{24,20},{28,16},{1,13},{... | collective-permute-start | bytes 393224 | tf_op jit(solution)/shard_map/ppermute | solution.py:207
  5.9 12.5 %collective-permute-start.3 = (bf16[64,1024]{1,0:T(8,128)(2,1)S(1)}, bf16[64,1024]{1,0:T(8,128)(2,1)S(1)}, u32[]{:S(2)}, u32[]{:S(2)}) collective-permute-start(bf16[64,1024]{1,0:T(8,128)(2,1)S(1)} %get-tuple-element.18), channel_id=1, source_target_pairs={{0,16},{4,20},{8,24},{12,28},{16,0},{20,4},{24,8},{28,12},{1,17},{... | collective-permute-start | bytes 393224 | tf_op jit(solution)/shard_map/ppermute | solution.py:207
  8.5 17.8 %collective-permute-start.4 = (bf16[64,1024]{1,0:T(8,128)(2,1)S(1)}, bf16[64,1024]{1,0:T(8,128)(2,1)S(1)}, u32[]{:S(2)}, u32[]{:S(2)}) collective-permute-start(bf16[64,1024]{1,0:T(8,128)(2,1)S(1)} %get-tuple-element.19), channel_id=1, source_target_pairs={{0,20},{4,16},{8,28},{12,24},{16,4},{20,0},{24,12},{28,8},{1,21},{... | collective-permute-start | bytes 393224 | tf_op jit(solution)/shard_map/ppermute | solution.py:207
  11.3 15.0 %collective-permute-start.1 = (bf16[64,1024]{1,0:T(8,128)(2,1)S(1)}, bf16[64,1024]{1,0:T(8,128)(2,1)S(1)}, u32[]{:S(2)}, u32[]{:S(2)}) collective-permute-start(bf16[64,1024]{1,0:T(8,128)(2,1)S(1)} %get-tuple-element.16), channel_id=1, source_target_pairs={{0,4},{4,0},{8,12},{12,8},{16,20},{20,16},{24,28},{28,24},{1,5},{5... | collective-permute-start | bytes 393224 | tf_op jit(solution)/shard_map/ppermute | solution.py:207
  13.2 13.1 %collective-permute-start.2 = (bf16[64,1024]{1,0:T(8,128)(2,1)S(1)}, bf16[64,1024]{1,0:T(8,128)(2,1)S(1)}, u32[]{:S(2)}, u32[]{:S(2)}) collective-permute-start(bf16[64,1024]{1,0:T(8,128)(2,1)S(1)} %get-tuple-element.17), channel_id=1, source_target_pairs={{0,8},{4,12},{8,0},{12,4},{16,24},{20,28},{24,16},{28,20},{1,9},{5... | collective-permute-start | bytes 393224 | tf_op jit(solution)/shard_map/ppermute | solution.py:207
  13.2 13.1 %collective-permute-start.5 = (bf16[64,1024]{1,0:T(8,128)(2,1)S(1)}, bf16[64,1024]{1,0:T(8,128)(2,1)S(1)}, u32[]{:S(2)}, u32[]{:S(2)}) collective-permute-start(bf16[64,1024]{1,0:T(8,128)(2,1)S(1)} %get-tuple-element.20), channel_id=1, source_target_pairs={{0,24},{4,28},{8,16},{12,20},{16,8},{20,12},{24,0},{28,4},{1,25},{... | collective-permute-start | bytes 393224 | tf_op jit(solution)/shard_map/ppermute | solution.py:207
  18.4 7.9 %collective-permute-start.6 = (bf16[64,1024]{1,0:T(8,128)(2,1)S(1)}, bf16[64,1024]{1,0:T(8,128)(2,1)S(1)}, u32[]{:S(2)}, u32[]{:S(2)}) collective-permute-start(bf16[64,1024]{1,0:T(8,128)(2,1)S(1)} %get-tuple-element.21), channel_id=1, source_target_pairs={{0,28},{4,24},{8,20},{12,16},{16,12},{20,8},{24,4},{28,0},{1,29},{... | collective-permute-start | bytes 393224 | tf_op jit(solution)/shard_map/ppermute | solution.py:207
  21.8 4.5 %copy-start.1 = (bf16[1,1024]{1,0:T(2,128)(2,1)S(1)}, bf16[1,1024]{1,0:T(2,128)(2,1)}, u32[]{:S(2)}) copy-start(bf16[1,1024]{1,0:T(2,128)(2,1)} %refs_8_.1) | copy-start | bytes 6148
  27.5 1.7 %collective-permute-start.7 = (f32[640,128]{1,0:T(8,128)S(1)}, f32[640,128]{1,0:T(8,128)S(1)}, u32[]{:S(2)}, u32[]{:S(2)}) collective-permute-start(f32[640,128]{1,0:T(8,128)S(1)} %dynamic-slice_bitcast_fusion), channel_id=1, source_target_pairs={{0,1},{1,0},{2,3},{3,2},{4,5},{5,4},{6,7},{7,6},{8,9},{9,8},{10,11... | collective-permute-start | bytes 983048 | tf_op jit(solution)/shard_map/ppermute | solution.py:180
  29.3 4.6 %collective-permute-start.8 = (f32[160,128]{1,0:T(8,128)S(1)}, f32[160,128]{1,0:T(8,128)S(1)}, u32[]{:S(2)}, u32[]{:S(2)}) collective-permute-start(f32[160,128]{1,0:T(8,128)S(1)} %get-tuple-element.26), channel_id=1, source_target_pairs={{0,2},{1,3},{2,0},{3,1},{4,6},{5,7},{6,4},{7,5},{8,10},{9,11},{10,... | collective-permute-start | bytes 245768 | tf_op jit(solution)/shard_map/ppermute | solution.py:180
  30.9 5.6 %collective-permute-start.10 = (f32[160,128]{1,0:T(8,128)S(1)}, f32[160,128]{1,0:T(8,128)S(1)}, u32[]{:S(2)}, u32[]{:S(2)}) collective-permute-start(f32[160,128]{1,0:T(8,128)S(1)} %get-tuple-element.27), channel_id=1, source_target_pairs={{0,6},{1,7},{2,4},{3,5},{4,2},{5,3},{6,0},{7,1},{8,14},{9,15},{10,... | collective-permute-start | bytes 245768 | tf_op jit(solution)/shard_map/ppermute | solution.py:180
  32.9 4.4 %collective-permute-start.9 = (f32[160,128]{1,0:T(8,128)S(1)}, f32[160,128]{1,0:T(8,128)S(1)}, u32[]{:S(2)}, u32[]{:S(2)}) collective-permute-start(f32[160,128]{1,0:T(8,128)S(1)} %get-tuple-element.28), channel_id=1, source_target_pairs={{0,4},{1,5},{2,6},{3,7},{4,0},{5,1},{6,2},{7,3},{8,12},{9,13},{10,... | collective-permute-start | bytes 245768 | tf_op jit(solution)/shard_map/ppermute | solution.py:180
  37.3 7.9 %collective-permute-start.11 = (f32[160,128]{1,0:T(8,128)S(1)}, f32[160,128]{1,0:T(8,128)S(1)}, u32[]{:S(2)}, u32[]{:S(2)}) collective-permute-start(f32[160,128]{1,0:T(8,128)S(1)} %fusion.1), channel_id=1, source_target_pairs={{0,8},{1,9},{2,10},{3,11},{4,12},{5,13},{6,14},{7,15},{8,0},{9,1},... | collective-permute-start | bytes 245768 | tf_op jit(solution)/shard_map/ppermute | solution.py:180
  45.3 5.5 %collective-permute-start.12 = (f32[160,128]{1,0:T(8,128)S(1)}, f32[160,128]{1,0:T(8,128)S(1)}, u32[]{:S(2)}, u32[]{:S(2)}) collective-permute-start(f32[160,128]{1,0:T(8,128)S(1)} %add.63), channel_id=1, source_target_pairs={{0,16},{1,17},{2,18},{3,19},{4,20},{5,21},{6,22},{7,23},{8,24},{9,... | collective-permute-start | bytes 245768 | tf_op jit(solution)/shard_map/ppermute | solution.py:180
  50.7 5.4 %collective-permute-start.15 = (f32[160,128]{1,0:T(8,128)S(1)}, f32[160,128]{1,0:T(8,128)S(1)}, u32[]{:S(2)}, u32[]{:S(2)}) collective-permute-start(f32[160,128]{1,0:T(8,128)S(1)} %add.64), channel_id=1, source_target_pairs={{0,6},{1,7},{2,4},{3,5},{4,2},{5,3},{6,0},{7,1},{8,14},{9,15},{10,... | collective-permute-start | bytes 245768 | tf_op jit(solution)/shard_map/ppermute | solution.py:180
  53.0 4.4 %collective-permute-start.14 = (f32[160,128]{1,0:T(8,128)S(1)}, f32[160,128]{1,0:T(8,128)S(1)}, u32[]{:S(2)}, u32[]{:S(2)}) collective-permute-start(f32[160,128]{1,0:T(8,128)S(1)} %add.64), channel_id=1, source_target_pairs={{0,4},{1,5},{2,6},{3,7},{4,0},{5,1},{6,2},{7,3},{8,12},{9,13},{10,... | collective-permute-start | bytes 245768 | tf_op jit(solution)/shard_map/ppermute | solution.py:180
  53.8 4.4 %collective-permute-start.13 = (f32[160,128]{1,0:T(8,128)S(1)}, f32[160,128]{1,0:T(8,128)S(1)}, u32[]{:S(2)}, u32[]{:S(2)}) collective-permute-start(f32[160,128]{1,0:T(8,128)S(1)} %add.64), channel_id=1, source_target_pairs={{0,2},{1,3},{2,0},{3,1},{4,6},{5,7},{6,4},{7,5},{8,10},{9,11},{10,... | collective-permute-start | bytes 245768 | tf_op jit(solution)/shard_map/ppermute | solution.py:180
  58.2 0.9 %copy-start.2 = (f32[512,64]{0,1:T(8,128)S(1)}, f32[512,64]{0,1:T(8,128)}, u32[]{:S(2)}) copy-start(f32[512,64]{0,1:T(8,128)} %param.5) | copy-start | bytes 393220
  58.3 1.7 %collective-permute-start.16 = (f32[4,160,128]{2,1,0:T(8,128)S(1)}, f32[4,160,128]{2,1,0:T(8,128)S(1)}, u32[]{:S(2)}, u32[]{:S(2)}) collective-permute-start(f32[4,160,128]{2,1,0:T(8,128)S(1)} %pad_maximum_fusion.refs_1_), channel_id=1, source_target_pairs={{0,1},{1,0},{2,3},{3,2},{4,5},{5,4},{6,7},{7,6},{8,9},{9,8},{10,11... | collective-permute-start | bytes 983048 | tf_op jit(solution)/shard_map/ppermute | solution.py:180

commit v4 on v3

--- a/solution.py
+++ b/solution.py
@@ -25,14 +25,10 @@
     return [(i, j) for i in range(count) for j in range(i, count)]
 
 
-def factor_half(square):
+def factor_half(rows, shift, work):
     tile = (8, LANES)
     sub = lax.broadcasted_iota(jnp.int32, tile, 0)
-    eye = (
-        lax.broadcasted_iota(jnp.int32, (HALF, HALF), 0)
-        == lax.broadcasted_iota(jnp.int32, (HALF, HALF), 1)
-    ).astype(jnp.float32)
-    both = jnp.concatenate([square, eye], axis=1)
+    both = jnp.where(own_lanes(shift), rows, unit_rows(HALF - shift))
     count = HALF // 8
     strips = [both[8 * j : 8 * j + 8, :] for j in range(count)]
 
@@ -40,59 +36,60 @@
         return jnp.broadcast_to(value[at : at + 1, :], tile)
 
     def spread_column(value, at):
-        return jnp.broadcast_to(value[:, at : at + 1], tile)
+        return jnp.broadcast_to(value[:, shift + at : shift + at + 1], tile)
 
     ahead = [spread_column(strips[0], t) for t in range(8)]
     for m in range(count):
-        columns = {(m, t): ahead[t] for t in range(8)}
-        for j in range(m + 1, count):
+        columns, near = ahead, {}
+        close = range(m + 1, min(m + 1 + 8, count))
+        for j in close:
             for t in range(8):
-                columns[j, t] = spread_column(strips[j], 8 * m + t)
+                near[j, t] = spread_column(strips[j], 8 * m + t)
         if m + 1 < count:
             ahead = [spread_column(strips[m + 1], 8 * m + 8 + t) for t in range(8)]
-        corner = {(t, u): spread_row(columns[m, u], t) for t in range(8) for u in range(t, 8)}
+        corner = {(t, u): spread_row(columns[u], t) for t in range(8) for u in range(t, 8)}
+        rows_left = [spread_row(strips[m], t) for t in range(8)]
+        lines = []
         for t in range(8):
             root = lax.rsqrt(corner[t, t])
             line = {u: corner[t, u] * root for u in range(t + 1, 8)}
             for u in range(t + 1, 8):
                 for v in range(u, 8):
                     corner[u, v] = corner[u, v] - line[u] * line[v]
-            row = spread_row(strips[m], t) * root
-            for j in range(m, count):
-                column = columns[j, t] * root
-                if j == m:
-                    column = jnp.where(sub > t, column, 0.0)
+            row = rows_left[t] * root
+            lines.append(row)
+            for u in range(t + 1, 8):
+                rows_left[u] = rows_left[u] - line[u] * row
+            for j in close:
+                column = near[j, t] * root
                 for u in range(t + 1, 8):
-                    columns[j, u] = columns[j, u] - column * line[u]
-                updated = strips[j] - column * row
-                strips[j] = jnp.where(sub == t, row, updated) if j == m else updated
+                    near[j, u] = near[j, u] - column * line[u]
+                strips[j] = strips[j] - column * row
                 if j == m + 1:
                     ahead = [ahead[u] - column * spread_row(column, u) for u in range(8)]
+        done = lines[0]
+        for t in range(1, 8):
+            done = jnp.where(sub == t, lines[t], done)
+        strips[m] = done
+        for _ in range(-(-len(work) // (count - m))):
+            work.pop(0)()
     return jnp.concatenate(strips, axis=0)
 
 
-def upper_part(square):
-    shape = square.shape
-    keep = lax.broadcasted_iota(jnp.int32, shape, 0) <= lax.broadcasted_iota(jnp.int32, shape, 1)
-    return jnp.where(keep, square, 0.0)
-
-
-def factor_block(square):
-    low, high = slice(0, HALF), slice(HALF, BLOCK)
-    both = factor_half(square[low, low])
-    r00, v00 = upper_part(both[:, :HALF]), both[:, HALF:]
-    r01 = dot(v00, square[low, high])
-    both = factor_half(square[high, high] - dot(r01, r01, FIRST))
-    r11, v11 = upper_part(both[:, :HALF]), both[:, HALF:]
-    v10 = -dot(v11, dot(r01, v00, FIRST))
-    zero = jnp.zeros((HALF, HALF), jnp.float32)
-    factor = jnp.concatenate(
-        [jnp.concatenate([r00, r01], axis=1), jnp.concatenate([zero, r11], axis=1)], axis=0
-    )
-    inverse = jnp.concatenate(
-        [jnp.concatenate([v00, zero], axis=1), jnp.concatenate([v10, v11], axis=1)], axis=0
-    )
-    return factor, inverse
+def lane_index():
+    return lax.broadcasted_iota(jnp.int32, (HALF, LANES), 1)
+
+
+def row_index():
+    return lax.broadcasted_iota(jnp.int32, (HALF, LANES), 0)
+
+
+def own_lanes(shift):
+    return lane_index() < HALF if shift == 0 else lane_index() >= HALF
+
+
+def unit_rows(shift):
+    return (lane_index() == row_index() + shift).astype(jnp.float32)
 
 
 def pack_kernel(partners, waited, place_ref, field_ref, *refs):
@@ -124,7 +121,19 @@
 
 
 def factor_kernel(
-    scale, place_ref, mine_ref, other_ref, design_ref, anomaly_ref, basis_ref, factor_ref, gram_ref, inv_ref
+    scale,
+    place_ref,
+    mine_ref,
+    other_ref,
+    design_ref,
+    anomaly_ref,
+    basis_ref,
+    out_ref,
+    gram_ref,
+    inv_ref,
+    factor_ref,
+    mix_ref,
+    sems,
 ):
     count = factor_ref.shape[0] // BLOCK
     slots, size = mine_ref.shape[0], mine_ref.shape[1]
@@ -134,46 +143,130 @@
         for side, ref in ((half, mine_ref), (1 - half, other_ref)):
             start = pl.multiple_of((side * slots + piece) * size, 8)
             gram_ref[pl.ds(start, size), :] = ref[slot] * scale
-    pairs = upper_pairs(count)
-    where = {pair: at for at, pair in enumerate(pairs)}
-
-    def gram_at(i, j):
-        return pl.ds(where[i, j] * BLOCK, BLOCK)
-
-    def span(i):
-        return pl.ds(i * BLOCK, BLOCK)
-
+    where = {pair: at for at, pair in enumerate(upper_pairs(count))}
+    zero = jnp.zeros((HALF, LANES), jnp.float32)
+
+    def gram_at(i, j, side=None):
+        start = where[i, j] * BLOCK
+        return pl.ds(start, BLOCK) if side is None else pl.ds(start + side * HALF, HALF)
+
+    def span(i, side=None):
+        return pl.ds(i * BLOCK, BLOCK) if side is None else pl.ds(i * BLOCK + side * HALF, HALF)
+
+    def apply(solved, side, rows):
+        return dot(solved, jnp.concatenate([zero, rows] if side == 0 else [rows, zero], axis=0))
+
+    def row_factor(k, side, solved, j):
+        def run():
+            factor_ref[span(k, side), span(j)] = apply(solved, side, gram_ref[gram_at(k, j, side), :])
+
+        return run
+
+    def row_inverse(k, side, solved, j):
+        def run():
+            if j < k:
+                rows = inv_ref[span(k, side), span(j)]
+            elif side == 0:
+                rows = unit_rows(0)
+            else:
+                rows = inv_ref[span(k, 1), span(k)] + unit_rows(HALF)
+            inv_ref[span(k, side), span(j)] = apply(solved, side, rows)
+
+        return run
+
+    def lower_gram(k, first, j):
+        def run():
+            part = dot(first, factor_ref[span(k, 0), span(j)], FIRST)[HALF:, :]
+            gram_ref[gram_at(k, j, 1), :] = gram_ref[gram_at(k, j, 1), :] - part
+
+        return run
+
+    def lower_inverse(k, first, j):
+        def run():
+            part = dot(first, inv_ref[span(k, 0), span(j)], FIRST)[HALF:, :]
+            old = inv_ref[span(k, 1), span(j)] if j < k else 0.0
+            inv_ref[span(k, 1), span(j)] = old - part
+
+        return run
+
+    def next_gram(k, side):
+        def run():
+            rows = factor_ref[span(k, side), span(k + 1)]
+            at = gram_at(k + 1, k + 1)
+            gram_ref[at, :] = gram_ref[at, :] - dot(rows, rows, FIRST)
+
+        return run
+
+    def later_gram(k, i, j):
+        def run():
+            part = dot(factor_ref[span(k), span(i)], factor_ref[span(k), span(j)], FIRST)
+            gram_ref[gram_at(i, j), :] = gram_ref[gram_at(i, j), :] - part
+
+        return run
+
+    def later_inverse(k, i, j):
+        def run():
+            part = dot(factor_ref[span(k), span(i)], inv_ref[span(k), span(j)], FIRST)
+            old = inv_ref[span(i), span(j)] if j < k else 0.0
+            inv_ref[span(i), span(j)] = old - part
+
+        return run
+
+    def mix(k, j):
+        def run():
+            part = dot(design_ref[span(k), :], inv_ref[span(k), span(j)], FIRST)
+            mix_ref[:, span(j)] = part if j == k else mix_ref[:, span(j)] + part
+
+        return run
+
+    def send(k):
+        return pltpu.make_async_copy(
+            factor_ref.at[span(k), :], out_ref.at[span(k), :], sems.at[k]
+        )
+
+    work = []
     for k in range(count):
-        factor, inverse = factor_block(gram_ref[gram_at(k, k), :])
-        factor_ref[span(k), span(k)] = factor
-        rows = {}
+        for j in range(k):
+            factor_ref[span(k), span(j)] = jnp.zeros((BLOCK, BLOCK), jnp.float32)
+        solved = factor_half(gram_ref[gram_at(k, k, 0), :], 0, work)
+        first = apply(solved, 0, gram_ref[gram_at(k, k, 0), :])
+        lower = gram_ref[gram_at(k, k, 1), :] - dot(first, first, FIRST)[HALF:, :]
+        first = jnp.where(
+            own_lanes(0), jnp.where(lane_index() >= row_index(), solved, 0.0), first
+        )
+        factor_ref[span(k, 0), span(k)] = first
         for j in range(k + 1, count):
-            rows[j] = dot(inverse, gram_ref[gram_at(k, j), :])
-            factor_ref[span(k), span(j)] = rows[j]
-            factor_ref[span(j), span(k)] = jnp.zeros((BLOCK, BLOCK), jnp.float32)
+            work += [row_factor(k, 0, solved, j), lower_gram(k, first, j)]
+            if j == k + 1:
+                work.append(next_gram(k, 0))
+        for j in range(k + 1):
+            work += [row_inverse(k, 0, solved, j), lower_inverse(k, first, j)]
+        solved = factor_half(lower, HALF, work)
+        factor_ref[span(k, 1), span(k)] = jnp.where(
+            lane_index() >= row_index() + HALF, solved, 0.0
+        )
+        if k + 1 < count:
+            row_factor(k, 1, solved, k + 1)()
+            next_gram(k, 1)()
+        for j in range(k + 2, count):
+            work.append(row_factor(k, 1, solved, j))
+        work.append(send(k).start)
         for i in range(k + 1, count):
-            for j in range(i, count):
-                gram_ref[gram_at(i, j), :] = gram_ref[gram_at(i, j), :] - dot(
-                    rows[i], rows[j], FIRST
-                )
-        done = {}
-        for j in range(k):
-            done[j] = dot(inverse, inv_ref[span(k), span(j)])
-            inv_ref[span(k), span(j)] = done[j]
-        done[k] = inverse
-        inv_ref[span(k), span(k)] = inverse
+            work += [later_gram(k, i, j) for j in range(i, count) if (i, j) != (k + 1, k + 1)]
+        work += [row_inverse(k, 1, solved, j) for j in range(k + 1)]
         for i in range(k + 1, count):
-            for j in range(k + 1):
-                old = inv_ref[span(i), span(j)] if j < k else 0.0
-                inv_ref[span(i), span(j)] = old - dot(rows[i], done[j], FIRST)
-    columns = []
-    for j in range(count):
-        tail = pl.ds(j * BLOCK, (count - j) * BLOCK)
-        columns.append(dot(design_ref[tail, :], inv_ref[tail, span(j)], FIRST))
-    mixing = jnp.concatenate(columns, axis=1).astype(jnp.bfloat16)
+            work += [later_inverse(k, i, j) for j in range(k + 1)]
+        work += [mix(k, j) for j in range(k + 1)]
+    while work:
+        work.pop(0)()
     basis_ref[...] = lax.dot_general(
-        mixing, anomaly_ref[...], NARROW, preferred_element_type=jnp.float32
+        mix_ref[...].astype(jnp.bfloat16),
+        anomaly_ref[...],
+        NARROW,
+        preferred_element_type=jnp.float32,
     ).astype(jnp.bfloat16)
+    for k in range(count):
+        send(k).wait()
 
 
 def swap(value, mask, devices):
@@ -251,10 +344,13 @@
             jax.ShapeDtypeStruct((runs, runs), jnp.float32),
         ),
         in_specs=[smem, vmem, vmem, vmem, vmem],
-        out_specs=(vmem, vmem),
+        out_specs=(vmem, pl.BlockSpec(memory_space=pl.ANY)),
         scratch_shapes=[
             pltpu.VMEM((packed, LANES), jnp.float32),
             pltpu.VMEM((runs, runs), jnp.float32),
+            pltpu.VMEM((runs, runs), jnp.float32),
+            pltpu.VMEM((modes, runs), jnp.float32),
+            pltpu.SemaphoreType.DMA((blocks,)),
         ],
         compiler_params=pltpu.CompilerParams(vmem_limit_bytes=32 * 2**20),
     )(jnp.stack([half, quarter]).astype(jnp.int32), mine, other, design, anomaly)

time: 76.6 us -> 75.2 us (0.982)
  Pallas kernels: 17.6 us -> 16.1 us
    pallas_call x1, Pallas kernels: 16.4 us -> 14.9 us  [shards(): pl.pallas_call(kernel, out_shape=(jax.ShapeDtypeStruct((modes, slab), jnp...]
where the time goes in v4:
time: 75.2 us; the launch traced here: 75 us
  starting transfers between devices  31.2 us (41%)
  waiting for transfers between devices  24.3 us (32%)
  Pallas kernels  16.1 us (21%)
  local copies, waits for them, and re-layouts  2.2 us (3%)
  between operations  0.97 us (1%)
    ppermute x10, starting transfers between devices, swap(): return lax.ppermute(value, AXES, [(i, i ^ mask) for i in range(devices)])  15.9 us
    ppermute x7, starting transfers between devices, shards(): pieces[m] = lax.ppermute(piece, 'cells', route) if m else piece  15.3 us
    ppermute x10, waiting for transfers between devices, swap(): return lax.ppermute(value, AXES, [(i, i ^ mask) for i in range(devices)])  15.3 us
    pallas_call x1, Pallas kernels, shards(): pl.pallas_call(kernel, out_shape=(jax.ShapeDtypeStruct((modes, slab), jnp...  14.9 us
    ppermute x7, waiting for transfers between devices, shards(): pieces[m] = lax.ppermute(piece, 'cells', route) if m else piece  9.02 us
    unnamed x7, local copies, waits for them, and re-layouts  2.14 us
  transfers between devices with their start and end apart: 17, of which 13 were waited for; matrix products, arithmetic and copies ran while one was open for 0% of the time, Pallas kernels for 0%

profile of v4, /device:TPU:0, one launch (start us, length us, event | category | flops | bytes accessed | tf_op | source)
XLA Modules:
  0.0 75.0 jit_solution(3728550000317882337)
XLA Ops:
  0.6 0.0 copy-start
  0.6 1.2 %copy-done = bf16[64,1,8192]{2,0,1:T(8,128)(2,1)S(1)} copy-done((bf16[64,1,8192]{2,0,1:T(8,128)(2,1)S(1)}, bf16[64,1,8192]{2,0,1:T(8,128)(2,1)}, u32[]{:S(2)}) %copy-start) | copy-done | bytes 1048600
  1.9 4.0 %collective-permute-start = (bf16[64,1024]{1,0:T(8,128)(2,1)S(1)}, bf16[64,1024]{1,0:T(8,128)(2,1)S(1)}, u32[]{:S(2)}, u32[]{:S(2)}) collective-permute-start(bf16[64,1024]{1,0:T(8,128)(2,1)S(1)} %get-tuple-element.15), channel_id=1, source_target_pairs={{0,12},{4,8},{8,4},{12,0},{16,28},{20,24},{24,20},{28,16},{1,13},{... | collective-permute-start | bytes 393224 | tf_op jit(solution)/shard_map/ppermute | solution.py:300
  5.9 2.6 %collective-permute-start.3 = (bf16[64,1024]{1,0:T(8,128)(2,1)S(1)}, bf16[64,1024]{1,0:T(8,128)(2,1)S(1)}, u32[]{:S(2)}, u32[]{:S(2)}) collective-permute-start(bf16[64,1024]{1,0:T(8,128)(2,1)S(1)} %get-tuple-element.18), channel_id=1, source_target_pairs={{0,16},{4,20},{8,24},{12,28},{16,0},{20,4},{24,8},{28,12},{1,17},{... | collective-permute-start | bytes 393224 | tf_op jit(solution)/shard_map/ppermute | solution.py:300
  8.5 0.3 collective-permute-start.4
  8.8 2.5 %collective-permute-done.refs_0_.refs_3_ = bf16[64,1024]{1,0:T(8,128)(2,1)S(1)} collective-permute-done((bf16[64,1024]{1,0:T(8,128)(2,1)S(1)}, bf16[64,1024]{1,0:T(8,128)(2,1)S(1)}, u32[]{:S(2)}, u32[]{:S(2)}) %collective-permute-start) | collective-permute-done | bytes 131104 | tf_op jit(solution)/shard_map/ppermute | solution.py:300
  11.3 1.9 %collective-permute-start.1 = (bf16[64,1024]{1,0:T(8,128)(2,1)S(1)}, bf16[64,1024]{1,0:T(8,128)(2,1)S(1)}, u32[]{:S(2)}, u32[]{:S(2)}) collective-permute-start(bf16[64,1024]{1,0:T(8,128)(2,1)S(1)} %get-tuple-element.16), channel_id=1, source_target_pairs={{0,4},{4,0},{8,12},{12,8},{16,20},{20,16},{24,28},{28,24},{1,5},{5... | collective-permute-start | bytes 393224 | tf_op jit(solution)/shard_map/ppermute | solution.py:300
  13.2 0.0 collective-permute-start.2
  13.2 3.1 %collective-permute-start.5 = (bf16[64,1024]{1,0:T(8,128)(2,1)S(1)}, bf16[64,1024]{1,0:T(8,128)(2,1)S(1)}, u32[]{:S(2)}, u32[]{:S(2)}) collective-permute-start(bf16[64,1024]{1,0:T(8,128)(2,1)S(1)} %get-tuple-element.20), channel_id=1, source_target_pairs={{0,24},{4,28},{8,16},{12,20},{16,8},{20,12},{24,0},{28,4},{1,25},{... | collective-permute-start | bytes 393224 | tf_op jit(solution)/shard_map/ppermute | solution.py:300
  16.3 2.1 %collective-permute-done.3.refs_4_ = bf16[64,1024]{1,0:T(8,128)(2,1)S(1)} collective-permute-done((bf16[64,1024]{1,0:T(8,128)(2,1)S(1)}, bf16[64,1024]{1,0:T(8,128)(2,1)S(1)}, u32[]{:S(2)}, u32[]{:S(2)}) %collective-permute-start.3) | collective-permute-done | bytes 131104 | tf_op jit(solution)/shard_map/ppermute | solution.py:300
  18.4 3.4 %collective-permute-start.6 = (bf16[64,1024]{1,0:T(8,128)(2,1)S(1)}, bf16[64,1024]{1,0:T(8,128)(2,1)S(1)}, u32[]{:S(2)}, u32[]{:S(2)}) collective-permute-start(bf16[64,1024]{1,0:T(8,128)(2,1)S(1)} %get-tuple-element.21), channel_id=1, source_target_pairs={{0,28},{4,24},{8,20},{12,16},{16,12},{20,8},{24,4},{28,0},{1,29},{... | collective-permute-start | bytes 393224 | tf_op jit(solution)/shard_map/ppermute | solution.py:300
  21.8 0.0 copy-start.1
  21.8 4.5 %collective-permute-done.4.refs_5_ = bf16[64,1024]{1,0:T(8,128)(2,1)S(1)} collective-permute-done((bf16[64,1024]{1,0:T(8,128)(2,1)S(1)}, bf16[64,1024]{1,0:T(8,128)(2,1)S(1)}, u32[]{:S(2)}, u32[]{:S(2)}) %collective-permute-start.4) | collective-permute-done | bytes 131104 | tf_op jit(solution)/shard_map/ppermute | solution.py:300
  26.3 0.0 collective-permute-done.1.refs_1_
  26.3 0.0 collective-permute-done.2.refs_2_
  26.3 0.0 collective-permute-done.5.refs_6_
  26.3 0.0 collective-permute-done.6.refs_7_
  26.3 0.0 copy-done.1
  26.3 1.1 %shard_map.52 = (bf16[512,1024]{1,0:T(8,128)(2,1)S(1)}, f32[1280,128]{1,0:T(8,128)S(1)}) custom-call(s32[1]{0:T(128)} %bitcast.2.place_ref, bf16[64,1024]{1,0:T(8,128)(2,1)S(1)} %get-tuple-element.14.refs_0_, bf16[64,1024]{1,0:T(8,128)(2,1)S(1)} %collective-permute-done.1.refs_1_, bf16[64,1024]{1,0:T(8,128)(2,1)S(1)} %collective-permute-done.2.refs_2_, ...), custom_call_target="tpu_custom_call" | custom-call | tf_op jit(solution)/shard_map/pallas_call | solution.py:306
  27.5 0.1 collective-permute-start.7
  27.6 1.6 %collective-permute-done.7 = f32[640,128]{1,0:T(8,128)S(1)} collective-permute-done((f32[640,128]{1,0:T(8,128)S(1)}, f32[640,128]{1,0:T(8,128)S(1)}, u32[]{:S(2)}, u32[]{:S(2)}) %collective-permute-start.7) | collective-permute-done | bytes 327712 | tf_op jit(solution)/shard_map/ppermute | solution.py:273
  29.3 1.6 %collective-permute-start.8 = (f32[160,128]{1,0:T(8,128)S(1)}, f32[160,128]{1,0:T(8,128)S(1)}, u32[]{:S(2)}, u32[]{:S(2)}) collective-permute-start(f32[160,128]{1,0:T(8,128)S(1)} %get-tuple-element.26), channel_id=1, source_target_pairs={{0,2},{1,3},{2,0},{3,1},{4,6},{5,7},{6,4},{7,5},{8,10},{9,11},{10,... | collective-permute-start | bytes 245768 | tf_op jit(solution)/shard_map/ppermute | solution.py:273
  30.9 2.0 %collective-permute-start.10 = (f32[160,128]{1,0:T(8,128)S(1)}, f32[160,128]{1,0:T(8,128)S(1)}, u32[]{:S(2)}, u32[]{:S(2)}) collective-permute-start(f32[160,128]{1,0:T(8,128)S(1)} %get-tuple-element.27), channel_id=1, source_target_pairs={{0,6},{1,7},{2,4},{3,5},{4,2},{5,3},{6,0},{7,1},{8,14},{9,15},{10,... | collective-permute-start | bytes 245768 | tf_op jit(solution)/shard_map/ppermute | solution.py:273
  32.9 0.1 collective-permute-start.9
  32.9 0.9 %collective-permute-done.8 = f32[160,128]{1,0:T(8,128)S(1)} collective-permute-done((f32[160,128]{1,0:T(8,128)S(1)}, f32[160,128]{1,0:T(8,128)S(1)}, u32[]{:S(2)}, u32[]{:S(2)}) %collective-permute-start.8) | collective-permute-done | bytes 81952 | tf_op jit(solution)/shard_map/ppermute | solution.py:273
  33.8 2.6 %collective-permute-done.10 = f32[160,128]{1,0:T(8,128)S(1)} collective-permute-done((f32[160,128]{1,0:T(8,128)S(1)}, f32[160,128]{1,0:T(8,128)S(1)}, u32[]{:S(2)}, u32[]{:S(2)}) %collective-permute-start.10) | collective-permute-done | bytes 81952 | tf_op jit(solution)/shard_map/ppermute | solution.py:273
  36.5 0.8 %collective-permute-done.9 = f32[160,128]{1,0:T(8,128)S(1)} collective-permute-done((f32[160,128]{1,0:T(8,128)S(1)}, f32[160,128]{1,0:T(8,128)S(1)}, u32[]{:S(2)}, u32[]{:S(2)}) %collective-permute-start.9) | collective-permute-done | bytes 81952 | tf_op jit(solution)/shard_map/ppermute | solution.py:273
  37.3 5.5 %collective-permute-start.11 = (f32[160,128]{1,0:T(8,128)S(1)}, f32[160,128]{1,0:T(8,128)S(1)}, u32[]{:S(2)}, u32[]{:S(2)}) collective-permute-start(f32[160,128]{1,0:T(8,128)S(1)} %fusion.1), channel_id=1, source_target_pairs={{0,8},{1,9},{2,10},{3,11},{4,12},{5,13},{6,14},{7,15},{8,0},{9,1},... | collective-permute-start | bytes 245768 | tf_op jit(solution)/shard_map/ppermute | solution.py:273
  42.8 2.4 %collective-permute-done.11 = f32[160,128]{1,0:T(8,128)S(1)} collective-permute-done((f32[160,128]{1,0:T(8,128)S(1)}, f32[160,128]{1,0:T(8,128)S(1)}, u32[]{:S(2)}, u32[]{:S(2)}) %collective-permute-start.11) | collective-permute-done | bytes 81952 | tf_op jit(solution)/shard_map/ppermute | solution.py:273
  45.3 3.0 %collective-permute-start.12 = (f32[160,128]{1,0:T(8,128)S(1)}, f32[160,128]{1,0:T(8,128)S(1)}, u32[]{:S(2)}, u32[]{:S(2)}) collective-permute-start(f32[160,128]{1,0:T(8,128)S(1)} %add.63), channel_id=1, source_target_pairs={{0,16},{1,17},{2,18},{3,19},{4,20},{5,21},{6,22},{7,23},{8,24},{9,... | collective-permute-start | bytes 245768 | tf_op jit(solution)/shard_map/ppermute | solution.py:273
  48.3 2.4 %collective-permute-done.12 = f32[160,128]{1,0:T(8,128)S(1)} collective-permute-done((f32[160,128]{1,0:T(8,128)S(1)}, f32[160,128]{1,0:T(8,128)S(1)}, u32[]{:S(2)}, u32[]{:S(2)}) %collective-permute-start.12) | collective-permute-done | bytes 81952 | tf_op jit(solution)/shard_map/ppermute | solution.py:273
  50.7 2.3 %collective-permute-start.15 = (f32[160,128]{1,0:T(8,128)S(1)}, f32[160,128]{1,0:T(8,128)S(1)}, u32[]{:S(2)}, u32[]{:S(2)}) collective-permute-start(f32[160,128]{1,0:T(8,128)S(1)} %add.64), channel_id=1, source_target_pairs={{0,6},{1,7},{2,4},{3,5},{4,2},{5,3},{6,0},{7,1},{8,14},{9,15},{10,... | collective-permute-start | bytes 245768 | tf_op jit(solution)/shard_map/ppermute | solution.py:273
  53.0 0.8 %collective-permute-start.14 = (f32[160,128]{1,0:T(8,128)S(1)}, f32[160,128]{1,0:T(8,128)S(1)}, u32[]{:S(2)}, u32[]{:S(2)}) collective-permute-start(f32[160,128]{1,0:T(8,128)S(1)} %add.64), channel_id=1, source_target_pairs={{0,4},{1,5},{2,6},{3,7},{4,0},{5,1},{6,2},{7,3},{8,12},{9,13},{10,... | collective-permute-start | bytes 245768 | tf_op jit(solution)/shard_map/ppermute | solution.py:273
  53.8 0.5 collective-permute-start.13
  54.3 1.9 %collective-permute-done.15 = f32[160,128]{1,0:T(8,128)S(1)} collective-permute-done((f32[160,128]{1,0:T(8,128)S(1)}, f32[160,128]{1,0:T(8,128)S(1)}, u32[]{:S(2)}, u32[]{:S(2)}) %collective-permute-start.15) | collective-permute-done | bytes 81952 | tf_op jit(solution)/shard_map/ppermute | solution.py:273
  56.1 1.3 %collective-permute-done.14 = f32[160,128]{1,0:T(8,128)S(1)} collective-permute-done((f32[160,128]{1,0:T(8,128)S(1)}, f32[160,128]{1,0:T(8,128)S(1)}, u32[]{:S(2)}, u32[]{:S(2)}) %collective-permute-start.14) | collective-permute-done | bytes 81952 | tf_op jit(solution)/shard_map/ppermute | solution.py:273
  57.5 0.8 %collective-permute-done.13 = f32[160,128]{1,0:T(8,128)S(1)} collective-permute-done((f32[160,128]{1,0:T(8,128)S(1)}, f32[160,128]{1,0:T(8,128)S(1)}, u32[]{:S(2)}, u32[]{:S(2)}) %collective-permute-start.13) | collective-permute-done | bytes 81952 | tf_op jit(solution)/shard_map/ppermute | solution.py:273
  58.2 0.0 copy-start.2
  58.3 0.1 collective-permute-start.16
  58.3 0.8 %copy-done.2 = f32[512,64]{0,1:T(8,128)S(1)} copy-done((f32[512,64]{0,1:T(8,128)S(1)}, f32[512,64]{0,1:T(8,128)}, u32[]{:S(2)}) %copy-start.2) | copy-done | bytes 131096
  59.1 0.1 copy.5.refs_3_
  59.3 0.1 pad_add_fusion.refs_0_
  59.3 0.6 collective-permute-done.16.refs_2_
  60.0 14.9 %shard_map.53 = (bf16[64,1024]{1,0:T(8,128)(2,1)}, f32[512,512]{1,0:T(8,128)}) custom-call(s32[2]{0:T(128)S(1)} %pad_add_fusion.refs_0_, f32[4,160,128]{2,1,0:T(8,128)S(1)} %pad_maximum_fusion.refs_1_, f32[4,160,128]{2,1,0:T(8,128)S(1)} %collective-permute-done.16.refs_2_, f32[512,64]{1,0:T(8,128)S(1)} %copy.5.refs_3_, ...), custom_call_target="tpu_custom_call" | custom-call | tf_op jit(solution)/shard_map/pallas_call | solution.py:340
  (9 shorter events, 0.2 us)
Async XLA Ops:
  0.6 1.2 %copy-start = (bf16[64,1,8192]{2,0,1:T(8,128)(2,1)S(1)}, bf16[64,1,8192]{2,0,1:T(8,128)(2,1)}, u32[]{:S(2)}) copy-start(bf16[64,1,8192]{2,0,1:T(8,128)(2,1)} %param.3) | copy-start | bytes 3145732
  1.9 9.4 %collective-permute-start = (bf16[64,1024]{1,0:T(8,128)(2,1)S(1)}, bf16[64,1024]{1,0:T(8,128)(2,1)S(1)}, u32[]{:S(2)}, u32[]{:S(2)}) collective-permute-start(bf16[64,1024]{1,0:T(8,128)(2,1)S(1)} %get-tuple-element.15), channel_id=1, source_target_pairs={{0,12},{4,8},{8,4},{12,0},{16,28},{20,24},{24,20},{28,16},{1,13},{... | collective-permute-start | bytes 393224 | tf_op jit(solution)/shard_map/ppermute | solution.py:300
  5.9 12.5 %collective-permute-start.3 = (bf16[64,1024]{1,0:T(8,128)(2,1)S(1)}, bf16[64,1024]{1,0:T(8,128)(2,1)S(1)}, u32[]{:S(2)}, u32[]{:S(2)}) collective-permute-start(bf16[64,1024]{1,0:T(8,128)(2,1)S(1)} %get-tuple-element.18), channel_id=1, source_target_pairs={{0,16},{4,20},{8,24},{12,28},{16,0},{20,4},{24,8},{28,12},{1,17},{... | collective-permute-start | bytes 393224 | tf_op jit(solution)/shard_map/ppermute | solution.py:300
  8.5 17.8 %collective-permute-start.4 = (bf16[64,1024]{1,0:T(8,128)(2,1)S(1)}, bf16[64,1024]{1,0:T(8,128)(2,1)S(1)}, u32[]{:S(2)}, u32[]{:S(2)}) collective-permute-start(bf16[64,1024]{1,0:T(8,128)(2,1)S(1)} %get-tuple-element.19), channel_id=1, source_target_pairs={{0,20},{4,16},{8,28},{12,24},{16,4},{20,0},{24,12},{28,8},{1,21},{... | collective-permute-start | bytes 393224 | tf_op jit(solution)/shard_map/ppermute | solution.py:300
  11.3 15.0 %collective-permute-start.1 = (bf16[64,1024]{1,0:T(8,128)(2,1)S(1)}, bf16[64,1024]{1,0:T(8,128)(2,1)S(1)}, u32[]{:S(2)}, u32[]{:S(2)}) collective-permute-start(bf16[64,1024]{1,0:T(8,128)(2,1)S(1)} %get-tuple-element.16), channel_id=1, source_target_pairs={{0,4},{4,0},{8,12},{12,8},{16,20},{20,16},{24,28},{28,24},{1,5},{5... | collective-permute-start | bytes 393224 | tf_op jit(solution)/shard_map/ppermute | solution.py:300
  13.2 13.1 %collective-permute-start.2 = (bf16[64,1024]{1,0:T(8,128)(2,1)S(1)}, bf16[64,1024]{1,0:T(8,128)(2,1)S(1)}, u32[]{:S(2)}, u32[]{:S(2)}) collective-permute-start(bf16[64,1024]{1,0:T(8,128)(2,1)S(1)} %get-tuple-element.17), channel_id=1, source_target_pairs={{0,8},{4,12},{8,0},{12,4},{16,24},{20,28},{24,16},{28,20},{1,9},{5... | collective-permute-start | bytes 393224 | tf_op jit(solution)/shard_map/ppermute | solution.py:300
  13.2 13.1 %collective-permute-start.5 = (bf16[64,1024]{1,0:T(8,128)(2,1)S(1)}, bf16[64,1024]{1,0:T(8,128)(2,1)S(1)}, u32[]{:S(2)}, u32[]{:S(2)}) collective-permute-start(bf16[64,1024]{1,0:T(8,128)(2,1)S(1)} %get-tuple-element.20), channel_id=1, source_target_pairs={{0,24},{4,28},{8,16},{12,20},{16,8},{20,12},{24,0},{28,4},{1,25},{... | collective-permute-start | bytes 393224 | tf_op jit(solution)/shard_map/ppermute | solution.py:300
  18.4 7.9 %collective-permute-start.6 = (bf16[64,1024]{1,0:T(8,128)(2,1)S(1)}, bf16[64,1024]{1,0:T(8,128)(2,1)S(1)}, u32[]{:S(2)}, u32[]{:S(2)}) collective-permute-start(bf16[64,1024]{1,0:T(8,128)(2,1)S(1)} %get-tuple-element.21), channel_id=1, source_target_pairs={{0,28},{4,24},{8,20},{12,16},{16,12},{20,8},{24,4},{28,0},{1,29},{... | collective-permute-start | bytes 393224 | tf_op jit(solution)/shard_map/ppermute | solution.py:300
  21.8 4.5 %copy-start.1 = (bf16[1,1024]{1,0:T(2,128)(2,1)S(1)}, bf16[1,1024]{1,0:T(2,128)(2,1)}, u32[]{:S(2)}) copy-start(bf16[1,1024]{1,0:T(2,128)(2,1)} %refs_8_.1) | copy-start | bytes 6148
  27.5 1.7 %collective-permute-start.7 = (f32[640,128]{1,0:T(8,128)S(1)}, f32[640,128]{1,0:T(8,128)S(1)}, u32[]{:S(2)}, u32[]{:S(2)}) collective-permute-start(f32[640,128]{1,0:T(8,128)S(1)} %dynamic-slice_bitcast_fusion), channel_id=1, source_target_pairs={{0,1},{1,0},{2,3},{3,2},{4,5},{5,4},{6,7},{7,6},{8,9},{9,8},{10,11... | collective-permute-start | bytes 983048 | tf_op jit(solution)/shard_map/ppermute | solution.py:273
  29.3 4.6 %collective-permute-start.8 = (f32[160,128]{1,0:T(8,128)S(1)}, f32[160,128]{1,0:T(8,128)S(1)}, u32[]{:S(2)}, u32[]{:S(2)}) collective-permute-start(f32[160,128]{1,0:T(8,128)S(1)} %get-tuple-element.26), channel_id=1, source_target_pairs={{0,2},{1,3},{2,0},{3,1},{4,6},{5,7},{6,4},{7,5},{8,10},{9,11},{10,... | collective-permute-start | bytes 245768 | tf_op jit(solution)/shard_map/ppermute | solution.py:273
  30.9 5.6 %collective-permute-start.10 = (f32[160,128]{1,0:T(8,128)S(1)}, f32[160,128]{1,0:T(8,128)S(1)}, u32[]{:S(2)}, u32[]{:S(2)}) collective-permute-start(f32[160,128]{1,0:T(8,128)S(1)} %get-tuple-element.27), channel_id=1, source_target_pairs={{0,6},{1,7},{2,4},{3,5},{4,2},{5,3},{6,0},{7,1},{8,14},{9,15},{10,... | collective-permute-start | bytes 245768 | tf_op jit(solution)/shard_map/ppermute | solution.py:273
  32.9 4.4 %collective-permute-start.9 = (f32[160,128]{1,0:T(8,128)S(1)}, f32[160,128]{1,0:T(8,128)S(1)}, u32[]{:S(2)}, u32[]{:S(2)}) collective-permute-start(f32[160,128]{1,0:T(8,128)S(1)} %get-tuple-element.28), channel_id=1, source_target_pairs={{0,4},{1,5},{2,6},{3,7},{4,0},{5,1},{6,2},{7,3},{8,12},{9,13},{10,... | collective-permute-start | bytes 245768 | tf_op jit(solution)/shard_map/ppermute | solution.py:273
  37.3 7.9 %collective-permute-start.11 = (f32[160,128]{1,0:T(8,128)S(1)}, f32[160,128]{1,0:T(8,128)S(1)}, u32[]{:S(2)}, u32[]{:S(2)}) collective-permute-start(f32[160,128]{1,0:T(8,128)S(1)} %fusion.1), channel_id=1, source_target_pairs={{0,8},{1,9},{2,10},{3,11},{4,12},{5,13},{6,14},{7,15},{8,0},{9,1},... | collective-permute-start | bytes 245768 | tf_op jit(solution)/shard_map/ppermute | solution.py:273
  45.3 5.5 %collective-permute-start.12 = (f32[160,128]{1,0:T(8,128)S(1)}, f32[160,128]{1,0:T(8,128)S(1)}, u32[]{:S(2)}, u32[]{:S(2)}) collective-permute-start(f32[160,128]{1,0:T(8,128)S(1)} %add.63), channel_id=1, source_target_pairs={{0,16},{1,17},{2,18},{3,19},{4,20},{5,21},{6,22},{7,23},{8,24},{9,... | collective-permute-start | bytes 245768 | tf_op jit(solution)/shard_map/ppermute | solution.py:273
  50.7 5.4 %collective-permute-start.15 = (f32[160,128]{1,0:T(8,128)S(1)}, f32[160,128]{1,0:T(8,128)S(1)}, u32[]{:S(2)}, u32[]{:S(2)}) collective-permute-start(f32[160,128]{1,0:T(8,128)S(1)} %add.64), channel_id=1, source_target_pairs={{0,6},{1,7},{2,4},{3,5},{4,2},{5,3},{6,0},{7,1},{8,14},{9,15},{10,... | collective-permute-start | bytes 245768 | tf_op jit(solution)/shard_map/ppermute | solution.py:273
  53.0 4.4 %collective-permute-start.14 = (f32[160,128]{1,0:T(8,128)S(1)}, f32[160,128]{1,0:T(8,128)S(1)}, u32[]{:S(2)}, u32[]{:S(2)}) collective-permute-start(f32[160,128]{1,0:T(8,128)S(1)} %add.64), channel_id=1, source_target_pairs={{0,4},{1,5},{2,6},{3,7},{4,0},{5,1},{6,2},{7,3},{8,12},{9,13},{10,... | collective-permute-start | bytes 245768 | tf_op jit(solution)/shard_map/ppermute | solution.py:273
  53.8 4.4 %collective-permute-start.13 = (f32[160,128]{1,0:T(8,128)S(1)}, f32[160,128]{1,0:T(8,128)S(1)}, u32[]{:S(2)}, u32[]{:S(2)}) collective-permute-start(f32[160,128]{1,0:T(8,128)S(1)} %add.64), channel_id=1, source_target_pairs={{0,2},{1,3},{2,0},{3,1},{4,6},{5,7},{6,4},{7,5},{8,10},{9,11},{10,... | collective-permute-start | bytes 245768 | tf_op jit(solution)/shard_map/ppermute | solution.py:273
  58.2 0.9 %copy-start.2 = (f32[512,64]{0,1:T(8,128)S(1)}, f32[512,64]{0,1:T(8,128)}, u32[]{:S(2)}) copy-start(f32[512,64]{0,1:T(8,128)} %param.5) | copy-start | bytes 393220
  58.3 1.7 %collective-permute-start.16 = (f32[4,160,128]{2,1,0:T(8,128)S(1)}, f32[4,160,128]{2,1,0:T(8,128)S(1)}, u32[]{:S(2)}, u32[]{:S(2)}) collective-permute-start(f32[4,160,128]{2,1,0:T(8,128)S(1)} %pad_maximum_fusion.refs_1_), channel_id=1, source_target_pairs={{0,1},{1,0},{2,3},{3,2},{4,5},{5,4},{6,7},{7,6},{8,9},{9,8},{10,11... | collective-permute-start | bytes 983048 | tf_op jit(solution)/shard_map/ppermute | solution.py:273

commit v5 on v4

--- a/solution.py
+++ b/solution.py
@@ -23,6 +23,17 @@
 
 def upper_pairs(count):
     return [(i, j) for i in range(count) for j in range(i, count)]
+
+
+def packing(count):
+    places, tails, at = {}, [], 0
+    for i, j in upper_pairs(count):
+        places[i, j] = at
+        at += HALF if i == j else BLOCK
+    for _ in range(count // 2):
+        tails.append(at)
+        at += HALF
+    return places, tails, at
 
 
 def factor_half(rows, shift, work):
@@ -110,25 +121,32 @@
         anomaly_ref[pl.ds(pl.multiple_of(start, size), size), :] = (
             piece_ref[...].astype(jnp.float32) - base
         ).astype(jnp.bfloat16)
-    at = 0
+    places, tails, _ = packing(count)
+    kept = None
     for i in range(count):
         rows = anomaly_ref[pl.ds(i * BLOCK, BLOCK), :]
         rest = anomaly_ref[pl.ds(i * BLOCK, (count - i) * BLOCK), :]
         part = lax.dot_general(rows, rest, LAST, preferred_element_type=jnp.float32)
-        for j in range(count - i):
-            gram_ref[pl.ds(at * BLOCK, BLOCK), :] = part[:, j * BLOCK : (j + 1) * BLOCK]
-            at += 1
+        gram_ref[pl.ds(places[i, i], HALF), :] = part[:HALF, :BLOCK]
+        for j in range(i + 1, count):
+            at = (j - i) * BLOCK
+            gram_ref[pl.ds(places[i, j], BLOCK), :] = part[:, at : at + BLOCK]
+        corner = part[HALF:, HALF:BLOCK]
+        if i % 2 == 0:
+            kept = corner
+        else:
+            gram_ref[pl.ds(tails[i // 2], HALF), :] = jnp.concatenate([kept, corner], axis=1)
 
 
 def factor_kernel(
     scale,
     place_ref,
-    mine_ref,
-    other_ref,
+    piece_refs,
     design_ref,
     anomaly_ref,
     basis_ref,
     out_ref,
+    packed_ref,
     gram_ref,
     inv_ref,
     factor_ref,
@@ -136,14 +154,23 @@
     sems,
 ):
     count = factor_ref.shape[0] // BLOCK
-    slots, size = mine_ref.shape[0], mine_ref.shape[1]
+    slots, size = len(piece_refs) // 2, piece_refs[0].shape[0]
     half, quarter = place_ref[0], place_ref[1]
     for slot in range(slots):
         piece = lax.bitwise_xor(quarter, slot)
-        for side, ref in ((half, mine_ref), (1 - half, other_ref)):
+        for side, ref in ((half, piece_refs[slot]), (1 - half, piece_refs[slots + slot])):
             start = pl.multiple_of((side * slots + piece) * size, 8)
-            gram_ref[pl.ds(start, size), :] = ref[slot] * scale
+            packed_ref[pl.ds(start, size), :] = ref[...] * scale
+    places, tails, _ = packing(count)
     where = {pair: at for at, pair in enumerate(upper_pairs(count))}
+    for (i, j), at in where.items():
+        size = HALF if i == j else BLOCK
+        gram_ref[pl.ds(at * BLOCK, size), :] = packed_ref[pl.ds(places[i, j], size), :]
+        if i == j:
+            corner = packed_ref[pl.ds(tails[i // 2], HALF), :]
+            if i % 2 == 0:
+                corner = jnp.concatenate([corner[:, :HALF], corner[:, :HALF]], axis=1)
+            gram_ref[pl.ds(at * BLOCK + HALF, HALF), :] = corner
     zero = jnp.zeros((HALF, LANES), jnp.float32)
 
     def gram_at(i, j, side=None):
@@ -280,7 +307,7 @@
     runs, modes = design.shape
     slab = base_field.shape[1]
     blocks = runs // BLOCK
-    packed = len(upper_pairs(blocks)) * BLOCK
+    packed = packing(blocks)[2]
     vmem = pl.BlockSpec(memory_space=pltpu.VMEM)
     smem = pl.BlockSpec(memory_space=pltpu.SMEM)
     column = lax.axis_index("cells").astype(jnp.int32).reshape(1)
@@ -331,11 +358,11 @@
     while mask < devices:
         total = total + swap(total, mask, devices)
         mask *= 2
-    mine = jnp.stack([total] + [swap(total, 2 * m, devices) for m in (1, 2, 3)])
-    other = swap(mine, 1, devices)
+    mine = [total] + [swap(total, 2 * m, devices) for m in (1, 2, 3)]
+    other = [swap(piece, 1, devices) for piece in mine]
 
     def kernel(*refs):
-        factor_kernel(1.0 / (slab * devices), *refs)
+        factor_kernel(1.0 / (slab * devices), refs[0], refs[1:9], *refs[9:])
 
     basis, factor = pl.pallas_call(
         kernel,
@@ -343,17 +370,18 @@
             jax.ShapeDtypeStruct((modes, slab), jnp.bfloat16),
             jax.ShapeDtypeStruct((runs, runs), jnp.float32),
         ),
-        in_specs=[smem, vmem, vmem, vmem, vmem],
+        in_specs=[smem] + [vmem] * 10,
         out_specs=(vmem, pl.BlockSpec(memory_space=pl.ANY)),
         scratch_shapes=[
             pltpu.VMEM((packed, LANES), jnp.float32),
+            pltpu.VMEM((len(upper_pairs(blocks)) * BLOCK, LANES), jnp.float32),
             pltpu.VMEM((runs, runs), jnp.float32),
             pltpu.VMEM((runs, runs), jnp.float32),
             pltpu.VMEM((modes, runs), jnp.float32),
             pltpu.SemaphoreType.DMA((blocks,)),
         ],
         compiler_params=pltpu.CompilerParams(vmem_limit_bytes=32 * 2**20),
-    )(jnp.stack([half, quarter]).astype(jnp.int32), mine, other, design, anomaly)
+    )(jnp.stack([half, quarter]).astype(jnp.int32), *mine, *other, design, anomaly)
     return (basis.reshape(modes, 1, slab), factor)
 
 

time: 75.2 us -> 74.2 us (0.987)
  local copies, waits for them, and re-layouts: 2.2 us -> 1.4 us
    unnamed x7, local copies, waits for them, and re-layouts: 2.14 us -> 1.35 us
    ppermute x10 -> x13, waiting for transfers between devices: 15.3 us -> 15.2 us  [swap(): return lax.ppermute(value, AXES, [(i, i ^ mask) for i in range(devices)])]
    ppermute x10 -> x13, starting transfers between devices: 15.9 us -> 15.8 us  [swap(): return lax.ppermute(value, AXES, [(i, i ^ mask) for i in range(devices)])]
  transfers between devices with their start and end apart: 17 -> 20, of which waited for: 13 -> 14; matrix products, arithmetic and copies ran while one was open for 0% -> 0% of each run, Pallas kernels for 0% -> 0%
where the time goes in v5:
time: 74.2 us; the launch traced here: 74 us
  starting transfers between devices  31.1 us (42%)
  waiting for transfers between devices  24.2 us (33%)
  Pallas kernels  16.2 us (22%)
  local copies, waits for them, and re-layouts  1.4 us (2%)
  between operations  0.96 us (1%)
    ppermute x13, starting transfers between devices, swap(): return lax.ppermute(value, AXES, [(i, i ^ mask) for i in range(devices)])  15.8 us
    ppermute x7, starting transfers between devices, shards(): pieces[m] = lax.ppermute(piece, 'cells', route) if m else piece  15.3 us
    ppermute x13, waiting for transfers between devices, swap(): return lax.ppermute(value, AXES, [(i, i ^ mask) for i in range(devices)])  15.2 us
    pallas_call x1, Pallas kernels, shards(): pl.pallas_call(kernel, out_shape=(jax.ShapeDtypeStruct((modes, slab), jnp...  14.9 us
    ppermute x7, waiting for transfers between devices, shards(): pieces[m] = lax.ppermute(piece, 'cells', route) if m else piece  9.02 us
  transfers between devices with their start and end apart: 20, of which 14 were waited for; matrix products, arithmetic and copies ran while one was open for 0% of the time, Pallas kernels for 0%

profile of v5, /device:TPU:0, one launch (start us, length us, event | category | flops | bytes accessed | tf_op | source)
XLA Modules:
  0.0 74.0 jit_solution(11530844994406812256)
XLA Ops:
  0.6 0.0 copy-start
  0.6 1.2 %copy-done = bf16[64,1,8192]{2,0,1:T(8,128)(2,1)S(1)} copy-done((bf16[64,1,8192]{2,0,1:T(8,128)(2,1)S(1)}, bf16[64,1,8192]{2,0,1:T(8,128)(2,1)}, u32[]{:S(2)}) %copy-start) | copy-done | bytes 1048600
  1.9 4.0 %collective-permute-start = (bf16[64,1024]{1,0:T(8,128)(2,1)S(1)}, bf16[64,1024]{1,0:T(8,128)(2,1)S(1)}, u32[]{:S(2)}, u32[]{:S(2)}) collective-permute-start(bf16[64,1024]{1,0:T(8,128)(2,1)S(1)} %get-tuple-element.15), channel_id=1, source_target_pairs={{0,12},{4,8},{8,4},{12,0},{16,28},{20,24},{24,20},{28,16},{1,13},{... | collective-permute-start | bytes 393224 | tf_op jit(solution)/shard_map/ppermute | solution.py:327
  5.9 2.6 %collective-permute-start.3 = (bf16[64,1024]{1,0:T(8,128)(2,1)S(1)}, bf16[64,1024]{1,0:T(8,128)(2,1)S(1)}, u32[]{:S(2)}, u32[]{:S(2)}) collective-permute-start(bf16[64,1024]{1,0:T(8,128)(2,1)S(1)} %get-tuple-element.18), channel_id=1, source_target_pairs={{0,16},{4,20},{8,24},{12,28},{16,0},{20,4},{24,8},{28,12},{1,17},{... | collective-permute-start | bytes 393224 | tf_op jit(solution)/shard_map/ppermute | solution.py:327
  8.5 0.3 collective-permute-start.4
  8.8 2.5 %collective-permute-done.refs_0_.refs_3_ = bf16[64,1024]{1,0:T(8,128)(2,1)S(1)} collective-permute-done((bf16[64,1024]{1,0:T(8,128)(2,1)S(1)}, bf16[64,1024]{1,0:T(8,128)(2,1)S(1)}, u32[]{:S(2)}, u32[]{:S(2)}) %collective-permute-start) | collective-permute-done | bytes 131104 | tf_op jit(solution)/shard_map/ppermute | solution.py:327
  11.3 1.9 %collective-permute-start.1 = (bf16[64,1024]{1,0:T(8,128)(2,1)S(1)}, bf16[64,1024]{1,0:T(8,128)(2,1)S(1)}, u32[]{:S(2)}, u32[]{:S(2)}) collective-permute-start(bf16[64,1024]{1,0:T(8,128)(2,1)S(1)} %get-tuple-element.16), channel_id=1, source_target_pairs={{0,4},{4,0},{8,12},{12,8},{16,20},{20,16},{24,28},{28,24},{1,5},{5... | collective-permute-start | bytes 393224 | tf_op jit(solution)/shard_map/ppermute | solution.py:327
  13.2 0.0 collective-permute-start.2
  13.2 3.1 %collective-permute-start.5 = (bf16[64,1024]{1,0:T(8,128)(2,1)S(1)}, bf16[64,1024]{1,0:T(8,128)(2,1)S(1)}, u32[]{:S(2)}, u32[]{:S(2)}) collective-permute-start(bf16[64,1024]{1,0:T(8,128)(2,1)S(1)} %get-tuple-element.20), channel_id=1, source_target_pairs={{0,24},{4,28},{8,16},{12,20},{16,8},{20,12},{24,0},{28,4},{1,25},{... | collective-permute-start | bytes 393224 | tf_op jit(solution)/shard_map/ppermute | solution.py:327
  16.3 2.1 %collective-permute-done.3.refs_4_ = bf16[64,1024]{1,0:T(8,128)(2,1)S(1)} collective-permute-done((bf16[64,1024]{1,0:T(8,128)(2,1)S(1)}, bf16[64,1024]{1,0:T(8,128)(2,1)S(1)}, u32[]{:S(2)}, u32[]{:S(2)}) %collective-permute-start.3) | collective-permute-done | bytes 131104 | tf_op jit(solution)/shard_map/ppermute | solution.py:327
  18.4 3.4 %collective-permute-start.6 = (bf16[64,1024]{1,0:T(8,128)(2,1)S(1)}, bf16[64,1024]{1,0:T(8,128)(2,1)S(1)}, u32[]{:S(2)}, u32[]{:S(2)}) collective-permute-start(bf16[64,1024]{1,0:T(8,128)(2,1)S(1)} %get-tuple-element.21), channel_id=1, source_target_pairs={{0,28},{4,24},{8,20},{12,16},{16,12},{20,8},{24,4},{28,0},{1,29},{... | collective-permute-start | bytes 393224 | tf_op jit(solution)/shard_map/ppermute | solution.py:327
  21.8 0.0 copy-start.1
  21.8 4.5 %collective-permute-done.4.refs_5_ = bf16[64,1024]{1,0:T(8,128)(2,1)S(1)} collective-permute-done((bf16[64,1024]{1,0:T(8,128)(2,1)S(1)}, bf16[64,1024]{1,0:T(8,128)(2,1)S(1)}, u32[]{:S(2)}, u32[]{:S(2)}) %collective-permute-start.4) | collective-permute-done | bytes 131104 | tf_op jit(solution)/shard_map/ppermute | solution.py:327
  26.3 0.0 collective-permute-done.1.refs_1_
  26.3 0.0 collective-permute-done.2.refs_2_
  26.3 0.0 collective-permute-done.5.refs_6_
  26.3 0.0 collective-permute-done.6.refs_7_
  26.3 0.0 copy-done.1
  26.3 1.2 %shard_map.52 = (bf16[512,1024]{1,0:T(8,128)(2,1)S(1)}, f32[1152,128]{1,0:T(8,128)S(1)}) custom-call(s32[1]{0:T(128)} %bitcast.2.place_ref, bf16[64,1024]{1,0:T(8,128)(2,1)S(1)} %get-tuple-element.14.refs_0_, bf16[64,1024]{1,0:T(8,128)(2,1)S(1)} %collective-permute-done.1.refs_1_, bf16[64,1024]{1,0:T(8,128)(2,1)S(1)} %collective-permute-done.2.refs_2_, ...), custom_call_target="tpu_custom_call" | custom-call | tf_op jit(solution)/shard_map/pallas_call | solution.py:333
  27.6 0.1 collective-permute-start.7
  27.7 1.5 %collective-permute-done.7 = f32[576,128]{1,0:T(8,128)S(1)} collective-permute-done((f32[576,128]{1,0:T(8,128)S(1)}, f32[576,128]{1,0:T(8,128)S(1)}, u32[]{:S(2)}, u32[]{:S(2)}) %collective-permute-start.7) | collective-permute-done | bytes 294944 | tf_op jit(solution)/shard_map/ppermute | solution.py:300
  29.3 1.6 %collective-permute-start.8 = (f32[144,128]{1,0:T(8,128)S(1)}, f32[144,128]{1,0:T(8,128)S(1)}, u32[]{:S(2)}, u32[]{:S(2)}) collective-permute-start(f32[144,128]{1,0:T(8,128)S(1)} %get-tuple-element.26), channel_id=1, source_target_pairs={{0,2},{1,3},{2,0},{3,1},{4,6},{5,7},{6,4},{7,5},{8,10},{9,11},{10,... | collective-permute-start | bytes 221192 | tf_op jit(solution)/shard_map/ppermute | solution.py:300
  30.9 2.0 %collective-permute-start.10 = (f32[144,128]{1,0:T(8,128)S(1)}, f32[144,128]{1,0:T(8,128)S(1)}, u32[]{:S(2)}, u32[]{:S(2)}) collective-permute-start(f32[144,128]{1,0:T(8,128)S(1)} %get-tuple-element.27), channel_id=1, source_target_pairs={{0,6},{1,7},{2,4},{3,5},{4,2},{5,3},{6,0},{7,1},{8,14},{9,15},{10,... | collective-permute-start | bytes 221192 | tf_op jit(solution)/shard_map/ppermute | solution.py:300
  32.9 0.1 collective-permute-start.9
  32.9 0.8 %collective-permute-done.8 = f32[144,128]{1,0:T(8,128)S(1)} collective-permute-done((f32[144,128]{1,0:T(8,128)S(1)}, f32[144,128]{1,0:T(8,128)S(1)}, u32[]{:S(2)}, u32[]{:S(2)}) %collective-permute-start.8) | collective-permute-done | bytes 73760 | tf_op jit(solution)/shard_map/ppermute | solution.py:300
  33.7 2.6 %collective-permute-done.10 = f32[144,128]{1,0:T(8,128)S(1)} collective-permute-done((f32[144,128]{1,0:T(8,128)S(1)}, f32[144,128]{1,0:T(8,128)S(1)}, u32[]{:S(2)}, u32[]{:S(2)}) %collective-permute-start.10) | collective-permute-done | bytes 73760 | tf_op jit(solution)/shard_map/ppermute | solution.py:300
  36.3 0.9 %collective-permute-done.9 = f32[144,128]{1,0:T(8,128)S(1)} collective-permute-done((f32[144,128]{1,0:T(8,128)S(1)}, f32[144,128]{1,0:T(8,128)S(1)}, u32[]{:S(2)}, u32[]{:S(2)}) %collective-permute-start.9) | collective-permute-done | bytes 73760 | tf_op jit(solution)/shard_map/ppermute | solution.py:300
  37.3 5.4 %collective-permute-start.11 = (f32[144,128]{1,0:T(8,128)S(1)}, f32[144,128]{1,0:T(8,128)S(1)}, u32[]{:S(2)}, u32[]{:S(2)}) collective-permute-start(f32[144,128]{1,0:T(8,128)S(1)} %fusion.1), channel_id=1, source_target_pairs={{0,8},{1,9},{2,10},{3,11},{4,12},{5,13},{6,14},{7,15},{8,0},{9,1},... | collective-permute-start | bytes 221192 | tf_op jit(solution)/shard_map/ppermute | solution.py:300
  42.6 2.3 %collective-permute-done.11 = f32[144,128]{1,0:T(8,128)S(1)} collective-permute-done((f32[144,128]{1,0:T(8,128)S(1)}, f32[144,128]{1,0:T(8,128)S(1)}, u32[]{:S(2)}, u32[]{:S(2)}) %collective-permute-start.11) | collective-permute-done | bytes 73760 | tf_op jit(solution)/shard_map/ppermute | solution.py:300
  45.0 0.0 copy-start.2
  45.0 3.0 %collective-permute-start.12 = (f32[144,128]{1,0:T(8,128)S(1)}, f32[144,128]{1,0:T(8,128)S(1)}, u32[]{:S(2)}, u32[]{:S(2)}) collective-permute-start(f32[144,128]{1,0:T(8,128)S(1)} %add.63), channel_id=1, source_target_pairs={{0,16},{1,17},{2,18},{3,19},{4,20},{5,21},{6,22},{7,23},{8,24},{9,... | collective-permute-start | bytes 221192 | tf_op jit(solution)/shard_map/ppermute | solution.py:300
  48.0 2.3 %collective-permute-done.12 = f32[144,128]{1,0:T(8,128)S(1)} collective-permute-done((f32[144,128]{1,0:T(8,128)S(1)}, f32[144,128]{1,0:T(8,128)S(1)}, u32[]{:S(2)}, u32[]{:S(2)}) %collective-permute-start.12) | collective-permute-done | bytes 73760 | tf_op jit(solution)/shard_map/ppermute | solution.py:300
  50.4 2.1 %collective-permute-start.15 = (f32[144,128]{1,0:T(8,128)S(1)}, f32[144,128]{1,0:T(8,128)S(1)}, u32[]{:S(2)}, u32[]{:S(2)}) collective-permute-start(f32[144,128]{1,0:T(8,128)S(1)} %add.64.refs_1_), channel_id=1, source_target_pairs={{0,6},{1,7},{2,4},{3,5},{4,2},{5,3},{6,0},{7,1},{8,14},{9,15},{10,... | collective-permute-start | bytes 221192 | tf_op jit(solution)/shard_map/ppermute | solution.py:300
  52.5 0.9 %collective-permute-start.14 = (f32[144,128]{1,0:T(8,128)S(1)}, f32[144,128]{1,0:T(8,128)S(1)}, u32[]{:S(2)}, u32[]{:S(2)}) collective-permute-start(f32[144,128]{1,0:T(8,128)S(1)} %add.64.refs_1_), channel_id=1, source_target_pairs={{0,4},{1,5},{2,6},{3,7},{4,0},{5,1},{6,2},{7,3},{8,12},{9,13},{10,... | collective-permute-start | bytes 221192 | tf_op jit(solution)/shard_map/ppermute | solution.py:300
  53.4 0.6 collective-permute-start.13
  53.9 0.0 copy-done.2
  53.9 0.1 copy.5.refs_9_
  54.1 0.1 collective-permute-start.16
  54.2 1.6 %collective-permute-done.15.refs_4_ = f32[144,128]{1,0:T(8,128)S(1)} collective-permute-done((f32[144,128]{1,0:T(8,128)S(1)}, f32[144,128]{1,0:T(8,128)S(1)}, u32[]{:S(2)}, u32[]{:S(2)}) %collective-permute-start.15) | collective-permute-done | bytes 73760 | tf_op jit(solution)/shard_map/ppermute | solution.py:300
  55.7 0.0 collective-permute-start.19
  55.7 1.2 %collective-permute-done.14.refs_3_ = f32[144,128]{1,0:T(8,128)S(1)} collective-permute-done((f32[144,128]{1,0:T(8,128)S(1)}, f32[144,128]{1,0:T(8,128)S(1)}, u32[]{:S(2)}, u32[]{:S(2)}) %collective-permute-start.14) | collective-permute-done | bytes 73760 | tf_op jit(solution)/shard_map/ppermute | solution.py:300
  56.9 0.0 collective-permute-start.18
  56.9 0.9 %collective-permute-done.13.refs_2_ = f32[144,128]{1,0:T(8,128)S(1)} collective-permute-done((f32[144,128]{1,0:T(8,128)S(1)}, f32[144,128]{1,0:T(8,128)S(1)}, u32[]{:S(2)}, u32[]{:S(2)}) %collective-permute-start.13) | collective-permute-done | bytes 73760 | tf_op jit(solution)/shard_map/ppermute | solution.py:300
  57.7 0.0 collective-permute-start.17
  57.7 0.1 pad_add_fusion.refs_0_
  57.8 0.0 collective-permute-done.16.refs_5_
  57.8 0.0 collective-permute-done.19.refs_8_
  57.8 0.3 collective-permute-done.18.refs_7_
  58.1 0.9 %collective-permute-done.17.refs_6_ = f32[144,128]{1,0:T(8,128)S(1)} collective-permute-done((f32[144,128]{1,0:T(8,128)S(1)}, f32[144,128]{1,0:T(8,128)S(1)}, u32[]{:S(2)}, u32[]{:S(2)}) %collective-permute-start.17) | collective-permute-done | bytes 73760 | tf_op jit(solution)/shard_map/ppermute | solution.py:300
  59.0 14.9 %shard_map.53 = (bf16[64,1024]{1,0:T(8,128)(2,1)}, f32[512,512]{1,0:T(8,128)}) custom-call(s32[2]{0:T(128)S(1)} %pad_add_fusion.refs_0_, f32[144,128]{1,0:T(8,128)S(1)} %add.64.refs_1_, f32[144,128]{1,0:T(8,128)S(1)} %collective-permute-done.13.refs_2_, f32[144,128]{1,0:T(8,128)S(1)} %collective-permute-done.14.refs_3_, ...), custom_call_target="tpu_custom_call" | custom-call | tf_op jit(solution)/shard_map/pallas_call | solution.py:367
  (8 shorter events, 0.2 us)
Async XLA Ops:
  0.6 1.2 %copy-start = (bf16[64,1,8192]{2,0,1:T(8,128)(2,1)S(1)}, bf16[64,1,8192]{2,0,1:T(8,128)(2,1)}, u32[]{:S(2)}) copy-start(bf16[64,1,8192]{2,0,1:T(8,128)(2,1)} %param.3) | copy-start | bytes 3145732
  1.9 9.4 %collective-permute-start = (bf16[64,1024]{1,0:T(8,128)(2,1)S(1)}, bf16[64,1024]{1,0:T(8,128)(2,1)S(1)}, u32[]{:S(2)}, u32[]{:S(2)}) collective-permute-start(bf16[64,1024]{1,0:T(8,128)(2,1)S(1)} %get-tuple-element.15), channel_id=1, source_target_pairs={{0,12},{4,8},{8,4},{12,0},{16,28},{20,24},{24,20},{28,16},{1,13},{... | collective-permute-start | bytes 393224 | tf_op jit(solution)/shard_map/ppermute | solution.py:327
  5.9 12.5 %collective-permute-start.3 = (bf16[64,1024]{1,0:T(8,128)(2,1)S(1)}, bf16[64,1024]{1,0:T(8,128)(2,1)S(1)}, u32[]{:S(2)}, u32[]{:S(2)}) collective-permute-start(bf16[64,1024]{1,0:T(8,128)(2,1)S(1)} %get-tuple-element.18), channel_id=1, source_target_pairs={{0,16},{4,20},{8,24},{12,28},{16,0},{20,4},{24,8},{28,12},{1,17},{... | collective-permute-start | bytes 393224 | tf_op jit(solution)/shard_map/ppermute | solution.py:327
  8.5 17.8 %collective-permute-start.4 = (bf16[64,1024]{1,0:T(8,128)(2,1)S(1)}, bf16[64,1024]{1,0:T(8,128)(2,1)S(1)}, u32[]{:S(2)}, u32[]{:S(2)}) collective-permute-start(bf16[64,1024]{1,0:T(8,128)(2,1)S(1)} %get-tuple-element.19), channel_id=1, source_target_pairs={{0,20},{4,16},{8,28},{12,24},{16,4},{20,0},{24,12},{28,8},{1,21},{... | collective-permute-start | bytes 393224 | tf_op jit(solution)/shard_map/ppermute | solution.py:327
  11.3 15.0 %collective-permute-start.1 = (bf16[64,1024]{1,0:T(8,128)(2,1)S(1)}, bf16[64,1024]{1,0:T(8,128)(2,1)S(1)}, u32[]{:S(2)}, u32[]{:S(2)}) collective-permute-start(bf16[64,1024]{1,0:T(8,128)(2,1)S(1)} %get-tuple-element.16), channel_id=1, source_target_pairs={{0,4},{4,0},{8,12},{12,8},{16,20},{20,16},{24,28},{28,24},{1,5},{5... | collective-permute-start | bytes 393224 | tf_op jit(solution)/shard_map/ppermute | solution.py:327
  13.2 13.1 %collective-permute-start.2 = (bf16[64,1024]{1,0:T(8,128)(2,1)S(1)}, bf16[64,1024]{1,0:T(8,128)(2,1)S(1)}, u32[]{:S(2)}, u32[]{:S(2)}) collective-permute-start(bf16[64,1024]{1,0:T(8,128)(2,1)S(1)} %get-tuple-element.17), channel_id=1, source_target_pairs={{0,8},{4,12},{8,0},{12,4},{16,24},{20,28},{24,16},{28,20},{1,9},{5... | collective-permute-start | bytes 393224 | tf_op jit(solution)/shard_map/ppermute | solution.py:327
  13.2 13.1 %collective-permute-start.5 = (bf16[64,1024]{1,0:T(8,128)(2,1)S(1)}, bf16[64,1024]{1,0:T(8,128)(2,1)S(1)}, u32[]{:S(2)}, u32[]{:S(2)}) collective-permute-start(bf16[64,1024]{1,0:T(8,128)(2,1)S(1)} %get-tuple-element.20), channel_id=1, source_target_pairs={{0,24},{4,28},{8,16},{12,20},{16,8},{20,12},{24,0},{28,4},{1,25},{... | collective-permute-start | bytes 393224 | tf_op jit(solution)/shard_map/ppermute | solution.py:327
  18.4 7.9 %collective-permute-start.6 = (bf16[64,1024]{1,0:T(8,128)(2,1)S(1)}, bf16[64,1024]{1,0:T(8,128)(2,1)S(1)}, u32[]{:S(2)}, u32[]{:S(2)}) collective-permute-start(bf16[64,1024]{1,0:T(8,128)(2,1)S(1)} %get-tuple-element.21), channel_id=1, source_target_pairs={{0,28},{4,24},{8,20},{12,16},{16,12},{20,8},{24,4},{28,0},{1,29},{... | collective-permute-start | bytes 393224 | tf_op jit(solution)/shard_map/ppermute | solution.py:327
  21.8 4.5 %copy-start.1 = (bf16[1,1024]{1,0:T(2,128)(2,1)S(1)}, bf16[1,1024]{1,0:T(2,128)(2,1)}, u32[]{:S(2)}) copy-start(bf16[1,1024]{1,0:T(2,128)(2,1)} %refs_8_.1) | copy-start | bytes 6148
  27.6 1.6 %collective-permute-start.7 = (f32[576,128]{1,0:T(8,128)S(1)}, f32[576,128]{1,0:T(8,128)S(1)}, u32[]{:S(2)}, u32[]{:S(2)}) collective-permute-start(f32[576,128]{1,0:T(8,128)S(1)} %dynamic-slice_bitcast_fusion), channel_id=1, source_target_pairs={{0,1},{1,0},{2,3},{3,2},{4,5},{5,4},{6,7},{7,6},{8,9},{9,8},{10,11... | collective-permute-start | bytes 884744 | tf_op jit(solution)/shard_map/ppermute | solution.py:300
  29.3 4.4 %collective-permute-start.8 = (f32[144,128]{1,0:T(8,128)S(1)}, f32[144,128]{1,0:T(8,128)S(1)}, u32[]{:S(2)}, u32[]{:S(2)}) collective-permute-start(f32[144,128]{1,0:T(8,128)S(1)} %get-tuple-element.26), channel_id=1, source_target_pairs={{0,2},{1,3},{2,0},{3,1},{4,6},{5,7},{6,4},{7,5},{8,10},{9,11},{10,... | collective-permute-start | bytes 221192 | tf_op jit(solution)/shard_map/ppermute | solution.py:300
  30.9 5.4 %collective-permute-start.10 = (f32[144,128]{1,0:T(8,128)S(1)}, f32[144,128]{1,0:T(8,128)S(1)}, u32[]{:S(2)}, u32[]{:S(2)}) collective-permute-start(f32[144,128]{1,0:T(8,128)S(1)} %get-tuple-element.27), channel_id=1, source_target_pairs={{0,6},{1,7},{2,4},{3,5},{4,2},{5,3},{6,0},{7,1},{8,14},{9,15},{10,... | collective-permute-start | bytes 221192 | tf_op jit(solution)/shard_map/ppermute | solution.py:300
  32.9 4.4 %collective-permute-start.9 = (f32[144,128]{1,0:T(8,128)S(1)}, f32[144,128]{1,0:T(8,128)S(1)}, u32[]{:S(2)}, u32[]{:S(2)}) collective-permute-start(f32[144,128]{1,0:T(8,128)S(1)} %get-tuple-element.28), channel_id=1, source_target_pairs={{0,4},{1,5},{2,6},{3,7},{4,0},{5,1},{6,2},{7,3},{8,12},{9,13},{10,... | collective-permute-start | bytes 221192 | tf_op jit(solution)/shard_map/ppermute | solution.py:300
  37.3 7.7 %collective-permute-start.11 = (f32[144,128]{1,0:T(8,128)S(1)}, f32[144,128]{1,0:T(8,128)S(1)}, u32[]{:S(2)}, u32[]{:S(2)}) collective-permute-start(f32[144,128]{1,0:T(8,128)S(1)} %fusion.1), channel_id=1, source_target_pairs={{0,8},{1,9},{2,10},{3,11},{4,12},{5,13},{6,14},{7,15},{8,0},{9,1},... | collective-permute-start | bytes 221192 | tf_op jit(solution)/shard_map/ppermute | solution.py:300
  45.0 9.0 %copy-start.2 = (f32[512,64]{0,1:T(8,128)S(1)}, f32[512,64]{0,1:T(8,128)}, u32[]{:S(2)}) copy-start(f32[512,64]{0,1:T(8,128)} %param.5) | copy-start | bytes 393220
  45.0 5.4 %collective-permute-start.12 = (f32[144,128]{1,0:T(8,128)S(1)}, f32[144,128]{1,0:T(8,128)S(1)}, u32[]{:S(2)}, u32[]{:S(2)}) collective-permute-start(f32[144,128]{1,0:T(8,128)S(1)} %add.63), channel_id=1, source_target_pairs={{0,16},{1,17},{2,18},{3,19},{4,20},{5,21},{6,22},{7,23},{8,24},{9,... | collective-permute-start | bytes 221192 | tf_op jit(solution)/shard_map/ppermute | solution.py:300
  50.4 5.3 %collective-permute-start.15 = (f32[144,128]{1,0:T(8,128)S(1)}, f32[144,128]{1,0:T(8,128)S(1)}, u32[]{:S(2)}, u32[]{:S(2)}) collective-permute-start(f32[144,128]{1,0:T(8,128)S(1)} %add.64.refs_1_), channel_id=1, source_target_pairs={{0,6},{1,7},{2,4},{3,5},{4,2},{5,3},{6,0},{7,1},{8,14},{9,15},{10,... | collective-permute-start | bytes 221192 | tf_op jit(solution)/shard_map/ppermute | solution.py:300
  52.5 4.4 %collective-permute-start.14 = (f32[144,128]{1,0:T(8,128)S(1)}, f32[144,128]{1,0:T(8,128)S(1)}, u32[]{:S(2)}, u32[]{:S(2)}) collective-permute-start(f32[144,128]{1,0:T(8,128)S(1)} %add.64.refs_1_), channel_id=1, source_target_pairs={{0,4},{1,5},{2,6},{3,7},{4,0},{5,1},{6,2},{7,3},{8,12},{9,13},{10,... | collective-permute-start | bytes 221192 | tf_op jit(solution)/shard_map/ppermute | solution.py:300
  53.4 4.4 %collective-permute-start.13 = (f32[144,128]{1,0:T(8,128)S(1)}, f32[144,128]{1,0:T(8,128)S(1)}, u32[]{:S(2)}, u32[]{:S(2)}) collective-permute-start(f32[144,128]{1,0:T(8,128)S(1)} %add.64.refs_1_), channel_id=1, source_target_pairs={{0,2},{1,3},{2,0},{3,1},{4,6},{5,7},{6,4},{7,5},{8,10},{9,11},{10,... | collective-permute-start | bytes 221192 | tf_op jit(solution)/shard_map/ppermute | solution.py:300
  54.1 3.7 %collective-permute-start.16 = (f32[144,128]{1,0:T(8,128)S(1)}, f32[144,128]{1,0:T(8,128)S(1)}, u32[]{:S(2)}, u32[]{:S(2)}) collective-permute-start(f32[144,128]{1,0:T(8,128)S(1)} %add.64.refs_1_), channel_id=1, source_target_pairs={{0,1},{1,0},{2,3},{3,2},{4,5},{5,4},{6,7},{7,6},{8,9},{9,8},{10,11... | collective-permute-start | bytes 221192 | tf_op jit(solution)/shard_map/ppermute | solution.py:300
  55.7 2.1 %collective-permute-start.19 = (f32[144,128]{1,0:T(8,128)S(1)}, f32[144,128]{1,0:T(8,128)S(1)}, u32[]{:S(2)}, u32[]{:S(2)}) collective-permute-start(f32[144,128]{1,0:T(8,128)S(1)} %collective-permute-done.15.refs_4_), channel_id=1, source_target_pairs={{0,1},{1,0},{2,3},{3,2},{4,5},{5,4},{6,7},{7,6},{8,9},{9,8},{10,11... | collective-permute-start | bytes 221192 | tf_op jit(solution)/shard_map/ppermute | solution.py:300
  56.9 1.3 %collective-permute-start.18 = (f32[144,128]{1,0:T(8,128)S(1)}, f32[144,128]{1,0:T(8,128)S(1)}, u32[]{:S(2)}, u32[]{:S(2)}) collective-permute-start(f32[144,128]{1,0:T(8,128)S(1)} %collective-permute-done.14.refs_3_), channel_id=1, source_target_pairs={{0,1},{1,0},{2,3},{3,2},{4,5},{5,4},{6,7},{7,6},{8,9},{9,8},{10,11... | collective-permute-start | bytes 221192 | tf_op jit(solution)/shard_map/ppermute | solution.py:300
  57.7 1.3 %collective-permute-start.17 = (f32[144,128]{1,0:T(8,128)S(1)}, f32[144,128]{1,0:T(8,128)S(1)}, u32[]{:S(2)}, u32[]{:S(2)}) collective-permute-start(f32[144,128]{1,0:T(8,128)S(1)} %collective-permute-done.13.refs_2_), channel_id=1, source_target_pairs={{0,1},{1,0},{2,3},{3,2},{4,5},{5,4},{6,7},{7,6},{8,9},{9,8},{10,11... | collective-permute-start | bytes 221192 | tf_op jit(solution)/shard_map/ppermute | solution.py:300

commit v6 on v5

--- a/solution.py
+++ b/solution.py
@@ -124,9 +124,11 @@
     places, tails, _ = packing(count)
     kept = None
     for i in range(count):
-        rows = anomaly_ref[pl.ds(i * BLOCK, BLOCK), :]
-        rest = anomaly_ref[pl.ds(i * BLOCK, (count - i) * BLOCK), :]
-        part = lax.dot_general(rows, rest, LAST, preferred_element_type=jnp.float32)
+        if i % 2 == 0:
+            rows = anomaly_ref[pl.ds(i * BLOCK, 2 * BLOCK), :]
+            rest = anomaly_ref[pl.ds(i * BLOCK, (count - i) * BLOCK), :]
+            wide = lax.dot_general(rows, rest, LAST, preferred_element_type=jnp.float32)
+        part = wide[:BLOCK, :] if i % 2 == 0 else wide[BLOCK:, BLOCK:]
         gram_ref[pl.ds(places[i, i], HALF), :] = part[:HALF, :BLOCK]
         for j in range(i + 1, count):
             at = (j - i) * BLOCK

time: 74.2 us -> 73.9 us (level)
  no operation moved by 1% of the time
where the time goes in v6:
time: 73.9 us; the launch traced here: 73.7 us
  starting transfers between devices  31.1 us (42%)
  waiting for transfers between devices  24.2 us (33%)
  Pallas kernels  15.8 us (21%)
  local copies, waits for them, and re-layouts  1.4 us (2%)
  between operations  0.97 us (1%)
    ppermute x13, starting transfers between devices, swap(): return lax.ppermute(value, AXES, [(i, i ^ mask) for i in range(devices)])  15.8 us
    ppermute x7, starting transfers between devices, shards(): pieces[m] = lax.ppermute(piece, 'cells', route) if m else piece  15.3 us
    ppermute x13, waiting for transfers between devices, swap(): return lax.ppermute(value, AXES, [(i, i ^ mask) for i in range(devices)])  15.2 us
    pallas_call x1, Pallas kernels, shards(): pl.pallas_call(kernel, out_shape=(jax.ShapeDtypeStruct((modes, slab), jnp...  14.9 us
    ppermute x7, waiting for transfers between devices, shards(): pieces[m] = lax.ppermute(piece, 'cells', route) if m else piece  9.02 us
  transfers between devices with their start and end apart: 20, of which 14 were waited for; matrix products, arithmetic and copies ran while one was open for 0% of the time, Pallas kernels for 0%

profile of v6, /device:TPU:0, one launch (start us, length us, event | category | flops | bytes accessed | tf_op | source)
XLA Modules:
  0.0 73.7 jit_solution(9657012535929448252)
XLA Ops:
  0.6 0.0 copy-start
  0.6 1.2 %copy-done = bf16[64,1,8192]{2,0,1:T(8,128)(2,1)S(1)} copy-done((bf16[64,1,8192]{2,0,1:T(8,128)(2,1)S(1)}, bf16[64,1,8192]{2,0,1:T(8,128)(2,1)}, u32[]{:S(2)}) %copy-start) | copy-done | bytes 1048600
  1.9 4.0 %collective-permute-start = (bf16[64,1024]{1,0:T(8,128)(2,1)S(1)}, bf16[64,1024]{1,0:T(8,128)(2,1)S(1)}, u32[]{:S(2)}, u32[]{:S(2)}) collective-permute-start(bf16[64,1024]{1,0:T(8,128)(2,1)S(1)} %get-tuple-element.15), channel_id=1, source_target_pairs={{0,12},{4,8},{8,4},{12,0},{16,28},{20,24},{24,20},{28,16},{1,13},{... | collective-permute-start | bytes 393224 | tf_op jit(solution)/shard_map/ppermute | solution.py:329
  5.9 2.6 %collective-permute-start.3 = (bf16[64,1024]{1,0:T(8,128)(2,1)S(1)}, bf16[64,1024]{1,0:T(8,128)(2,1)S(1)}, u32[]{:S(2)}, u32[]{:S(2)}) collective-permute-start(bf16[64,1024]{1,0:T(8,128)(2,1)S(1)} %get-tuple-element.18), channel_id=1, source_target_pairs={{0,16},{4,20},{8,24},{12,28},{16,0},{20,4},{24,8},{28,12},{1,17},{... | collective-permute-start | bytes 393224 | tf_op jit(solution)/shard_map/ppermute | solution.py:329
  8.5 0.3 collective-permute-start.4
  8.8 2.5 %collective-permute-done.refs_0_.refs_3_ = bf16[64,1024]{1,0:T(8,128)(2,1)S(1)} collective-permute-done((bf16[64,1024]{1,0:T(8,128)(2,1)S(1)}, bf16[64,1024]{1,0:T(8,128)(2,1)S(1)}, u32[]{:S(2)}, u32[]{:S(2)}) %collective-permute-start) | collective-permute-done | bytes 131104 | tf_op jit(solution)/shard_map/ppermute | solution.py:329
  11.3 1.9 %collective-permute-start.1 = (bf16[64,1024]{1,0:T(8,128)(2,1)S(1)}, bf16[64,1024]{1,0:T(8,128)(2,1)S(1)}, u32[]{:S(2)}, u32[]{:S(2)}) collective-permute-start(bf16[64,1024]{1,0:T(8,128)(2,1)S(1)} %get-tuple-element.16), channel_id=1, source_target_pairs={{0,4},{4,0},{8,12},{12,8},{16,20},{20,16},{24,28},{28,24},{1,5},{5... | collective-permute-start | bytes 393224 | tf_op jit(solution)/shard_map/ppermute | solution.py:329
  13.2 0.0 collective-permute-start.2
  13.2 3.1 %collective-permute-start.5 = (bf16[64,1024]{1,0:T(8,128)(2,1)S(1)}, bf16[64,1024]{1,0:T(8,128)(2,1)S(1)}, u32[]{:S(2)}, u32[]{:S(2)}) collective-permute-start(bf16[64,1024]{1,0:T(8,128)(2,1)S(1)} %get-tuple-element.20), channel_id=1, source_target_pairs={{0,24},{4,28},{8,16},{12,20},{16,8},{20,12},{24,0},{28,4},{1,25},{... | collective-permute-start | bytes 393224 | tf_op jit(solution)/shard_map/ppermute | solution.py:329
  16.3 2.1 %collective-permute-done.3.refs_4_ = bf16[64,1024]{1,0:T(8,128)(2,1)S(1)} collective-permute-done((bf16[64,1024]{1,0:T(8,128)(2,1)S(1)}, bf16[64,1024]{1,0:T(8,128)(2,1)S(1)}, u32[]{:S(2)}, u32[]{:S(2)}) %collective-permute-start.3) | collective-permute-done | bytes 131104 | tf_op jit(solution)/shard_map/ppermute | solution.py:329
  18.4 3.4 %collective-permute-start.6 = (bf16[64,1024]{1,0:T(8,128)(2,1)S(1)}, bf16[64,1024]{1,0:T(8,128)(2,1)S(1)}, u32[]{:S(2)}, u32[]{:S(2)}) collective-permute-start(bf16[64,1024]{1,0:T(8,128)(2,1)S(1)} %get-tuple-element.21), channel_id=1, source_target_pairs={{0,28},{4,24},{8,20},{12,16},{16,12},{20,8},{24,4},{28,0},{1,29},{... | collective-permute-start | bytes 393224 | tf_op jit(solution)/shard_map/ppermute | solution.py:329
  21.8 0.0 copy-start.1
  21.8 4.5 %collective-permute-done.4.refs_5_ = bf16[64,1024]{1,0:T(8,128)(2,1)S(1)} collective-permute-done((bf16[64,1024]{1,0:T(8,128)(2,1)S(1)}, bf16[64,1024]{1,0:T(8,128)(2,1)S(1)}, u32[]{:S(2)}, u32[]{:S(2)}) %collective-permute-start.4) | collective-permute-done | bytes 131104 | tf_op jit(solution)/shard_map/ppermute | solution.py:329
  26.3 0.0 collective-permute-done.1.refs_1_
  26.3 0.0 collective-permute-done.2.refs_2_
  26.3 0.0 collective-permute-done.5.refs_6_
  26.3 0.0 collective-permute-done.6.refs_7_
  26.3 0.0 copy-done.1
  26.3 0.8 %shard_map.52 = (bf16[512,1024]{1,0:T(8,128)(2,1)S(1)}, f32[1152,128]{1,0:T(8,128)S(1)}) custom-call(s32[1]{0:T(128)} %bitcast.2.place_ref, bf16[64,1024]{1,0:T(8,128)(2,1)S(1)} %get-tuple-element.14.refs_0_, bf16[64,1024]{1,0:T(8,128)(2,1)S(1)} %collective-permute-done.1.refs_1_, bf16[64,1024]{1,0:T(8,128)(2,1)S(1)} %collective-permute-done.2.refs_2_, ...), custom_call_target="tpu_custom_call" | custom-call | tf_op jit(solution)/shard_map/pallas_call | solution.py:335
  27.2 0.1 collective-permute-start.7
  27.3 1.5 %collective-permute-done.7 = f32[576,128]{1,0:T(8,128)S(1)} collective-permute-done((f32[576,128]{1,0:T(8,128)S(1)}, f32[576,128]{1,0:T(8,128)S(1)}, u32[]{:S(2)}, u32[]{:S(2)}) %collective-permute-start.7) | collective-permute-done | bytes 294944 | tf_op jit(solution)/shard_map/ppermute | solution.py:302
  28.9 1.6 %collective-permute-start.8 = (f32[144,128]{1,0:T(8,128)S(1)}, f32[144,128]{1,0:T(8,128)S(1)}, u32[]{:S(2)}, u32[]{:S(2)}) collective-permute-start(f32[144,128]{1,0:T(8,128)S(1)} %get-tuple-element.26), channel_id=1, source_target_pairs={{0,2},{1,3},{2,0},{3,1},{4,6},{5,7},{6,4},{7,5},{8,10},{9,11},{10,... | collective-permute-start | bytes 221192 | tf_op jit(solution)/shard_map/ppermute | solution.py:302
  30.5 2.0 %collective-permute-start.10 = (f32[144,128]{1,0:T(8,128)S(1)}, f32[144,128]{1,0:T(8,128)S(1)}, u32[]{:S(2)}, u32[]{:S(2)}) collective-permute-start(f32[144,128]{1,0:T(8,128)S(1)} %get-tuple-element.27), channel_id=1, source_target_pairs={{0,6},{1,7},{2,4},{3,5},{4,2},{5,3},{6,0},{7,1},{8,14},{9,15},{10,... | collective-permute-start | bytes 221192 | tf_op jit(solution)/shard_map/ppermute | solution.py:302
  32.5 0.1 collective-permute-start.9
  32.6 0.8 %collective-permute-done.8 = f32[144,128]{1,0:T(8,128)S(1)} collective-permute-done((f32[144,128]{1,0:T(8,128)S(1)}, f32[144,128]{1,0:T(8,128)S(1)}, u32[]{:S(2)}, u32[]{:S(2)}) %collective-permute-start.8) | collective-permute-done | bytes 73760 | tf_op jit(solution)/shard_map/ppermute | solution.py:302
  33.3 2.6 %collective-permute-done.10 = f32[144,128]{1,0:T(8,128)S(1)} collective-permute-done((f32[144,128]{1,0:T(8,128)S(1)}, f32[144,128]{1,0:T(8,128)S(1)}, u32[]{:S(2)}, u32[]{:S(2)}) %collective-permute-start.10) | collective-permute-done | bytes 73760 | tf_op jit(solution)/shard_map/ppermute | solution.py:302
  35.9 0.9 %collective-permute-done.9 = f32[144,128]{1,0:T(8,128)S(1)} collective-permute-done((f32[144,128]{1,0:T(8,128)S(1)}, f32[144,128]{1,0:T(8,128)S(1)}, u32[]{:S(2)}, u32[]{:S(2)}) %collective-permute-start.9) | collective-permute-done | bytes 73760 | tf_op jit(solution)/shard_map/ppermute | solution.py:302
  36.9 5.4 %collective-permute-start.11 = (f32[144,128]{1,0:T(8,128)S(1)}, f32[144,128]{1,0:T(8,128)S(1)}, u32[]{:S(2)}, u32[]{:S(2)}) collective-permute-start(f32[144,128]{1,0:T(8,128)S(1)} %fusion.1), channel_id=1, source_target_pairs={{0,8},{1,9},{2,10},{3,11},{4,12},{5,13},{6,14},{7,15},{8,0},{9,1},... | collective-permute-start | bytes 221192 | tf_op jit(solution)/shard_map/ppermute | solution.py:302
  42.3 2.3 %collective-permute-done.11 = f32[144,128]{1,0:T(8,128)S(1)} collective-permute-done((f32[144,128]{1,0:T(8,128)S(1)}, f32[144,128]{1,0:T(8,128)S(1)}, u32[]{:S(2)}, u32[]{:S(2)}) %collective-permute-start.11) | collective-permute-done | bytes 73760 | tf_op jit(solution)/shard_map/ppermute | solution.py:302
  44.6 0.0 copy-start.2
  44.6 3.1 %collective-permute-start.12 = (f32[144,128]{1,0:T(8,128)S(1)}, f32[144,128]{1,0:T(8,128)S(1)}, u32[]{:S(2)}, u32[]{:S(2)}) collective-permute-start(f32[144,128]{1,0:T(8,128)S(1)} %add.63), channel_id=1, source_target_pairs={{0,16},{1,17},{2,18},{3,19},{4,20},{5,21},{6,22},{7,23},{8,24},{9,... | collective-permute-start | bytes 221192 | tf_op jit(solution)/shard_map/ppermute | solution.py:302
  47.7 2.3 %collective-permute-done.12 = f32[144,128]{1,0:T(8,128)S(1)} collective-permute-done((f32[144,128]{1,0:T(8,128)S(1)}, f32[144,128]{1,0:T(8,128)S(1)}, u32[]{:S(2)}, u32[]{:S(2)}) %collective-permute-start.12) | collective-permute-done | bytes 73760 | tf_op jit(solution)/shard_map/ppermute | solution.py:302
  50.0 2.1 %collective-permute-start.15 = (f32[144,128]{1,0:T(8,128)S(1)}, f32[144,128]{1,0:T(8,128)S(1)}, u32[]{:S(2)}, u32[]{:S(2)}) collective-permute-start(f32[144,128]{1,0:T(8,128)S(1)} %add.64.refs_1_), channel_id=1, source_target_pairs={{0,6},{1,7},{2,4},{3,5},{4,2},{5,3},{6,0},{7,1},{8,14},{9,15},{10,... | collective-permute-start | bytes 221192 | tf_op jit(solution)/shard_map/ppermute | solution.py:302
  52.2 0.9 %collective-permute-start.14 = (f32[144,128]{1,0:T(8,128)S(1)}, f32[144,128]{1,0:T(8,128)S(1)}, u32[]{:S(2)}, u32[]{:S(2)}) collective-permute-start(f32[144,128]{1,0:T(8,128)S(1)} %add.64.refs_1_), channel_id=1, source_target_pairs={{0,4},{1,5},{2,6},{3,7},{4,0},{5,1},{6,2},{7,3},{8,12},{9,13},{10,... | collective-permute-start | bytes 221192 | tf_op jit(solution)/shard_map/ppermute | solution.py:302
  53.0 0.6 collective-permute-start.13
  53.6 0.0 copy-done.2
  53.6 0.1 copy.5.refs_9_
  53.7 0.1 collective-permute-start.16
  53.8 1.6 %collective-permute-done.15.refs_4_ = f32[144,128]{1,0:T(8,128)S(1)} collective-permute-done((f32[144,128]{1,0:T(8,128)S(1)}, f32[144,128]{1,0:T(8,128)S(1)}, u32[]{:S(2)}, u32[]{:S(2)}) %collective-permute-start.15) | collective-permute-done | bytes 73760 | tf_op jit(solution)/shard_map/ppermute | solution.py:302
  55.4 0.0 collective-permute-start.19
  55.4 1.1 %collective-permute-done.14.refs_3_ = f32[144,128]{1,0:T(8,128)S(1)} collective-permute-done((f32[144,128]{1,0:T(8,128)S(1)}, f32[144,128]{1,0:T(8,128)S(1)}, u32[]{:S(2)}, u32[]{:S(2)}) %collective-permute-start.14) | collective-permute-done | bytes 73760 | tf_op jit(solution)/shard_map/ppermute | solution.py:302
  56.5 0.0 collective-permute-start.18
  56.5 0.9 %collective-permute-done.13.refs_2_ = f32[144,128]{1,0:T(8,128)S(1)} collective-permute-done((f32[144,128]{1,0:T(8,128)S(1)}, f32[144,128]{1,0:T(8,128)S(1)}, u32[]{:S(2)}, u32[]{:S(2)}) %collective-permute-start.13) | collective-permute-done | bytes 73760 | tf_op jit(solution)/shard_map/ppermute | solution.py:302
  57.4 0.0 collective-permute-start.17
  57.4 0.1 pad_add_fusion.refs_0_
  57.4 0.0 collective-permute-done.16.refs_5_
  57.4 0.0 collective-permute-done.19.refs_8_
  57.4 0.3 collective-permute-done.18.refs_7_
  57.8 0.9 %collective-permute-done.17.refs_6_ = f32[144,128]{1,0:T(8,128)S(1)} collective-permute-done((f32[144,128]{1,0:T(8,128)S(1)}, f32[144,128]{1,0:T(8,128)S(1)}, u32[]{:S(2)}, u32[]{:S(2)}) %collective-permute-start.17) | collective-permute-done | bytes 73760 | tf_op jit(solution)/shard_map/ppermute | solution.py:302
  58.6 14.9 %shard_map.53 = (bf16[64,1024]{1,0:T(8,128)(2,1)}, f32[512,512]{1,0:T(8,128)}) custom-call(s32[2]{0:T(128)S(1)} %pad_add_fusion.refs_0_, f32[144,128]{1,0:T(8,128)S(1)} %add.64.refs_1_, f32[144,128]{1,0:T(8,128)S(1)} %collective-permute-done.13.refs_2_, f32[144,128]{1,0:T(8,128)S(1)} %collective-permute-done.14.refs_3_, ...), custom_call_target="tpu_custom_call" | custom-call | tf_op jit(solution)/shard_map/pallas_call | solution.py:369
  (8 shorter events, 0.2 us)
Async XLA Ops:
  0.6 1.2 %copy-start = (bf16[64,1,8192]{2,0,1:T(8,128)(2,1)S(1)}, bf16[64,1,8192]{2,0,1:T(8,128)(2,1)}, u32[]{:S(2)}) copy-start(bf16[64,1,8192]{2,0,1:T(8,128)(2,1)} %param.3) | copy-start | bytes 3145732
  1.9 9.4 %collective-permute-start = (bf16[64,1024]{1,0:T(8,128)(2,1)S(1)}, bf16[64,1024]{1,0:T(8,128)(2,1)S(1)}, u32[]{:S(2)}, u32[]{:S(2)}) collective-permute-start(bf16[64,1024]{1,0:T(8,128)(2,1)S(1)} %get-tuple-element.15), channel_id=1, source_target_pairs={{0,12},{4,8},{8,4},{12,0},{16,28},{20,24},{24,20},{28,16},{1,13},{... | collective-permute-start | bytes 393224 | tf_op jit(solution)/shard_map/ppermute | solution.py:329
  5.9 12.5 %collective-permute-start.3 = (bf16[64,1024]{1,0:T(8,128)(2,1)S(1)}, bf16[64,1024]{1,0:T(8,128)(2,1)S(1)}, u32[]{:S(2)}, u32[]{:S(2)}) collective-permute-start(bf16[64,1024]{1,0:T(8,128)(2,1)S(1)} %get-tuple-element.18), channel_id=1, source_target_pairs={{0,16},{4,20},{8,24},{12,28},{16,0},{20,4},{24,8},{28,12},{1,17},{... | collective-permute-start | bytes 393224 | tf_op jit(solution)/shard_map/ppermute | solution.py:329
  8.5 17.8 %collective-permute-start.4 = (bf16[64,1024]{1,0:T(8,128)(2,1)S(1)}, bf16[64,1024]{1,0:T(8,128)(2,1)S(1)}, u32[]{:S(2)}, u32[]{:S(2)}) collective-permute-start(bf16[64,1024]{1,0:T(8,128)(2,1)S(1)} %get-tuple-element.19), channel_id=1, source_target_pairs={{0,20},{4,16},{8,28},{12,24},{16,4},{20,0},{24,12},{28,8},{1,21},{... | collective-permute-start | bytes 393224 | tf_op jit(solution)/shard_map/ppermute | solution.py:329
  11.3 15.0 %collective-permute-start.1 = (bf16[64,1024]{1,0:T(8,128)(2,1)S(1)}, bf16[64,1024]{1,0:T(8,128)(2,1)S(1)}, u32[]{:S(2)}, u32[]{:S(2)}) collective-permute-start(bf16[64,1024]{1,0:T(8,128)(2,1)S(1)} %get-tuple-element.16), channel_id=1, source_target_pairs={{0,4},{4,0},{8,12},{12,8},{16,20},{20,16},{24,28},{28,24},{1,5},{5... | collective-permute-start | bytes 393224 | tf_op jit(solution)/shard_map/ppermute | solution.py:329
  13.2 13.1 %collective-permute-start.2 = (bf16[64,1024]{1,0:T(8,128)(2,1)S(1)}, bf16[64,1024]{1,0:T(8,128)(2,1)S(1)}, u32[]{:S(2)}, u32[]{:S(2)}) collective-permute-start(bf16[64,1024]{1,0:T(8,128)(2,1)S(1)} %get-tuple-element.17), channel_id=1, source_target_pairs={{0,8},{4,12},{8,0},{12,4},{16,24},{20,28},{24,16},{28,20},{1,9},{5... | collective-permute-start | bytes 393224 | tf_op jit(solution)/shard_map/ppermute | solution.py:329
  13.2 13.1 %collective-permute-start.5 = (bf16[64,1024]{1,0:T(8,128)(2,1)S(1)}, bf16[64,1024]{1,0:T(8,128)(2,1)S(1)}, u32[]{:S(2)}, u32[]{:S(2)}) collective-permute-start(bf16[64,1024]{1,0:T(8,128)(2,1)S(1)} %get-tuple-element.20), channel_id=1, source_target_pairs={{0,24},{4,28},{8,16},{12,20},{16,8},{20,12},{24,0},{28,4},{1,25},{... | collective-permute-start | bytes 393224 | tf_op jit(solution)/shard_map/ppermute | solution.py:329
  18.4 7.9 %collective-permute-start.6 = (bf16[64,1024]{1,0:T(8,128)(2,1)S(1)}, bf16[64,1024]{1,0:T(8,128)(2,1)S(1)}, u32[]{:S(2)}, u32[]{:S(2)}) collective-permute-start(bf16[64,1024]{1,0:T(8,128)(2,1)S(1)} %get-tuple-element.21), channel_id=1, source_target_pairs={{0,28},{4,24},{8,20},{12,16},{16,12},{20,8},{24,4},{28,0},{1,29},{... | collective-permute-start | bytes 393224 | tf_op jit(solution)/shard_map/ppermute | solution.py:329
  21.8 4.5 %copy-start.1 = (bf16[1,1024]{1,0:T(2,128)(2,1)S(1)}, bf16[1,1024]{1,0:T(2,128)(2,1)}, u32[]{:S(2)}) copy-start(bf16[1,1024]{1,0:T(2,128)(2,1)} %refs_8_.1) | copy-start | bytes 6148
  27.2 1.6 %collective-permute-start.7 = (f32[576,128]{1,0:T(8,128)S(1)}, f32[576,128]{1,0:T(8,128)S(1)}, u32[]{:S(2)}, u32[]{:S(2)}) collective-permute-start(f32[576,128]{1,0:T(8,128)S(1)} %dynamic-slice_bitcast_fusion), channel_id=1, source_target_pairs={{0,1},{1,0},{2,3},{3,2},{4,5},{5,4},{6,7},{7,6},{8,9},{9,8},{10,11... | collective-permute-start | bytes 884744 | tf_op jit(solution)/shard_map/ppermute | solution.py:302
  28.9 4.4 %collective-permute-start.8 = (f32[144,128]{1,0:T(8,128)S(1)}, f32[144,128]{1,0:T(8,128)S(1)}, u32[]{:S(2)}, u32[]{:S(2)}) collective-permute-start(f32[144,128]{1,0:T(8,128)S(1)} %get-tuple-element.26), channel_id=1, source_target_pairs={{0,2},{1,3},{2,0},{3,1},{4,6},{5,7},{6,4},{7,5},{8,10},{9,11},{10,... | collective-permute-start | bytes 221192 | tf_op jit(solution)/shard_map/ppermute | solution.py:302
  30.5 5.4 %collective-permute-start.10 = (f32[144,128]{1,0:T(8,128)S(1)}, f32[144,128]{1,0:T(8,128)S(1)}, u32[]{:S(2)}, u32[]{:S(2)}) collective-permute-start(f32[144,128]{1,0:T(8,128)S(1)} %get-tuple-element.27), channel_id=1, source_target_pairs={{0,6},{1,7},{2,4},{3,5},{4,2},{5,3},{6,0},{7,1},{8,14},{9,15},{10,... | collective-permute-start | bytes 221192 | tf_op jit(solution)/shard_map/ppermute | solution.py:302
  32.5 4.4 %collective-permute-start.9 = (f32[144,128]{1,0:T(8,128)S(1)}, f32[144,128]{1,0:T(8,128)S(1)}, u32[]{:S(2)}, u32[]{:S(2)}) collective-permute-start(f32[144,128]{1,0:T(8,128)S(1)} %get-tuple-element.28), channel_id=1, source_target_pairs={{0,4},{1,5},{2,6},{3,7},{4,0},{5,1},{6,2},{7,3},{8,12},{9,13},{10,... | collective-permute-start | bytes 221192 | tf_op jit(solution)/shard_map/ppermute | solution.py:302
  36.9 7.7 %collective-permute-start.11 = (f32[144,128]{1,0:T(8,128)S(1)}, f32[144,128]{1,0:T(8,128)S(1)}, u32[]{:S(2)}, u32[]{:S(2)}) collective-permute-start(f32[144,128]{1,0:T(8,128)S(1)} %fusion.1), channel_id=1, source_target_pairs={{0,8},{1,9},{2,10},{3,11},{4,12},{5,13},{6,14},{7,15},{8,0},{9,1},... | collective-permute-start | bytes 221192 | tf_op jit(solution)/shard_map/ppermute | solution.py:302
  44.6 9.0 %copy-start.2 = (f32[512,64]{0,1:T(8,128)S(1)}, f32[512,64]{0,1:T(8,128)}, u32[]{:S(2)}) copy-start(f32[512,64]{0,1:T(8,128)} %param.5) | copy-start | bytes 393220
  44.6 5.4 %collective-permute-start.12 = (f32[144,128]{1,0:T(8,128)S(1)}, f32[144,128]{1,0:T(8,128)S(1)}, u32[]{:S(2)}, u32[]{:S(2)}) collective-permute-start(f32[144,128]{1,0:T(8,128)S(1)} %add.63), channel_id=1, source_target_pairs={{0,16},{1,17},{2,18},{3,19},{4,20},{5,21},{6,22},{7,23},{8,24},{9,... | collective-permute-start | bytes 221192 | tf_op jit(solution)/shard_map/ppermute | solution.py:302
  50.0 5.3 %collective-permute-start.15 = (f32[144,128]{1,0:T(8,128)S(1)}, f32[144,128]{1,0:T(8,128)S(1)}, u32[]{:S(2)}, u32[]{:S(2)}) collective-permute-start(f32[144,128]{1,0:T(8,128)S(1)} %add.64.refs_1_), channel_id=1, source_target_pairs={{0,6},{1,7},{2,4},{3,5},{4,2},{5,3},{6,0},{7,1},{8,14},{9,15},{10,... | collective-permute-start | bytes 221192 | tf_op jit(solution)/shard_map/ppermute | solution.py:302
  52.2 4.4 %collective-permute-start.14 = (f32[144,128]{1,0:T(8,128)S(1)}, f32[144,128]{1,0:T(8,128)S(1)}, u32[]{:S(2)}, u32[]{:S(2)}) collective-permute-start(f32[144,128]{1,0:T(8,128)S(1)} %add.64.refs_1_), channel_id=1, source_target_pairs={{0,4},{1,5},{2,6},{3,7},{4,0},{5,1},{6,2},{7,3},{8,12},{9,13},{10,... | collective-permute-start | bytes 221192 | tf_op jit(solution)/shard_map/ppermute | solution.py:302
  53.0 4.4 %collective-permute-start.13 = (f32[144,128]{1,0:T(8,128)S(1)}, f32[144,128]{1,0:T(8,128)S(1)}, u32[]{:S(2)}, u32[]{:S(2)}) collective-permute-start(f32[144,128]{1,0:T(8,128)S(1)} %add.64.refs_1_), channel_id=1, source_target_pairs={{0,2},{1,3},{2,0},{3,1},{4,6},{5,7},{6,4},{7,5},{8,10},{9,11},{10,... | collective-permute-start | bytes 221192 | tf_op jit(solution)/shard_map/ppermute | solution.py:302
  53.7 3.7 %collective-permute-start.16 = (f32[144,128]{1,0:T(8,128)S(1)}, f32[144,128]{1,0:T(8,128)S(1)}, u32[]{:S(2)}, u32[]{:S(2)}) collective-permute-start(f32[144,128]{1,0:T(8,128)S(1)} %add.64.refs_1_), channel_id=1, source_target_pairs={{0,1},{1,0},{2,3},{3,2},{4,5},{5,4},{6,7},{7,6},{8,9},{9,8},{10,11... | collective-permute-start | bytes 221192 | tf_op jit(solution)/shard_map/ppermute | solution.py:302
  55.4 2.1 %collective-permute-start.19 = (f32[144,128]{1,0:T(8,128)S(1)}, f32[144,128]{1,0:T(8,128)S(1)}, u32[]{:S(2)}, u32[]{:S(2)}) collective-permute-start(f32[144,128]{1,0:T(8,128)S(1)} %collective-permute-done.15.refs_4_), channel_id=1, source_target_pairs={{0,1},{1,0},{2,3},{3,2},{4,5},{5,4},{6,7},{7,6},{8,9},{9,8},{10,11... | collective-permute-start | bytes 221192 | tf_op jit(solution)/shard_map/ppermute | solution.py:302
  56.5 1.3 %collective-permute-start.18 = (f32[144,128]{1,0:T(8,128)S(1)}, f32[144,128]{1,0:T(8,128)S(1)}, u32[]{:S(2)}, u32[]{:S(2)}) collective-permute-start(f32[144,128]{1,0:T(8,128)S(1)} %collective-permute-done.14.refs_3_), channel_id=1, source_target_pairs={{0,1},{1,0},{2,3},{3,2},{4,5},{5,4},{6,7},{7,6},{8,9},{9,8},{10,11... | collective-permute-start | bytes 221192 | tf_op jit(solution)/shard_map/ppermute | solution.py:302
  57.4 1.3 %collective-permute-start.17 = (f32[144,128]{1,0:T(8,128)S(1)}, f32[144,128]{1,0:T(8,128)S(1)}, u32[]{:S(2)}, u32[]{:S(2)}) collective-permute-start(f32[144,128]{1,0:T(8,128)S(1)} %collective-permute-done.13.refs_2_), channel_id=1, source_target_pairs={{0,1},{1,0},{2,3},{3,2},{4,5},{5,4},{6,7},{7,6},{8,9},{9,8},{10,11... | collective-permute-start | bytes 221192 | tf_op jit(solution)/shard_map/ppermute | solution.py:302

commit v7 on v6

--- a/solution.py
+++ b/solution.py
@@ -243,7 +243,7 @@
 
     def mix(k, j):
         def run():
-            part = dot(design_ref[span(k), :], inv_ref[span(k), span(j)], FIRST)
+            part = dot(design_ref[:, span(k)], inv_ref[span(k), span(j)])
             mix_ref[:, span(j)] = part if j == k else mix_ref[:, span(j)] + part
 
         return run
@@ -383,7 +383,7 @@
             pltpu.SemaphoreType.DMA((blocks,)),
         ],
         compiler_params=pltpu.CompilerParams(vmem_limit_bytes=32 * 2**20),
-    )(jnp.stack([half, quarter]).astype(jnp.int32), *mine, *other, design, anomaly)
+    )(jnp.stack([half, quarter]).astype(jnp.int32), *mine, *other, design.T, anomaly)
     return (basis.reshape(modes, 1, slab), factor)
 
 

time: 73.9 us -> 73.9 us (level)
  no operation moved by 1% of the time
where the time goes in v7:
time: 73.9 us; the launch traced here: 73.7 us
  starting transfers between devices  31.1 us (42%)
  waiting for transfers between devices  24.4 us (33%)
  Pallas kernels  15.8 us (21%)
  local copies, waits for them, and re-layouts  1.28 us (2%)
  between operations  0.95 us (1%)
    ppermute x13, starting transfers between devices, swap(): return lax.ppermute(value, AXES, [(i, i ^ mask) for i in range(devices)])  15.7 us
    ppermute x13, waiting for transfers between devices, swap(): return lax.ppermute(value, AXES, [(i, i ^ mask) for i in range(devices)])  15.4 us
    ppermute x7, starting transfers between devices, shards(): pieces[m] = lax.ppermute(piece, 'cells', route) if m else piece  15.3 us
    pallas_call x1, Pallas kernels, shards(): pl.pallas_call(kernel, out_shape=(jax.ShapeDtypeStruct((modes, slab), jnp...  14.9 us
    ppermute x7, waiting for transfers between devices, shards(): pieces[m] = lax.ppermute(piece, 'cells', route) if m else piece  9.02 us
  transfers between devices with their start and end apart: 20, of which 14 were waited for; matrix products, arithmetic and copies ran while one was open for 0% of the time, Pallas kernels for 0%

profile of v7, /device:TPU:0, one launch (start us, length us, event | category | flops | bytes accessed | tf_op | source)
XLA Modules:
  0.0 73.7 jit_solution(12359112420168291968)
XLA Ops:
  0.6 0.0 copy-start
  0.6 1.2 %copy-done = bf16[64,1,8192]{2,0,1:T(8,128)(2,1)S(1)} copy-done((bf16[64,1,8192]{2,0,1:T(8,128)(2,1)S(1)}, bf16[64,1,8192]{2,0,1:T(8,128)(2,1)}, u32[]{:S(2)}) %copy-start) | copy-done | bytes 1048600
  1.9 4.0 %collective-permute-start = (bf16[64,1024]{1,0:T(8,128)(2,1)S(1)}, bf16[64,1024]{1,0:T(8,128)(2,1)S(1)}, u32[]{:S(2)}, u32[]{:S(2)}) collective-permute-start(bf16[64,1024]{1,0:T(8,128)(2,1)S(1)} %get-tuple-element.15), channel_id=1, source_target_pairs={{0,12},{4,8},{8,4},{12,0},{16,28},{20,24},{24,20},{28,16},{1,13},{... | collective-permute-start | bytes 393224 | tf_op jit(solution)/shard_map/ppermute | solution.py:329
  5.9 2.6 %collective-permute-start.3 = (bf16[64,1024]{1,0:T(8,128)(2,1)S(1)}, bf16[64,1024]{1,0:T(8,128)(2,1)S(1)}, u32[]{:S(2)}, u32[]{:S(2)}) collective-permute-start(bf16[64,1024]{1,0:T(8,128)(2,1)S(1)} %get-tuple-element.18), channel_id=1, source_target_pairs={{0,16},{4,20},{8,24},{12,28},{16,0},{20,4},{24,8},{28,12},{1,17},{... | collective-permute-start | bytes 393224 | tf_op jit(solution)/shard_map/ppermute | solution.py:329
  8.5 0.3 collective-permute-start.4
  8.8 2.5 %collective-permute-done.refs_0_.refs_3_ = bf16[64,1024]{1,0:T(8,128)(2,1)S(1)} collective-permute-done((bf16[64,1024]{1,0:T(8,128)(2,1)S(1)}, bf16[64,1024]{1,0:T(8,128)(2,1)S(1)}, u32[]{:S(2)}, u32[]{:S(2)}) %collective-permute-start) | collective-permute-done | bytes 131104 | tf_op jit(solution)/shard_map/ppermute | solution.py:329
  11.3 1.9 %collective-permute-start.1 = (bf16[64,1024]{1,0:T(8,128)(2,1)S(1)}, bf16[64,1024]{1,0:T(8,128)(2,1)S(1)}, u32[]{:S(2)}, u32[]{:S(2)}) collective-permute-start(bf16[64,1024]{1,0:T(8,128)(2,1)S(1)} %get-tuple-element.16), channel_id=1, source_target_pairs={{0,4},{4,0},{8,12},{12,8},{16,20},{20,16},{24,28},{28,24},{1,5},{5... | collective-permute-start | bytes 393224 | tf_op jit(solution)/shard_map/ppermute | solution.py:329
  13.2 0.0 collective-permute-start.2
  13.2 3.1 %collective-permute-start.5 = (bf16[64,1024]{1,0:T(8,128)(2,1)S(1)}, bf16[64,1024]{1,0:T(8,128)(2,1)S(1)}, u32[]{:S(2)}, u32[]{:S(2)}) collective-permute-start(bf16[64,1024]{1,0:T(8,128)(2,1)S(1)} %get-tuple-element.20), channel_id=1, source_target_pairs={{0,24},{4,28},{8,16},{12,20},{16,8},{20,12},{24,0},{28,4},{1,25},{... | collective-permute-start | bytes 393224 | tf_op jit(solution)/shard_map/ppermute | solution.py:329
  16.3 2.1 %collective-permute-done.3.refs_4_ = bf16[64,1024]{1,0:T(8,128)(2,1)S(1)} collective-permute-done((bf16[64,1024]{1,0:T(8,128)(2,1)S(1)}, bf16[64,1024]{1,0:T(8,128)(2,1)S(1)}, u32[]{:S(2)}, u32[]{:S(2)}) %collective-permute-start.3) | collective-permute-done | bytes 131104 | tf_op jit(solution)/shard_map/ppermute | solution.py:329
  18.4 3.4 %collective-permute-start.6 = (bf16[64,1024]{1,0:T(8,128)(2,1)S(1)}, bf16[64,1024]{1,0:T(8,128)(2,1)S(1)}, u32[]{:S(2)}, u32[]{:S(2)}) collective-permute-start(bf16[64,1024]{1,0:T(8,128)(2,1)S(1)} %get-tuple-element.21), channel_id=1, source_target_pairs={{0,28},{4,24},{8,20},{12,16},{16,12},{20,8},{24,4},{28,0},{1,29},{... | collective-permute-start | bytes 393224 | tf_op jit(solution)/shard_map/ppermute | solution.py:329
  21.8 0.0 copy-start.2
  21.8 4.5 %collective-permute-done.4.refs_5_ = bf16[64,1024]{1,0:T(8,128)(2,1)S(1)} collective-permute-done((bf16[64,1024]{1,0:T(8,128)(2,1)S(1)}, bf16[64,1024]{1,0:T(8,128)(2,1)S(1)}, u32[]{:S(2)}, u32[]{:S(2)}) %collective-permute-start.4) | collective-permute-done | bytes 131104 | tf_op jit(solution)/shard_map/ppermute | solution.py:329
  26.3 0.0 collective-permute-done.1.refs_1_
  26.3 0.0 collective-permute-done.2.refs_2_
  26.3 0.0 collective-permute-done.5.refs_6_
  26.3 0.0 collective-permute-done.6.refs_7_
  26.3 0.0 copy-done.2
  26.3 0.8 %shard_map.52 = (bf16[512,1024]{1,0:T(8,128)(2,1)S(1)}, f32[1152,128]{1,0:T(8,128)S(1)}) custom-call(s32[1]{0:T(128)} %bitcast.2.place_ref, bf16[64,1024]{1,0:T(8,128)(2,1)S(1)} %get-tuple-element.14.refs_0_, bf16[64,1024]{1,0:T(8,128)(2,1)S(1)} %collective-permute-done.1.refs_1_, bf16[64,1024]{1,0:T(8,128)(2,1)S(1)} %collective-permute-done.2.refs_2_, ...), custom_call_target="tpu_custom_call" | custom-call | tf_op jit(solution)/shard_map/pallas_call | solution.py:335
  27.2 0.1 collective-permute-start.7
  27.3 1.5 %collective-permute-done.7 = f32[576,128]{1,0:T(8,128)S(1)} collective-permute-done((f32[576,128]{1,0:T(8,128)S(1)}, f32[576,128]{1,0:T(8,128)S(1)}, u32[]{:S(2)}, u32[]{:S(2)}) %collective-permute-start.7) | collective-permute-done | bytes 294944 | tf_op jit(solution)/shard_map/ppermute | solution.py:302
  28.9 1.6 %collective-permute-start.8 = (f32[144,128]{1,0:T(8,128)S(1)}, f32[144,128]{1,0:T(8,128)S(1)}, u32[]{:S(2)}, u32[]{:S(2)}) collective-permute-start(f32[144,128]{1,0:T(8,128)S(1)} %get-tuple-element.26), channel_id=1, source_target_pairs={{0,2},{1,3},{2,0},{3,1},{4,6},{5,7},{6,4},{7,5},{8,10},{9,11},{10,... | collective-permute-start | bytes 221192 | tf_op jit(solution)/shard_map/ppermute | solution.py:302
  30.5 2.0 %collective-permute-start.10 = (f32[144,128]{1,0:T(8,128)S(1)}, f32[144,128]{1,0:T(8,128)S(1)}, u32[]{:S(2)}, u32[]{:S(2)}) collective-permute-start(f32[144,128]{1,0:T(8,128)S(1)} %get-tuple-element.27), channel_id=1, source_target_pairs={{0,6},{1,7},{2,4},{3,5},{4,2},{5,3},{6,0},{7,1},{8,14},{9,15},{10,... | collective-permute-start | bytes 221192 | tf_op jit(solution)/shard_map/ppermute | solution.py:302
  32.5 0.1 collective-permute-start.9
  32.6 0.8 %collective-permute-done.8 = f32[144,128]{1,0:T(8,128)S(1)} collective-permute-done((f32[144,128]{1,0:T(8,128)S(1)}, f32[144,128]{1,0:T(8,128)S(1)}, u32[]{:S(2)}, u32[]{:S(2)}) %collective-permute-start.8) | collective-permute-done | bytes 73760 | tf_op jit(solution)/shard_map/ppermute | solution.py:302
  33.3 2.6 %collective-permute-done.10 = f32[144,128]{1,0:T(8,128)S(1)} collective-permute-done((f32[144,128]{1,0:T(8,128)S(1)}, f32[144,128]{1,0:T(8,128)S(1)}, u32[]{:S(2)}, u32[]{:S(2)}) %collective-permute-start.10) | collective-permute-done | bytes 73760 | tf_op jit(solution)/shard_map/ppermute | solution.py:302
  35.9 0.9 %collective-permute-done.9 = f32[144,128]{1,0:T(8,128)S(1)} collective-permute-done((f32[144,128]{1,0:T(8,128)S(1)}, f32[144,128]{1,0:T(8,128)S(1)}, u32[]{:S(2)}, u32[]{:S(2)}) %collective-permute-start.9) | collective-permute-done | bytes 73760 | tf_op jit(solution)/shard_map/ppermute | solution.py:302
  36.9 5.4 %collective-permute-start.11 = (f32[144,128]{1,0:T(8,128)S(1)}, f32[144,128]{1,0:T(8,128)S(1)}, u32[]{:S(2)}, u32[]{:S(2)}) collective-permute-start(f32[144,128]{1,0:T(8,128)S(1)} %fusion.1), channel_id=1, source_target_pairs={{0,8},{1,9},{2,10},{3,11},{4,12},{5,13},{6,14},{7,15},{8,0},{9,1},... | collective-permute-start | bytes 221192 | tf_op jit(solution)/shard_map/ppermute | solution.py:302
  42.3 2.3 %collective-permute-done.11 = f32[144,128]{1,0:T(8,128)S(1)} collective-permute-done((f32[144,128]{1,0:T(8,128)S(1)}, f32[144,128]{1,0:T(8,128)S(1)}, u32[]{:S(2)}, u32[]{:S(2)}) %collective-permute-start.11) | collective-permute-done | bytes 73760 | tf_op jit(solution)/shard_map/ppermute | solution.py:302
  44.6 0.0 copy-start.1
  44.6 3.1 %collective-permute-start.12 = (f32[144,128]{1,0:T(8,128)S(1)}, f32[144,128]{1,0:T(8,128)S(1)}, u32[]{:S(2)}, u32[]{:S(2)}) collective-permute-start(f32[144,128]{1,0:T(8,128)S(1)} %add.63), channel_id=1, source_target_pairs={{0,16},{1,17},{2,18},{3,19},{4,20},{5,21},{6,22},{7,23},{8,24},{9,... | collective-permute-start | bytes 221192 | tf_op jit(solution)/shard_map/ppermute | solution.py:302
  47.7 2.3 %collective-permute-done.12 = f32[144,128]{1,0:T(8,128)S(1)} collective-permute-done((f32[144,128]{1,0:T(8,128)S(1)}, f32[144,128]{1,0:T(8,128)S(1)}, u32[]{:S(2)}, u32[]{:S(2)}) %collective-permute-start.12) | collective-permute-done | bytes 73760 | tf_op jit(solution)/shard_map/ppermute | solution.py:302
  50.0 2.1 %collective-permute-start.15 = (f32[144,128]{1,0:T(8,128)S(1)}, f32[144,128]{1,0:T(8,128)S(1)}, u32[]{:S(2)}, u32[]{:S(2)}) collective-permute-start(f32[144,128]{1,0:T(8,128)S(1)} %add.64.refs_1_), channel_id=1, source_target_pairs={{0,6},{1,7},{2,4},{3,5},{4,2},{5,3},{6,0},{7,1},{8,14},{9,15},{10,... | collective-permute-start | bytes 221192 | tf_op jit(solution)/shard_map/ppermute | solution.py:302
  52.1 0.9 %collective-permute-start.14 = (f32[144,128]{1,0:T(8,128)S(1)}, f32[144,128]{1,0:T(8,128)S(1)}, u32[]{:S(2)}, u32[]{:S(2)}) collective-permute-start(f32[144,128]{1,0:T(8,128)S(1)} %add.64.refs_1_), channel_id=1, source_target_pairs={{0,4},{1,5},{2,6},{3,7},{4,0},{5,1},{6,2},{7,3},{8,12},{9,13},{10,... | collective-permute-start | bytes 221192 | tf_op jit(solution)/shard_map/ppermute | solution.py:302
  53.0 0.6 collective-permute-start.13
  53.6 0.0 collective-permute-start.16
  53.6 1.8 %collective-permute-done.15.refs_4_ = f32[144,128]{1,0:T(8,128)S(1)} collective-permute-done((f32[144,128]{1,0:T(8,128)S(1)}, f32[144,128]{1,0:T(8,128)S(1)}, u32[]{:S(2)}, u32[]{:S(2)}) %collective-permute-start.15) | collective-permute-done | bytes 73760 | tf_op jit(solution)/shard_map/ppermute | solution.py:302
  55.3 0.0 collective-permute-start.19
  55.4 1.1 %collective-permute-done.14.refs_3_ = f32[144,128]{1,0:T(8,128)S(1)} collective-permute-done((f32[144,128]{1,0:T(8,128)S(1)}, f32[144,128]{1,0:T(8,128)S(1)}, u32[]{:S(2)}, u32[]{:S(2)}) %collective-permute-start.14) | collective-permute-done | bytes 73760 | tf_op jit(solution)/shard_map/ppermute | solution.py:302
  56.5 0.0 collective-permute-start.18
  56.5 0.9 %collective-permute-done.13.refs_2_ = f32[144,128]{1,0:T(8,128)S(1)} collective-permute-done((f32[144,128]{1,0:T(8,128)S(1)}, f32[144,128]{1,0:T(8,128)S(1)}, u32[]{:S(2)}, u32[]{:S(2)}) %collective-permute-start.13) | collective-permute-done | bytes 73760 | tf_op jit(solution)/shard_map/ppermute | solution.py:302
  57.4 0.0 collective-permute-start.17
  57.4 0.1 pad_add_fusion.refs_0_
  57.4 0.0 collective-permute-done.16.refs_5_
  57.4 0.0 collective-permute-done.19.refs_8_
  57.4 0.3 collective-permute-done.18.refs_7_
  57.8 0.9 %collective-permute-done.17.refs_6_ = f32[144,128]{1,0:T(8,128)S(1)} collective-permute-done((f32[144,128]{1,0:T(8,128)S(1)}, f32[144,128]{1,0:T(8,128)S(1)}, u32[]{:S(2)}, u32[]{:S(2)}) %collective-permute-start.17) | collective-permute-done | bytes 73760 | tf_op jit(solution)/shard_map/ppermute | solution.py:302
  58.6 0.0 copy-done.1
  58.6 14.9 %shard_map.53 = (bf16[64,1024]{1,0:T(8,128)(2,1)}, f32[512,512]{1,0:T(8,128)}) custom-call(s32[2]{0:T(128)S(1)} %pad_add_fusion.refs_0_, f32[144,128]{1,0:T(8,128)S(1)} %add.64.refs_1_, f32[144,128]{1,0:T(8,128)S(1)} %collective-permute-done.13.refs_2_, f32[144,128]{1,0:T(8,128)S(1)} %collective-permute-done.14.refs_3_, ...), custom_call_target="tpu_custom_call" | custom-call | tf_op jit(solution)/shard_map/pallas_call | solution.py:369
  (8 shorter events, 0.2 us)
Async XLA Ops:
  0.6 1.2 %copy-start = (bf16[64,1,8192]{2,0,1:T(8,128)(2,1)S(1)}, bf16[64,1,8192]{2,0,1:T(8,128)(2,1)}, u32[]{:S(2)}) copy-start(bf16[64,1,8192]{2,0,1:T(8,128)(2,1)} %param.3) | copy-start | bytes 3145732
  1.9 9.4 %collective-permute-start = (bf16[64,1024]{1,0:T(8,128)(2,1)S(1)}, bf16[64,1024]{1,0:T(8,128)(2,1)S(1)}, u32[]{:S(2)}, u32[]{:S(2)}) collective-permute-start(bf16[64,1024]{1,0:T(8,128)(2,1)S(1)} %get-tuple-element.15), channel_id=1, source_target_pairs={{0,12},{4,8},{8,4},{12,0},{16,28},{20,24},{24,20},{28,16},{1,13},{... | collective-permute-start | bytes 393224 | tf_op jit(solution)/shard_map/ppermute | solution.py:329
  5.9 12.5 %collective-permute-start.3 = (bf16[64,1024]{1,0:T(8,128)(2,1)S(1)}, bf16[64,1024]{1,0:T(8,128)(2,1)S(1)}, u32[]{:S(2)}, u32[]{:S(2)}) collective-permute-start(bf16[64,1024]{1,0:T(8,128)(2,1)S(1)} %get-tuple-element.18), channel_id=1, source_target_pairs={{0,16},{4,20},{8,24},{12,28},{16,0},{20,4},{24,8},{28,12},{1,17},{... | collective-permute-start | bytes 393224 | tf_op jit(solution)/shard_map/ppermute | solution.py:329
  8.5 17.8 %collective-permute-start.4 = (bf16[64,1024]{1,0:T(8,128)(2,1)S(1)}, bf16[64,1024]{1,0:T(8,128)(2,1)S(1)}, u32[]{:S(2)}, u32[]{:S(2)}) collective-permute-start(bf16[64,1024]{1,0:T(8,128)(2,1)S(1)} %get-tuple-element.19), channel_id=1, source_target_pairs={{0,20},{4,16},{8,28},{12,24},{16,4},{20,0},{24,12},{28,8},{1,21},{... | collective-permute-start | bytes 393224 | tf_op jit(solution)/shard_map/ppermute | solution.py:329
  11.3 15.0 %collective-permute-start.1 = (bf16[64,1024]{1,0:T(8,128)(2,1)S(1)}, bf16[64,1024]{1,0:T(8,128)(2,1)S(1)}, u32[]{:S(2)}, u32[]{:S(2)}) collective-permute-start(bf16[64,1024]{1,0:T(8,128)(2,1)S(1)} %get-tuple-element.16), channel_id=1, source_target_pairs={{0,4},{4,0},{8,12},{12,8},{16,20},{20,16},{24,28},{28,24},{1,5},{5... | collective-permute-start | bytes 393224 | tf_op jit(solution)/shard_map/ppermute | solution.py:329
  13.2 13.1 %collective-permute-start.2 = (bf16[64,1024]{1,0:T(8,128)(2,1)S(1)}, bf16[64,1024]{1,0:T(8,128)(2,1)S(1)}, u32[]{:S(2)}, u32[]{:S(2)}) collective-permute-start(bf16[64,1024]{1,0:T(8,128)(2,1)S(1)} %get-tuple-element.17), channel_id=1, source_target_pairs={{0,8},{4,12},{8,0},{12,4},{16,24},{20,28},{24,16},{28,20},{1,9},{5... | collective-permute-start | bytes 393224 | tf_op jit(solution)/shard_map/ppermute | solution.py:329
  13.2 13.1 %collective-permute-start.5 = (bf16[64,1024]{1,0:T(8,128)(2,1)S(1)}, bf16[64,1024]{1,0:T(8,128)(2,1)S(1)}, u32[]{:S(2)}, u32[]{:S(2)}) collective-permute-start(bf16[64,1024]{1,0:T(8,128)(2,1)S(1)} %get-tuple-element.20), channel_id=1, source_target_pairs={{0,24},{4,28},{8,16},{12,20},{16,8},{20,12},{24,0},{28,4},{1,25},{... | collective-permute-start | bytes 393224 | tf_op jit(solution)/shard_map/ppermute | solution.py:329
  18.4 7.9 %collective-permute-start.6 = (bf16[64,1024]{1,0:T(8,128)(2,1)S(1)}, bf16[64,1024]{1,0:T(8,128)(2,1)S(1)}, u32[]{:S(2)}, u32[]{:S(2)}) collective-permute-start(bf16[64,1024]{1,0:T(8,128)(2,1)S(1)} %get-tuple-element.21), channel_id=1, source_target_pairs={{0,28},{4,24},{8,20},{12,16},{16,12},{20,8},{24,4},{28,0},{1,29},{... | collective-permute-start | bytes 393224 | tf_op jit(solution)/shard_map/ppermute | solution.py:329
  21.8 4.5 %copy-start.2 = (bf16[1,1024]{1,0:T(2,128)(2,1)S(1)}, bf16[1,1024]{1,0:T(2,128)(2,1)}, u32[]{:S(2)}) copy-start(bf16[1,1024]{1,0:T(2,128)(2,1)} %refs_8_.1) | copy-start | bytes 6148
  27.2 1.6 %collective-permute-start.7 = (f32[576,128]{1,0:T(8,128)S(1)}, f32[576,128]{1,0:T(8,128)S(1)}, u32[]{:S(2)}, u32[]{:S(2)}) collective-permute-start(f32[576,128]{1,0:T(8,128)S(1)} %dynamic-slice_bitcast_fusion), channel_id=1, source_target_pairs={{0,1},{1,0},{2,3},{3,2},{4,5},{5,4},{6,7},{7,6},{8,9},{9,8},{10,11... | collective-permute-start | bytes 884744 | tf_op jit(solution)/shard_map/ppermute | solution.py:302
  28.9 4.4 %collective-permute-start.8 = (f32[144,128]{1,0:T(8,128)S(1)}, f32[144,128]{1,0:T(8,128)S(1)}, u32[]{:S(2)}, u32[]{:S(2)}) collective-permute-start(f32[144,128]{1,0:T(8,128)S(1)} %get-tuple-element.26), channel_id=1, source_target_pairs={{0,2},{1,3},{2,0},{3,1},{4,6},{5,7},{6,4},{7,5},{8,10},{9,11},{10,... | collective-permute-start | bytes 221192 | tf_op jit(solution)/shard_map/ppermute | solution.py:302
  30.5 5.4 %collective-permute-start.10 = (f32[144,128]{1,0:T(8,128)S(1)}, f32[144,128]{1,0:T(8,128)S(1)}, u32[]{:S(2)}, u32[]{:S(2)}) collective-permute-start(f32[144,128]{1,0:T(8,128)S(1)} %get-tuple-element.27), channel_id=1, source_target_pairs={{0,6},{1,7},{2,4},{3,5},{4,2},{5,3},{6,0},{7,1},{8,14},{9,15},{10,... | collective-permute-start | bytes 221192 | tf_op jit(solution)/shard_map/ppermute | solution.py:302
  32.5 4.4 %collective-permute-start.9 = (f32[144,128]{1,0:T(8,128)S(1)}, f32[144,128]{1,0:T(8,128)S(1)}, u32[]{:S(2)}, u32[]{:S(2)}) collective-permute-start(f32[144,128]{1,0:T(8,128)S(1)} %get-tuple-element.28), channel_id=1, source_target_pairs={{0,4},{1,5},{2,6},{3,7},{4,0},{5,1},{6,2},{7,3},{8,12},{9,13},{10,... | collective-permute-start | bytes 221192 | tf_op jit(solution)/shard_map/ppermute | solution.py:302
  36.9 7.7 %collective-permute-start.11 = (f32[144,128]{1,0:T(8,128)S(1)}, f32[144,128]{1,0:T(8,128)S(1)}, u32[]{:S(2)}, u32[]{:S(2)}) collective-permute-start(f32[144,128]{1,0:T(8,128)S(1)} %fusion.1), channel_id=1, source_target_pairs={{0,8},{1,9},{2,10},{3,11},{4,12},{5,13},{6,14},{7,15},{8,0},{9,1},... | collective-permute-start | bytes 221192 | tf_op jit(solution)/shard_map/ppermute | solution.py:302
  44.6 14.0 %copy-start.1 = (f32[512,64]{0,1:T(8,128)S(1)}, f32[512,64]{0,1:T(8,128)}, u32[]{:S(2)}) copy-start(f32[512,64]{0,1:T(8,128)} %param.5) | copy-start | bytes 393220
  44.6 5.4 %collective-permute-start.12 = (f32[144,128]{1,0:T(8,128)S(1)}, f32[144,128]{1,0:T(8,128)S(1)}, u32[]{:S(2)}, u32[]{:S(2)}) collective-permute-start(f32[144,128]{1,0:T(8,128)S(1)} %add.63), channel_id=1, source_target_pairs={{0,16},{1,17},{2,18},{3,19},{4,20},{5,21},{6,22},{7,23},{8,24},{9,... | collective-permute-start | bytes 221192 | tf_op jit(solution)/shard_map/ppermute | solution.py:302
  50.0 5.3 %collective-permute-start.15 = (f32[144,128]{1,0:T(8,128)S(1)}, f32[144,128]{1,0:T(8,128)S(1)}, u32[]{:S(2)}, u32[]{:S(2)}) collective-permute-start(f32[144,128]{1,0:T(8,128)S(1)} %add.64.refs_1_), channel_id=1, source_target_pairs={{0,6},{1,7},{2,4},{3,5},{4,2},{5,3},{6,0},{7,1},{8,14},{9,15},{10,... | collective-permute-start | bytes 221192 | tf_op jit(solution)/shard_map/ppermute | solution.py:302
  52.1 4.4 %collective-permute-start.14 = (f32[144,128]{1,0:T(8,128)S(1)}, f32[144,128]{1,0:T(8,128)S(1)}, u32[]{:S(2)}, u32[]{:S(2)}) collective-permute-start(f32[144,128]{1,0:T(8,128)S(1)} %add.64.refs_1_), channel_id=1, source_target_pairs={{0,4},{1,5},{2,6},{3,7},{4,0},{5,1},{6,2},{7,3},{8,12},{9,13},{10,... | collective-permute-start | bytes 221192 | tf_op jit(solution)/shard_map/ppermute | solution.py:302
  53.0 4.4 %collective-permute-start.13 = (f32[144,128]{1,0:T(8,128)S(1)}, f32[144,128]{1,0:T(8,128)S(1)}, u32[]{:S(2)}, u32[]{:S(2)}) collective-permute-start(f32[144,128]{1,0:T(8,128)S(1)} %add.64.refs_1_), channel_id=1, source_target_pairs={{0,2},{1,3},{2,0},{3,1},{4,6},{5,7},{6,4},{7,5},{8,10},{9,11},{10,... | collective-permute-start | bytes 221192 | tf_op jit(solution)/shard_map/ppermute | solution.py:302
  53.6 3.9 %collective-permute-start.16 = (f32[144,128]{1,0:T(8,128)S(1)}, f32[144,128]{1,0:T(8,128)S(1)}, u32[]{:S(2)}, u32[]{:S(2)}) collective-permute-start(f32[144,128]{1,0:T(8,128)S(1)} %add.64.refs_1_), channel_id=1, source_target_pairs={{0,1},{1,0},{2,3},{3,2},{4,5},{5,4},{6,7},{7,6},{8,9},{9,8},{10,11... | collective-permute-start | bytes 221192 | tf_op jit(solution)/shard_map/ppermute | solution.py:302
  55.3 2.1 %collective-permute-start.19 = (f32[144,128]{1,0:T(8,128)S(1)}, f32[144,128]{1,0:T(8,128)S(1)}, u32[]{:S(2)}, u32[]{:S(2)}) collective-permute-start(f32[144,128]{1,0:T(8,128)S(1)} %collective-permute-done.15.refs_4_), channel_id=1, source_target_pairs={{0,1},{1,0},{2,3},{3,2},{4,5},{5,4},{6,7},{7,6},{8,9},{9,8},{10,11... | collective-permute-start | bytes 221192 | tf_op jit(solution)/shard_map/ppermute | solution.py:302
  56.5 1.3 %collective-permute-start.18 = (f32[144,128]{1,0:T(8,128)S(1)}, f32[144,128]{1,0:T(8,128)S(1)}, u32[]{:S(2)}, u32[]{:S(2)}) collective-permute-start(f32[144,128]{1,0:T(8,128)S(1)} %collective-permute-done.14.refs_3_), channel_id=1, source_target_pairs={{0,1},{1,0},{2,3},{3,2},{4,5},{5,4},{6,7},{7,6},{8,9},{9,8},{10,11... | collective-permute-start | bytes 221192 | tf_op jit(solution)/shard_map/ppermute | solution.py:302
  57.4 1.3 %collective-permute-start.17 = (f32[144,128]{1,0:T(8,128)S(1)}, f32[144,128]{1,0:T(8,128)S(1)}, u32[]{:S(2)}, u32[]{:S(2)}) collective-permute-start(f32[144,128]{1,0:T(8,128)S(1)} %collective-permute-done.13.refs_2_), channel_id=1, source_target_pairs={{0,1},{1,0},{2,3},{3,2},{4,5},{5,4},{6,7},{7,6},{8,9},{9,8},{10,11... | collective-permute-start | bytes 221192 | tf_op jit(solution)/shard_map/ppermute | solution.py:302
